TPU v7x, 32 devices: a whole 2x2x4 slice. The times are simulated.
32 devices in a mesh: groups: 2 (over x), row: 16 (over z, y, core).
Axes of the slice: x: 2, y: 2, z: 4, core: 2. Of those that a mesh axis runs over, the one named last changes fastest.
Arguments:
- field: bfloat16 [512, 128, 512], P(('groups', 'row')), parts along dimension 0, may hold values from -6 to 6
- cotangent: bfloat16 [512, 128, 512], P(('groups', 'row')), parts along dimension 0, may hold values from -6 to 6
- row_filters: float32 [2, 4], replicated, may hold values from -0.7 to 0.7
- col_filter_1: bfloat16 [512, 512], replicated, may hold values from -1 to 1, as said below
- col_filter_2: bfloat16 [256, 256], replicated, may hold values from -1 to 1, as said below
- col_filter_3: bfloat16 [128, 128], replicated, may hold values from -1 to 1, as said below
- detail_weight: bfloat16 [3, 3, 128, 128], replicated, may hold values from -0.5 to 0.5
- skip_weight: bfloat16 [128, 128], replicated, may hold values from -0.5 to 0.5
- spectral_weight: float32 [2, 1024, 128, 128], P(None, 'row'), may hold values from -1.5 to 1.5
- row_modes: int32 [32], replicated, may hold values from 0 to 31, as said below
- col_modes: int32 [32], replicated, may hold values from 0 to 63, as said below
Outputs:
- grad_field: float32 [512, 128, 512], P(('groups', 'row')), parts along dimension 0
- grad_detail: float32 [6, 3, 128, 128], P('groups'), parts along dimension 0
- grad_skip: float32 [256, 128], P('groups'), parts along dimension 0
- grad_spectral: float32 [4, 1024, 128, 128], P('groups', 'row'), parts along dimension 0
There are 2 independent parts, one for each index of `groups`. A program takes and returns all parts, laid end to end along the dimension named above; an argument that names none is the same for every part. Nothing has to cross between parts.
Inputs may be any that keep to these rules, and one draw needn't show every extreme that they name: `row_modes`: 32 distinct row frequencies. `col_modes`: 32 distinct column frequencies. `col_filter_1`: zero outside the 128-blocks (j, j) and (j+1 mod n, j). `col_filter_2`: zero outside the 128-blocks (j, j) and (j+1 mod n, j). `col_filter_3`: zero outside the 128-blocks (j, j) and (j+1 mod n, j).
All inputs are finite; a program needn't handle non-finite values.
Results may differ from a plain program's by a relative error of at most 0.02.
Values may be sent and summed in bfloat16 or wider, within the bound.
A program may use at most 128 MiB of HBM per device.

v0:
```python
import math

import jax
import jax.numpy as jnp
from jax import lax
from jax.sharding import PartitionSpec as P


def shifted(shard, axis, by):
    size = lax.axis_size(axis)
    return lax.ppermute(shard, axis, [(i, (i + by) % size) for i in range(size)])


def as_float(values):
    return values.astype(jnp.float32)


def precise(form, first_in, second_in):
    return jnp.einsum(form, first_in, second_in, precision=lax.Precision.HIGHEST)


def narrow(form, first_in, second_in):
    return jnp.einsum(form, first_in, second_in, preferred_element_type=jnp.float32)


def column_tables(col_modes, length):
    positions = jnp.arange(length, dtype=jnp.int32)
    turns = positions[:, None] * col_modes[None, :] % length
    angles = turns.astype(jnp.float32) * (2.0 * math.pi / length)
    return (jnp.cos(angles), jnp.sin(angles))


def row_tables(row_modes, positions, length):
    turns = row_modes[:, None] * positions[None, :] % length
    angles = turns.astype(jnp.float32) * (2.0 * math.pi / length)
    return (jnp.cos(angles), jnp.sin(angles))


def row_pass(values, row_filters):
    incoming = shifted(values[:2], "row", -1)
    spread = as_float(jnp.concatenate([values, incoming], axis=0))
    row_count = values.shape[0]
    outputs = []
    for branch in range(2):
        running = row_filters[branch, 0] * spread[0:row_count:2]
        for offset in range(1, 4):
            running = (
                running + row_filters[branch, offset] * spread[offset : offset + row_count : 2]
            )
        outputs.append(running.astype(jnp.bfloat16))
    return (outputs[0], outputs[1])


def analysis(values, row_filters, matrices):
    band_list = []
    current = values
    for matrix in matrices:
        low_rows, high_rows = row_pass(current, row_filters)
        low_cols = narrow("hcw,wv->hcv", low_rows, matrix).astype(jnp.bfloat16)
        high_cols = narrow("hcw,wv->hcv", high_rows, matrix).astype(jnp.bfloat16)
        halfway = low_cols.shape[2] // 2
        current = low_cols[:, :, :halfway]
        band_list.append(
            (low_cols[:, :, halfway:], high_cols[:, :, :halfway], high_cols[:, :, halfway:])
        )
    return (current, band_list)


def combine_rows(low_now, high_now, low_prev, high_prev, row_filters):
    parities = []
    for parity in range(2):
        running = row_filters[0, parity] * low_now + row_filters[1, parity] * high_now
        running = running + row_filters[0, parity + 2] * low_prev
        running = running + row_filters[1, parity + 2] * high_prev
        parities.append(running)
    stacked = jnp.stack(parities, axis=1)
    return stacked.reshape((2 * low_now.shape[0],) + low_now.shape[1:])


def synthesis(top_array, band_list, row_filters, matrices):
    current = top_array
    for octave in (2, 1, 0):
        band_one, band_two, band_three = band_list[octave]
        low_sum = narrow(
            "hcv,wv->hcw", jnp.concatenate([current, band_one], axis=2), matrices[octave]
        ).astype(jnp.bfloat16)
        high_sum = narrow(
            "hcv,wv->hcw", jnp.concatenate([band_two, band_three], axis=2), matrices[octave]
        ).astype(jnp.bfloat16)
        edges = jnp.concatenate([low_sum[-1:], high_sum[-1:]], axis=0)
        earlier = shifted(edges, "row", 1)
        low_prev = jnp.concatenate([earlier[0:1], low_sum[:-1]], axis=0)
        high_prev = jnp.concatenate([earlier[1:2], high_sum[:-1]], axis=0)
        current = combine_rows(
            as_float(low_sum),
            as_float(high_sum),
            as_float(low_prev),
            as_float(high_prev),
            row_filters,
        )
        if octave > 0:
            current = current.astype(jnp.bfloat16)
    return current


def owned_modes(coarse, row_modes, col_modes):
    local_rows, channels, columns = coarse.shape
    devices = lax.axis_size("row")
    height = local_rows * devices
    cos_col, sin_col = column_tables(col_modes, columns)
    values = as_float(coarse)
    real_one = precise("hcw,wm->hcm", values, cos_col)
    imag_one = -precise("hcw,wm->hcm", values, sin_col)
    positions = lax.axis_index("row") * local_rows + jnp.arange(local_rows, dtype=jnp.int32)
    cos_row, sin_row = row_tables(row_modes, positions, height)
    real_two = precise("ph,hcm->pmc", cos_row, real_one) + precise("ph,hcm->pmc", sin_row, imag_one)
    imag_two = precise("ph,hcm->pmc", cos_row, imag_one) - precise("ph,hcm->pmc", sin_row, real_one)
    term_all = jnp.stack([real_two.reshape(-1, channels), imag_two.reshape(-1, channels)], axis=1)
    owned = lax.psum_scatter(term_all, "row", scatter_dimension=0, tiled=True)
    return (owned[:, 0], owned[:, 1])


def owned_image(real_owned, imag_owned, row_modes, col_modes, local_rows, columns):
    devices = lax.axis_size("row")
    height = local_rows * devices
    mode_rows = row_modes.shape[0]
    mode_cols = col_modes.shape[0]
    positions = lax.axis_index("row") * local_rows + jnp.arange(local_rows, dtype=jnp.int32)
    real_piece = lax.all_gather(real_owned, "row", axis=0, tiled=True)
    imag_piece = lax.all_gather(imag_owned, "row", axis=0, tiled=True)
    piece_rows = real_piece.shape[0]
    flat = jnp.arange(piece_rows, dtype=jnp.int32)
    row_pick = (flat // mode_cols)[:, None] == jnp.arange(mode_rows, dtype=jnp.int32)[None, :]
    frequency = jnp.sum(jnp.where(row_pick, row_modes[None, :], 0), axis=1)
    column_pick = (
        (flat % mode_cols)[:, None] == jnp.arange(mode_cols, dtype=jnp.int32)[None, :]
    ).astype(jnp.float32)
    turns = positions[:, None] * frequency[None, :] % height
    angles = turns.astype(jnp.float32) * (2.0 * math.pi / height)
    cos_part = jnp.cos(angles)
    sin_part = jnp.sin(angles)
    cos_pick = cos_part[:, :, None] * column_pick[None, :, :]
    sin_pick = sin_part[:, :, None] * column_pick[None, :, :]
    real_sum = precise("hnm,nc->hcm", cos_pick, real_piece) - precise(
        "hnm,nc->hcm", sin_pick, imag_piece
    )
    imag_sum = precise("hnm,nc->hcm", cos_pick, imag_piece) + precise(
        "hnm,nc->hcm", sin_pick, real_piece
    )
    cos_col, sin_col = column_tables(col_modes, columns)
    image = precise("hcm,wm->hcw", real_sum, cos_col) - precise("hcm,wm->hcw", imag_sum, sin_col)
    return image.astype(jnp.bfloat16)


def mix_modes(real_in, imag_in, weight_real, weight_imag, factor):
    real_out = (
        precise("nc,nco->no", real_in, weight_real) - precise("nc,nco->no", imag_in, weight_imag)
    ) * factor
    imag_out = (
        precise("nc,nco->no", real_in, weight_imag) + precise("nc,nco->no", imag_in, weight_real)
    ) * factor
    return (real_out, imag_out)


def mix_modes_back(real_in, imag_in, weight_real, weight_imag, factor):
    real_out = (
        precise("no,nco->nc", real_in, weight_real) + precise("no,nco->nc", imag_in, weight_imag)
    ) * factor
    imag_out = (
        precise("no,nco->nc", imag_in, weight_real) - precise("no,nco->nc", real_in, weight_imag)
    ) * factor
    return (real_out, imag_out)


def per_device(
    field,
    cotangent,
    row_filters,
    col_filter_1,
    col_filter_2,
    col_filter_3,
    detail_weight,
    skip_weight,
    spectral_weight,
    row_modes,
    col_modes,
):
    matrices = (col_filter_1, col_filter_2, col_filter_3)
    devices = lax.axis_size("row")
    coarse_field, bands_field = analysis(field, row_filters, matrices)
    local_rows, channels, columns = coarse_field.shape
    height = local_rows * devices
    factor = 1.0 / (height * columns)
    weight_real = spectral_weight[0]
    weight_imag = spectral_weight[1]
    spec_real, spec_imag = owned_modes(coarse_field, row_modes, col_modes)
    out_real, out_imag = mix_modes(spec_real, spec_imag, weight_real, weight_imag, factor)
    coarse_image = owned_image(out_real, out_imag, row_modes, col_modes, local_rows, columns)
    mixed_field = [
        tuple(
            (
                narrow(
                    "hcw,co->how", bands_field[octave][member], detail_weight[octave, member]
                ).astype(jnp.bfloat16)
                for member in range(3)
            )
        )
        for octave in range(3)
    ]
    rebuilt_field = synthesis(coarse_image, mixed_field, row_filters, matrices)
    activation_in = rebuilt_field + narrow("hcw,co->how", field, skip_weight)
    upstream = jax.vjp(jax.nn.gelu, activation_in)[1](as_float(cotangent))[0].astype(jnp.bfloat16)
    coarse_slope, bands_slope = analysis(upstream, row_filters, matrices)
    back_real, back_imag = owned_modes(coarse_slope, row_modes, col_modes)
    turned_real, turned_imag = mix_modes_back(
        back_real, back_imag, weight_real, weight_imag, factor
    )
    image_back = owned_image(turned_real, turned_imag, row_modes, col_modes, local_rows, columns)
    back_bands = [
        tuple(
            (
                narrow(
                    "how,co->hcw", bands_slope[octave][member], detail_weight[octave, member]
                ).astype(jnp.bfloat16)
                for member in range(3)
            )
        )
        for octave in range(3)
    ]
    rebuilt_slope = synthesis(image_back, back_bands, row_filters, matrices)
    grad_field = rebuilt_slope + narrow("how,co->hcw", upstream, skip_weight)
    skip_local = narrow("hcw,how->co", field, upstream)
    detail_local = jnp.stack(
        [
            jnp.stack(
                [
                    narrow("hcw,how->co", bands_field[octave][member], bands_slope[octave][member])
                    for member in range(3)
                ]
            )
            for octave in range(3)
        ]
    )
    skip_total, detail_total = lax.psum((skip_local, detail_local), "row")
    total_rows = field.shape[0] * devices
    total_cols = field.shape[2]
    grad_skip = skip_total / math.sqrt(total_rows * total_cols)
    divisors = jnp.array(
        [
            [
                math.sqrt((total_rows >> octave + 1) * (total_cols >> octave + 1))
                for member in range(3)
            ]
            for octave in range(3)
        ],
        jnp.float32,
    )
    grad_detail = detail_total / divisors[:, :, None, None]
    grad_real = (
        spec_real[:, :, None] * back_real[:, None, :]
        + spec_imag[:, :, None] * back_imag[:, None, :]
    ) * factor
    grad_imag = (
        spec_real[:, :, None] * back_imag[:, None, :]
        - spec_imag[:, :, None] * back_real[:, None, :]
    ) * factor
    grad_spectral = jnp.stack([grad_real, grad_imag])
    return (grad_field, grad_detail, grad_skip, grad_spectral)


def solution(mesh):
    placed = (
        P(("groups", "row"), None, None),
        P(("groups", "row"), None, None),
        P(),
        P(),
        P(),
        P(),
        P(),
        P(),
        P(None, "row", None, None),
        P(),
        P(),
    )
    return jax.shard_map(
        per_device,
        mesh=mesh,
        in_specs=placed,
        out_specs=(
            P(("groups", "row"), None, None),
            P("groups", None, None, None),
            P("groups", None),
            P("groups", "row", None, None),
        ),
        check_vma=False,
    )
```

profile of v0, /device:TPU:0, one launch (start us, length us, event | category | flops | bytes accessed | tf_op | source)
XLA Modules:
  0.0 574.2 jit_solution(12100149623124554629)
XLA Ops:
  8.2 5.5 collective-permute-start
  19.6 3.4 convolution_convert_fusion.5
  24.0 3.2 convolution_convert_fusion.7
  27.2 4.7 collective-permute-start.1
  34.5 2.7 convolution_convert_fusion.21
  37.2 2.9 convolution_convert_fusion.19
  40.1 4.6 collective-permute-start.2
  46.7 2.6 convolution_convert_fusion.35
  55.4 2.8 convolution_convert_fusion.33
  58.8 54.6 %reduce-scatter.3.cloned.1.call-done = f32[64,2,128]{2,0,1:T(8,128)} async-done(((f32[1024,2,128]{2,0,1:T(8,128)}), f32[64,2,128]{2,0,1:T(8,128)}) %reduce-scatter.3.cloned.1.call-update) | async-done | bytes 65552 | tf_op jit(solution)/shard_map/reduce_scatter | solution.py:119
  114.8 5.3 fusion.22
  120.1 5.3 fusion.16
  125.4 5.3 fusion.14
  130.7 5.3 fusion.24
  135.9 20.8 %all_gather.13 = f32[1024,128]{1,0:T(8,128)S(1)} all-gather(f32[64,128]{1,0:T(8,128)S(1)} %add_multiply_fusion.2), channel_id=1, replica_groups=mesh['groups'=2,'row'=16] {'row'}, dimensions={0}, use_global_device_ids=true | all-gather | bytes 557056 | tf_op jit(solution)/shard_map/all_gather | solution.py:130
  157.7 18.9 %all_gather.12 = f32[1024,128]{1,0:T(8,128)S(1)} all-gather(f32[64,128]{1,0:T(8,128)S(1)} %subtract_multiply_fusion.2), channel_id=1, replica_groups=mesh['groups'=2,'row'=16] {'row'}, dimensions={0}, use_global_device_ids=true | all-gather | bytes 557056 | tf_op jit(solution)/shard_map/all_gather | solution.py:129
  179.2 5.8 %collective-permute-done.3 = bf16[2,128,128]{2,1,0:T(8,128)(2,1)S(1)} collective-permute-done((bf16[2,128,128]{2,1,0:T(8,128)(2,1)S(1)}, bf16[2,128,128]{2,1,0:T(8,128)(2,1)S(1)}, u32[]{:S(2)}, u32[]{:S(2)}) %collective-permute-start.3) | collective-permute-done | bytes 65568 | tf_op jit(solution)/shard_map/ppermute | solution.py:11
  185.0 5.1 fusion.178
  193.2 5.9 %collective-permute-done.4 = bf16[2,128,256]{2,1,0:T(8,128)(2,1)S(1)} collective-permute-done((bf16[2,128,256]{2,1,0:T(8,128)(2,1)S(1)}, bf16[2,128,256]{2,1,0:T(8,128)(2,1)S(1)}, u32[]{:S(2)}, u32[]{:S(2)}) %collective-permute-start.4) | collective-permute-done | bytes 131104 | tf_op jit(solution)/shard_map/ppermute | solution.py:11
  199.1 5.4 fusion.125
  206.0 8.4 %collective-permute-done.5 = bf16[2,128,512]{2,1,0:T(8,128)(2,1)S(1)} collective-permute-done((bf16[2,128,512]{2,1,0:T(8,128)(2,1)S(1)}, bf16[2,128,512]{2,1,0:T(8,128)(2,1)S(1)}, u32[]{:S(2)}, u32[]{:S(2)}) %collective-permute-start.5) | collective-permute-done | bytes 262176 | tf_op jit(solution)/shard_map/ppermute | solution.py:11
  214.5 6.3 %fusion.37 = (f32[8,1,128,512]{3,2,0,1:T(8,128)S(1)}, f32[8,1,128,512]{3,2,0,1:T(8,128)S(1)}) fusion(bf16[8,128,512]{2,1,0:T(8,128)(2,1)S(1)} %convolution_convert_fusion.6, bf16[8,128,512]{2,1,0:T(8,128)(2,1)S(1)} %copy-done.6, f32[]{:T(128)} %bitcast.53, f32[]{:T(128)} %bitcast.51, f32[]{:T(128)} %bitcast.2, f32[]{:T(128)} %bitcast, ...), kind=kLoop, calls=%fused_computation.66 | loop fusion | flops 10485760 | bytes 8388640 | tf_op jit(solution)/shard_map/stack | solution.py:76
  223.6 4.0 fusion.2
  231.9 3.2 convolution_convert_fusion.3
  235.1 3.5 convolution_convert_fusion.1
  240.8 4.7 collective-permute-start.7
  248.6 2.7 convolution_convert_fusion.17
  251.3 2.9 convolution_convert_fusion.15
  255.6 4.1 collective-permute-start.8
  264.4 2.8 convolution_convert_fusion.29
  280.8 85.2 %all-reduce.3.cloned.1.call-done = (f32[3,3,128,128]{3,2,1,0:T(8,128)}, f32[128,128]{0,1:T(8,128)}) async-done(((f32[3,3,128,128]{3,2,1,0:T(8,128)}, f32[128,128]{0,1:T(8,128)}), (f32[3,3,128,128]{3,2,1,0:T(8,128)}, f32[128,128]{0,1:T(8,128)})) %all-reduce.3.cloned.1.call-update) | async-done | bytes 655376 | tf_op jit(solution)/shard_map/psum | solution.py:244
  367.9 59.9 %reduce-scatter.5.cloned.1.call-done = f32[64,2,128]{2,0,1:T(8,128)} async-done(((f32[1024,2,128]{2,0,1:T(8,128)}), f32[64,2,128]{2,0,1:T(8,128)}) %reduce-scatter.5.cloned.1.call-update) | async-done | bytes 65552 | tf_op jit(solution)/shard_map/reduce_scatter | solution.py:119
  428.6 8.3 %fusion.18 = f32[64,1,128]{2,1,0:T(1,128)S(1)} fusion(f32[64,128,1]{1,2,0:T(1,128)S(1)} %bitcast.435, f32[2,64,128,128]{3,2,1,0:T(8,128)} %param.20), kind=kOutput, calls=%fused_computation.27 | convolution fusion | flops 12582912 | bytes 4259840 | tf_op jit(solution)/shard_map/no,nco->nc/dot_general | solution.py:19
  436.9 8.3 %fusion.12 = f32[64,1,128]{2,1,0:T(1,128)S(1)} fusion(f32[64,128,1]{1,2,0:T(1,128)S(1)} %bitcast.436, f32[2,64,128,128]{3,2,1,0:T(8,128)} %param.20), kind=kOutput, calls=%fused_computation.21 | convolution fusion | flops 12582912 | bytes 4259840 | tf_op jit(solution)/shard_map/no,nco->nc/dot_general | solution.py:19
  445.2 8.3 %fusion.10 = f32[64,1,128]{2,1,0:T(1,128)S(1)} fusion(f32[64,128,1]{1,2,0:T(1,128)S(1)} %bitcast.431, f32[2,64,128,128]{3,2,1,0:T(8,128)} %param.20), kind=kOutput, calls=%fused_computation.19 | convolution fusion | flops 12582912 | bytes 4259840 | tf_op jit(solution)/shard_map/no,nco->nc/dot_general | solution.py:19
  453.5 8.3 %fusion.20 = f32[64,1,128]{2,1,0:T(1,128)S(1)} fusion(f32[64,128,1]{1,2,0:T(1,128)S(1)} %bitcast.432, f32[2,64,128,128]{3,2,1,0:T(8,128)} %param.20), kind=kOutput, calls=%fused_computation.29 | convolution fusion | flops 12582912 | bytes 4259840 | tf_op jit(solution)/shard_map/no,nco->nc/dot_general | solution.py:19
  461.9 21.1 %all_gather.15 = f32[1024,128]{1,0:T(8,128)S(1)} all-gather(f32[64,128]{1,0:T(8,128)S(1)} %subtract_multiply_fusion.1), channel_id=1, replica_groups=mesh['groups'=2,'row'=16] {'row'}, dimensions={0}, use_global_device_ids=true | all-gather | bytes 557056 | tf_op jit(solution)/shard_map/all_gather | solution.py:130
  483.9 18.9 %all_gather.14 = f32[1024,128]{1,0:T(8,128)S(1)} all-gather(f32[64,128]{1,0:T(8,128)S(1)} %add_multiply_fusion.1), channel_id=1, replica_groups=mesh['groups'=2,'row'=16] {'row'}, dimensions={0}, use_global_device_ids=true | all-gather | bytes 557056 | tf_op jit(solution)/shard_map/all_gather | solution.py:129
  505.8 5.3 collective-permute-done.9
  511.1 5.1 fusion.176
  517.9 4.6 add_multiply_fusion
  524.9 5.4 fusion.123
  533.9 6.4 %pad_maximum_fusion = f32[2,64,128,128]{3,2,1,0:T(8,128)} fusion(f32[1,64,128,128]{3,2,1,0:T(8,128)} %get-tuple-element.35, f32[1,64,128,128]{3,2,1,0:T(8,128)S(1)} %copy-done.1), kind=kLoop, calls=%fused_computation | loop fusion | flops 2097152 | bytes 16777216 | tf_op jit(solution)/shard_map/stack | solution.py:267
  542.2 6.3 %fusion.45 = (f32[8,1,128,512]{3,2,0,1:T(8,128)S(1)}, f32[8,1,128,512]{3,2,0,1:T(8,128)S(1)}) fusion(bf16[8,128,512]{2,1,0:T(8,128)(2,1)S(1)} %convolution_convert_fusion.2, bf16[8,128,512]{2,1,0:T(8,128)(2,1)S(1)} %copy-done.4, f32[]{:T(128)} %bitcast.53, f32[]{:T(128)} %bitcast.51, f32[]{:T(128)} %bitcast.2, f32[]{:T(128)} %bitcast, ...), kind=kLoop, calls=%fused_computation.74 | loop fusion | flops 10485760 | bytes 8388640 | tf_op jit(solution)/shard_map/stack | solution.py:76
  549.1 2.7 copy.121
  551.8 5.4 copy.123
  557.1 4.9 bitcast_add_fusion
  562.1 5.3 copy.124
  (276 shorter events, 76.3 us)
Async XLA Ops:
  7.2 12.4 %copy-start = (bf16[512,512]{1,0:T(8,128)(2,1)S(1)}, bf16[512,512]{1,0:T(8,128)(2,1)}, u32[]{:S(2)}) copy-start(bf16[512,512]{1,0:T(8,128)(2,1)} %param.15) | copy-start | bytes 1572868
  7.2 106.3 %reduce-scatter.3.cloned.1.call-start = ((), (), s32[]{:S(2)}) async-start(), calls=%async_computation.2 | async-start | bytes 1114112 | tf_op jit(solution)/shard_map/reduce_scatter | solution.py:119
  8.2 9.4 %collective-permute-start = (bf16[2,128,512]{2,1,0:T(8,128)(2,1)S(1)}, bf16[2,128,512]{2,1,0:T(8,128)(2,1)S(1)}, u32[]{:S(2)}, u32[]{:S(2)}) collective-permute-start(bf16[2,128,512]{2,1,0:T(8,128)(2,1)S(1)} %slice.231), channel_id=1, source_target_pairs={{0,15},{1,0},{2,1},{3,2},{4,3},{5,4},{6,5},{7,6},{8,7},{9,8},{10,9... | collective-permute-start | bytes 786440 | tf_op jit(solution)/shard_map/ppermute | solution.py:11
  27.1 5.5 copy-start.9
  27.2 7.2 %collective-permute-start.1 = (bf16[2,128,256]{2,1,0:T(8,128)(2,1)S(1)}, bf16[2,128,256]{2,1,0:T(8,128)(2,1)S(1)}, u32[]{:S(2)}, u32[]{:S(2)}) collective-permute-start(bf16[2,128,256]{2,1,0:T(8,128)(2,1)S(1)} %slice.578), channel_id=1, source_target_pairs={{0,15},{1,0},{2,1},{3,2},{4,3},{5,4},{6,5},{7,6},{8,7},{9,8},{10,9... | collective-permute-start | bytes 393224 | tf_op jit(solution)/shard_map/ppermute | solution.py:11
  32.6 4.6 copy-start.5
  34.4 12.3 %copy-start.24 = (bf16[128,128]{1,0:T(8,128)(2,1)S(1)}, bf16[128,128]{1,0:T(8,128)(2,1)}, u32[]{:S(2)}) copy-start(bf16[128,128]{1,0:T(8,128)(2,1)} %param.17) | copy-start | bytes 98308
  34.5 14.9 %copy-start.40 = (s32[32]{0:T(128)S(1)}, s32[32]{0:T(128)}, u32[]{:S(2)}) copy-start(s32[32]{0:T(128)} %param.22) | copy-start | bytes 388
  37.2 141.7 %copy-start.21 = (bf16[4,128,256]{2,1,0:T(8,128)(2,1)}, bf16[4,128,256]{2,1,0:T(8,128)(2,1)S(1)}, u32[]{:S(2)}) copy-start(bf16[4,128,256]{2,1,0:T(8,128)(2,1)S(1)} %convolution_convert_fusion.21) | copy-start | bytes 786436
  37.2 12.8 %copy-start.37 = (s32[32]{0:T(128)S(1)}, s32[32]{0:T(128)}, u32[]{:S(2)}) copy-start(s32[32]{0:T(128)} %param.21) | copy-start | bytes 388
  40.1 14.7 %copy-start.15 = (bf16[4,128,256]{2,1,0:T(8,128)(2,1)}, bf16[4,128,256]{2,1,0:T(8,128)(2,1)S(1)}, u32[]{:S(2)}) copy-start(bf16[4,128,256]{2,1,0:T(8,128)(2,1)S(1)} %convolution_convert_fusion.19) | copy-start | bytes 786436
  40.1 6.5 %collective-permute-start.2 = (bf16[2,128,128]{2,1,0:T(8,128)(2,1)S(1)}, bf16[2,128,128]{2,1,0:T(8,128)(2,1)S(1)}, u32[]{:S(2)}, u32[]{:S(2)}) collective-permute-start(bf16[2,128,128]{2,1,0:T(8,128)(2,1)S(1)} %slice.580), channel_id=1, source_target_pairs={{0,15},{1,0},{2,1},{3,2},{4,3},{5,4},{6,5},{7,6},{8,7},{9,8},{10,9... | collective-permute-start | bytes 196616 | tf_op jit(solution)/shard_map/ppermute | solution.py:11
  49.4 9.1 %copy-start.33 = (bf16[2,128,128]{1,2,0:T(8,128)(2,1)}, bf16[2,128,128]{1,2,0:T(8,128)(2,1)S(1)}, u32[]{:S(2)}) copy-start(bf16[2,128,128]{1,2,0:T(8,128)(2,1)S(1)} %convolution_convert_fusion.35) | copy-start | bytes 196612
  54.6 311.3 %all-reduce.3.cloned.1.call-start = ((), (), s32[]{:S(2)}) async-start(), calls=%async_computation.4 | async-start | bytes 1310720 | tf_op jit(solution)/shard_map/psum | solution.py:244
  55.4 123.8 %copy-start.19 = (bf16[4,128,256]{2,1,0:T(8,128)(2,1)}, bf16[4,128,256]{2,1,0:T(8,128)(2,1)S(1)}, u32[]{:S(2)}) copy-start(bf16[4,128,256]{2,1,0:T(8,128)(2,1)S(1)} %convolution_convert_fusion.18) | copy-start | bytes 786436
  177.0 15.0 %copy-start.10 = (bf16[8,128,512]{2,1,0:T(8,128)(2,1)S(1)}, bf16[8,128,512]{2,1,0:T(8,128)(2,1)}, u32[]{:S(2)}) copy-start(bf16[8,128,512]{2,1,0:T(8,128)(2,1)} %copy-done.9) | copy-start | bytes 3145732
  178.5 6.4 %collective-permute-start.3 = (bf16[2,128,128]{2,1,0:T(8,128)(2,1)S(1)}, bf16[2,128,128]{2,1,0:T(8,128)(2,1)S(1)}, u32[]{:S(2)}, u32[]{:S(2)}) collective-permute-start(bf16[2,128,128]{2,1,0:T(8,128)(2,1)S(1)} %pad_maximum_fusion.22), channel_id=1, source_target_pairs={{0,1},{1,2},{2,3},{3,4},{4,5},{5,6},{6,7},{7,8},{8,9},{9,10},{10,1... | collective-permute-start | bytes 196616 | tf_op jit(solution)/shard_map/ppermute | solution.py:11
  179.2 12.3 %slice-start.7 = ((bf16[4,128,256]{2,1,0:T(8,128)(2,1)}), bf16[1,128,256]{2,1,0:T(8,128)(2,1)S(1)}, s32[]{:S(2)}) async-start(bf16[4,128,256]{2,1,0:T(8,128)(2,1)} %copy-done.19), calls=%async_computation.12 | async-start | bytes 131072 | tf_op jit(solution)/shard_map/slice | solution.py:90
  190.1 9.0 %copy-start.20 = (bf16[4,128,256]{2,1,0:T(8,128)(2,1)S(1)}, bf16[4,128,256]{2,1,0:T(8,128)(2,1)}, u32[]{:S(2)}) copy-start(bf16[4,128,256]{2,1,0:T(8,128)(2,1)} %copy-done.19) | copy-start | bytes 786436
  190.1 9.0 %slice-start.8 = ((bf16[4,128,256]{2,1,0:T(8,128)(2,1)}), bf16[3,128,256]{2,1,0:T(8,128)(2,1)S(1)}, s32[]{:S(2)}) async-start(bf16[4,128,256]{2,1,0:T(8,128)(2,1)} %copy-done.19), calls=%async_computation.13 | async-start | bytes 393216 | tf_op jit(solution)/shard_map/slice | solution.py:93
  191.5 7.5 %collective-permute-start.4 = (bf16[2,128,256]{2,1,0:T(8,128)(2,1)S(1)}, bf16[2,128,256]{2,1,0:T(8,128)(2,1)S(1)}, u32[]{:S(2)}, u32[]{:S(2)}) collective-permute-start(bf16[2,128,256]{2,1,0:T(8,128)(2,1)S(1)} %pad_maximum_fusion.19), channel_id=1, source_target_pairs={{0,1},{1,2},{2,3},{3,4},{4,5},{5,6},{6,7},{7,8},{8,9},{9,10},{10,1... | collective-permute-start | bytes 393224 | tf_op jit(solution)/shard_map/ppermute | solution.py:11
  199.1 5.8 %copy-start.25 = (bf16[8,128,256]{1,2,0:T(8,128)(2,1)S(1)}, bf16[8,128,256]{1,2,0:T(8,128)(2,1)}, u32[]{:S(2)}) copy-start(bf16[8,128,256]{1,2,0:T(8,128)(2,1)} %fusion.54) | copy-start | bytes 1572868
  205.9 8.6 %copy-start.6 = (bf16[8,128,512]{2,1,0:T(8,128)(2,1)S(1)}, bf16[8,128,512]{2,1,0:T(8,128)(2,1)}, u32[]{:S(2)}) copy-start(bf16[8,128,512]{2,1,0:T(8,128)(2,1)} %copy-done.5) | copy-start | bytes 3145732
  205.9 8.6 %slice-start.3 = ((bf16[8,128,512]{2,1,0:T(8,128)(2,1)}), bf16[7,128,512]{2,1,0:T(8,128)(2,1)S(1)}, s32[]{:S(2)}) async-start(bf16[8,128,512]{2,1,0:T(8,128)(2,1)} %copy-done.5), calls=%async_computation.8 | async-start | bytes 1835008 | tf_op jit(solution)/shard_map/slice | solution.py:93
  205.9 8.5 %collective-permute-start.5 = (bf16[2,128,512]{2,1,0:T(8,128)(2,1)S(1)}, bf16[2,128,512]{2,1,0:T(8,128)(2,1)S(1)}, u32[]{:S(2)}, u32[]{:S(2)}) collective-permute-start(bf16[2,128,512]{2,1,0:T(8,128)(2,1)S(1)} %pad_maximum_fusion.14), channel_id=1, source_target_pairs={{0,1},{1,2},{2,3},{3,4},{4,5},{5,6},{6,7},{7,8},{8,9},{9,10},{10,1... | collective-permute-start | bytes 786440 | tf_op jit(solution)/shard_map/ppermute | solution.py:11
  227.6 3.9 collective-permute-start.6
  235.1 12.3 %copy-start.8 = (bf16[8,128,512]{2,1,0:T(8,128)(2,1)}, bf16[8,128,512]{2,1,0:T(8,128)(2,1)S(1)}, u32[]{:S(2)}) copy-start(bf16[8,128,512]{2,1,0:T(8,128)(2,1)S(1)} %convolution_convert_fusion.3) | copy-start | bytes 3145732
  240.8 7.2 %collective-permute-start.7 = (bf16[2,128,256]{2,1,0:T(8,128)(2,1)S(1)}, bf16[2,128,256]{2,1,0:T(8,128)(2,1)S(1)}, u32[]{:S(2)}, u32[]{:S(2)}) collective-permute-start(bf16[2,128,256]{2,1,0:T(8,128)(2,1)S(1)} %slice.613), channel_id=1, source_target_pairs={{0,15},{1,0},{2,1},{3,2},{4,3},{5,4},{6,5},{7,6},{8,7},{9,8},{10,9... | collective-permute-start | bytes 393224 | tf_op jit(solution)/shard_map/ppermute | solution.py:11
  248.6 5.7 copy-start.16
  248.6 6.1 %copy-start.22 = (bf16[4,128,256]{2,1,0:T(8,128)(2,1)S(1)}, bf16[4,128,256]{2,1,0:T(8,128)(2,1)}, u32[]{:S(2)}) copy-start(bf16[4,128,256]{2,1,0:T(8,128)(2,1)} %copy-done.21) | copy-start | bytes 786436
  251.3 4.3 copy-start.23
  254.6 12.6 %copy-start.34 = (bf16[2,128,128]{1,2,0:T(8,128)(2,1)S(1)}, bf16[2,128,128]{1,2,0:T(8,128)(2,1)}, u32[]{:S(2)}) copy-start(bf16[2,128,128]{1,2,0:T(8,128)(2,1)} %copy-done.33) | copy-start | bytes 196612
  255.6 13.5 %copy-start.17 = (bf16[4,128,256]{2,1,0:T(8,128)(2,1)}, bf16[4,128,256]{2,1,0:T(8,128)(2,1)S(1)}, u32[]{:S(2)}) copy-start(bf16[4,128,256]{2,1,0:T(8,128)(2,1)S(1)} %convolution_convert_fusion.14) | copy-start | bytes 786436
  255.6 6.0 %collective-permute-start.8 = (bf16[2,128,128]{2,1,0:T(8,128)(2,1)S(1)}, bf16[2,128,128]{2,1,0:T(8,128)(2,1)S(1)}, u32[]{:S(2)}, u32[]{:S(2)}) collective-permute-start(bf16[2,128,128]{2,1,0:T(8,128)(2,1)S(1)} %slice.615), channel_id=1, source_target_pairs={{0,15},{1,0},{2,1},{3,2},{4,3},{5,4},{6,5},{7,6},{8,7},{9,8},{10,9... | collective-permute-start | bytes 196616 | tf_op jit(solution)/shard_map/ppermute | solution.py:11
  273.4 154.4 %reduce-scatter.5.cloned.1.call-start = ((), (), s32[]{:S(2)}) async-start(), calls=%async_computation.3 | async-start | bytes 1114112 | tf_op jit(solution)/shard_map/reduce_scatter | solution.py:119
  275.5 4.7 copy-start.27
  275.8 90.1 %copy-start.41 = (f32[3,3]{1,0:T(4,128)S(1)}, f32[3,3]{1,0:T(4,128)}, u32[]{:S(2)}) copy-start(f32[3,3]{1,0:T(4,128)} %constant.116) | copy-start | bytes 112
  482.9 21.5 %copy-start.30 = (bf16[2,128,64]{1,2,0:T(8,128)(2,1)S(1)}, bf16[2,128,64]{1,2,0:T(8,128)(2,1)}, u32[]{:S(2)}) copy-start(bf16[2,128,64]{1,2,0:T(8,128)(2,1)} %fusion.71) | copy-start | bytes 98308
  483.4 21.7 %copy-start.35 = (f32[128,128]{0,1:T(8,128)S(1)}, f32[128,128]{0,1:T(8,128)}, u32[]{:S(2)}) copy-start(f32[128,128]{0,1:T(8,128)} %get-tuple-element.17) | copy-start | bytes 196612
  503.2 14.5 %slice-start.5 = ((bf16[4,128,256]{2,1,0:T(8,128)(2,1)}), bf16[1,128,256]{2,1,0:T(8,128)(2,1)S(1)}, s32[]{:S(2)}) async-start(bf16[4,128,256]{2,1,0:T(8,128)(2,1)} %copy-done.17), calls=%async_computation.10 | async-start | bytes 131072 | tf_op jit(solution)/shard_map/slice | solution.py:90
  503.2 14.6 %copy-start.28 = (f32[64,128]{1,0:T(8,128)S(1)}, f32[64,128]{1,0:T(8,128)}, u32[]{:S(2)}) copy-start(f32[64,128]{1,0:T(8,128)} %get-tuple-element.42) | copy-start | bytes 98308
  503.2 14.6 %copy-start.29 = (f32[64,128]{1,0:T(8,128)S(1)}, f32[64,128]{1,0:T(8,128)}, u32[]{:S(2)}) copy-start(f32[64,128]{1,0:T(8,128)} %get-tuple-element.43) | copy-start | bytes 98308
  504.7 6.4 %collective-permute-start.9 = (bf16[2,128,128]{2,1,0:T(8,128)(2,1)S(1)}, bf16[2,128,128]{2,1,0:T(8,128)(2,1)S(1)}, u32[]{:S(2)}, u32[]{:S(2)}) collective-permute-start(bf16[2,128,128]{2,1,0:T(8,128)(2,1)S(1)} %pad_maximum_fusion.25), channel_id=1, source_target_pairs={{0,1},{1,2},{2,3},{3,4},{4,5},{5,6},{6,7},{7,8},{8,9},{9,10},{10,1... | collective-permute-start | bytes 196616 | tf_op jit(solution)/shard_map/ppermute | solution.py:11
  517.8 7.1 %collective-permute-start.10 = (bf16[2,128,256]{2,1,0:T(8,128)(2,1)S(1)}, bf16[2,128,256]{2,1,0:T(8,128)(2,1)S(1)}, u32[]{:S(2)}, u32[]{:S(2)}) collective-permute-start(bf16[2,128,256]{2,1,0:T(8,128)(2,1)S(1)} %pad_maximum_fusion.21), channel_id=1, source_target_pairs={{0,1},{1,2},{2,3},{3,4},{4,5},{5,6},{6,7},{7,8},{8,9},{9,10},{10,1... | collective-permute-start | bytes 393224 | tf_op jit(solution)/shard_map/ppermute | solution.py:11
  517.8 7.1 %copy-start.18 = (bf16[4,128,256]{2,1,0:T(8,128)(2,1)S(1)}, bf16[4,128,256]{2,1,0:T(8,128)(2,1)}, u32[]{:S(2)}) copy-start(bf16[4,128,256]{2,1,0:T(8,128)(2,1)} %copy-done.17) | copy-start | bytes 786436
  517.9 7.1 %slice-start.6 = ((bf16[4,128,256]{2,1,0:T(8,128)(2,1)}), bf16[3,128,256]{2,1,0:T(8,128)(2,1)S(1)}, s32[]{:S(2)}) async-start(bf16[4,128,256]{2,1,0:T(8,128)(2,1)} %copy-done.17), calls=%async_computation.11 | async-start | bytes 393216 | tf_op jit(solution)/shard_map/slice | solution.py:93
  533.6 8.5 %collective-permute-start.11 = (bf16[2,128,512]{2,1,0:T(8,128)(2,1)S(1)}, bf16[2,128,512]{2,1,0:T(8,128)(2,1)S(1)}, u32[]{:S(2)}, u32[]{:S(2)}) collective-permute-start(bf16[2,128,512]{2,1,0:T(8,128)(2,1)S(1)} %pad_maximum_fusion.17), channel_id=1, source_target_pairs={{0,1},{1,2},{2,3},{3,4},{4,5},{5,6},{6,7},{7,8},{8,9},{9,10},{10,1... | collective-permute-start | bytes 786440 | tf_op jit(solution)/shard_map/ppermute | solution.py:11
  551.8 5.4 copy-start.39
  (22 other events, 43.8 us)
Sparse Core Ops, SparseCore 0:
  54.8 58.6 reduce-scatter.2
  273.6 92.3 all-reduce.2
  370.6 57.2 reduce-scatter.4
where the time goes:
time: 582 us; the launch traced here: 574 us
  waiting for transfers between devices  239 us (41%)
  matrix products  133 us (23%)
  blocking collectives  79.7 us (14%)
  other arithmetic  54.5 us (9%)
  local copies, waits for them, and re-layouts  27.3 us (5%)
  starting transfers between devices  25.5 us (4%)
  between operations  15.6 us (3%)
    reduce_scatter x2, waiting for transfers between devices, owned_modes(): owned = lax.psum_scatter(term_all, 'row', scatter_dimension=0, tiled=True)  114 us
    psum x1, waiting for transfers between devices, per_device(): skip_total, detail_total = lax.psum((skip_local, detail_local), 'row')  85.2 us
    dot_general x24, matrix products, precise(): jnp.einsum(form, first_in, second_in, precision=lax.Precision.HIGHEST)  64.8 us
    dot_general x54, matrix products, narrow(): jnp.einsum(form, first_in, second_in, preferred_element_type=jnp.float32)  64.5 us
    all_gather x2, blocking collectives, owned_image(): imag_piece = lax.all_gather(imag_owned, 'row', axis=0, tiled=True)  41.9 us
    ppermute x12, waiting for transfers between devices, shifted(): lax.ppermute(shard, axis, [(i, (i + by) % size) for i in range(size)])  39 us
    all_gather x2, blocking collectives, owned_image(): real_piece = lax.all_gather(real_owned, 'row', axis=0, tiled=True)  37.8 us
    another operation x12, other arithmetic, combine_rows(): stacked = jnp.stack(parities, axis=1)  34.9 us
  transfers between devices with their start and end apart: 15, of which 15 were waited for; matrix products, arithmetic and copies ran while one was open for 6% of the time, Pallas kernels for 0%

commit v1 on v0

--- a/solution.py
+++ b/solution.py
@@ -1,9 +1,226 @@
+import functools
 import math
 
 import jax
 import jax.numpy as jnp
 from jax import lax
+from jax.experimental import pallas as pl
+from jax.experimental.pallas import tpu as pltpu
 from jax.sharding import PartitionSpec as P
+
+MESH = pl.DeviceIdType.MESH
+HIGHEST = lax.Precision.HIGHEST
+NN = (((1,), (0,)), ((), ()))
+NT = (((1,), (1,)), ((), ()))
+TN = (((0,), (0,)), ((), ()))
+
+
+def enter_together(size):
+    me = lax.axis_index("row")
+    barrier = pltpu.get_barrier_semaphore()
+
+    def greet(step, carry):
+        pl.semaphore_signal(
+            barrier, inc=1, device_id={"row": lax.rem(me + step, size)}, device_id_type=MESH
+        )
+        return carry
+
+    lax.fori_loop(1, size, greet, 0)
+    pl.semaphore_wait(barrier, size - 1)
+
+
+def exchange(size, tile, send, land, send_sem, recv_sem):
+    me = lax.axis_index("row")
+
+    def copy(step, partner, place):
+        return pltpu.make_async_remote_copy(
+            src_ref=send.at[pl.ds(pl.multiple_of(partner * tile, tile), tile)],
+            dst_ref=land.at[pl.ds(pl.multiple_of(place * tile, tile), tile)],
+            send_sem=send_sem.at[step],
+            recv_sem=recv_sem.at[step],
+            device_id={"row": partner},
+            device_id_type=MESH,
+        )
+
+    def start(step, carry):
+        copy(step, lax.rem(me + step, size), me).start()
+        return carry
+
+    def finish(step, carry):
+        source = lax.rem(me + size - step, size)
+        copy(step, source, source).wait_recv()
+        copy(step, lax.rem(me + step, size), me).wait_send()
+        return carry
+
+    lax.fori_loop(1, size, start, 0)
+    own = pl.ds(pl.multiple_of(me * tile, tile), tile)
+    land[own, :] = send[own, :]
+    lax.fori_loop(1, size, finish, 0)
+
+
+def spectral_kernel(
+    size,
+    near_cols,
+    back,
+    coarse_ref,
+    col_ref,
+    row_ref,
+    row_inv_ref,
+    col_inv_ref,
+    weight_hbm,
+    image_ref,
+    spec_ref,
+    weight,
+    send_a,
+    land_a,
+    send_b,
+    send_c,
+    land_c,
+    send_d,
+    land_d,
+    rotated,
+    weight_sem,
+    send_sem,
+    recv_sem,
+):
+    fetch = pltpu.make_async_copy(weight_hbm, weight, weight_sem)
+    fetch.start()
+    enter_together(size)
+    rows = coarse_ref.shape[0]
+    total = None
+    for row in range(rows):
+        part = lax.dot_general(
+            col_ref[row],
+            coarse_ref[row].astype(jnp.float32),
+            NT,
+            precision=HIGHEST,
+            preferred_element_type=jnp.float32,
+        )
+        total = part if total is None else total + part
+    send_a[...] = total
+    tile_a = send_a.shape[0] // size
+    exchange(size, tile_a, send_a, land_a, send_sem.at[0], recv_sem.at[0])
+    send_b[...] = lax.dot_general(
+        row_ref[...], land_a[...], NN, precision=HIGHEST, preferred_element_type=jnp.float32
+    )
+    tile_b = send_b.shape[0] // size
+    exchange(size, tile_b, send_b, spec_ref, send_sem.at[1], recv_sem.at[1])
+    spec = spec_ref[...]
+    count = spec.shape[0]
+    even = lax.broadcasted_iota(jnp.int32, spec.shape, 0) % 2 == 0
+    turned = jnp.where(even, -pltpu.roll(spec, count - 1, 0), pltpu.roll(spec, 1, 0))
+    rotated[...] = -turned if back else turned
+    fetch.wait()
+    per_tile = tile_b // 2
+    modes = weight.shape[1]
+    per_row = near_cols
+    mode_rows = per_tile // per_row
+    dims = NT if back else NN
+
+    def mix(source, carry):
+        here = pl.ds(pl.multiple_of(source * tile_b, tile_b), tile_b)
+        plain = spec_ref[here, :].astype(jnp.bfloat16)
+        turn = rotated[here, :].astype(jnp.bfloat16)
+        pair = lax.broadcasted_iota(jnp.int32, (tile_b, plain.shape[1]), 0) // 2
+        result = jnp.zeros((tile_b, plain.shape[1]), jnp.float32)
+        for member in range(per_tile):
+            mode = (member // per_row) * (modes // mode_rows) + source * per_row + member % per_row
+            one = lax.dot_general(
+                plain,
+                weight[0, mode].astype(jnp.bfloat16),
+                dims,
+                preferred_element_type=jnp.float32,
+            )
+            two = lax.dot_general(
+                turn,
+                weight[1, mode].astype(jnp.bfloat16),
+                dims,
+                preferred_element_type=jnp.float32,
+            )
+            result = jnp.where(pair == member, one + two, result)
+        send_c[here, :] = result
+        return carry
+
+    lax.fori_loop(0, size, mix, 0)
+    exchange(size, tile_b, send_c, land_c, send_sem.at[2], recv_sem.at[2])
+    send_d[...] = lax.dot_general(
+        row_inv_ref[...], land_c[...], NN, precision=HIGHEST, preferred_element_type=jnp.float32
+    )
+    exchange(size, tile_a, send_d, land_d, send_sem.at[3], recv_sem.at[3])
+    across = land_d[...].T
+    for row in range(rows):
+        image_ref[row] = lax.dot_general(
+            across, col_inv_ref[row], NN, precision=HIGHEST, preferred_element_type=jnp.float32
+        ).astype(jnp.bfloat16)
+
+
+def spectral_tables(row_modes, col_modes, local_rows, columns, size):
+    height = local_rows * size
+    mode_rows, mode_cols = row_modes.shape[0], col_modes.shape[0]
+    near_rows, near_cols = mode_rows // size, mode_cols // size
+    cos_col, sin_col = column_tables(col_modes, columns)
+    cos_row, sin_row = row_tables(row_modes, jnp.arange(height, dtype=jnp.int32), height)
+    same_row = jnp.eye(local_rows, dtype=jnp.float32)
+    wave = jnp.stack([cos_col.T, -sin_col.T], axis=1).reshape(size, near_cols, 2, columns)
+    col = jnp.einsum("hg,dmrw->gdhmrw", same_row, wave).reshape(local_rows, -1, columns)
+    col_inv = col
+    turn = jnp.stack(
+        [jnp.stack([cos_row, sin_row], axis=-1), jnp.stack([-sin_row, cos_row], axis=-1)], axis=2
+    )
+    same_col = jnp.eye(near_cols, dtype=jnp.float32)
+    row = jnp.einsum("phrs,mn->pmrhns", turn, same_col)
+    row = row.reshape(mode_rows * near_cols * 2, height * near_cols * 2)
+    row_inv = row.T * (1.0 / (height * columns))
+    return col, row, row_inv, col_inv
+
+
+def spectral_path(coarse, weight, tables, near_cols, back):
+    col, row, row_inv, col_inv = tables
+    size = lax.axis_size("row")
+    local_rows, channels, columns = coarse.shape
+    count_a, count_b = col.shape[1], row.shape[0]
+    f32 = jnp.float32
+    vmem = pl.BlockSpec(memory_space=pltpu.VMEM)
+    image, spec = pl.pallas_call(
+        functools.partial(spectral_kernel, size, near_cols, back),
+        out_shape=(
+            jax.ShapeDtypeStruct(coarse.shape, jnp.bfloat16),
+            jax.ShapeDtypeStruct((count_b, channels), f32),
+        ),
+        in_specs=[vmem] * 5 + [pl.BlockSpec(memory_space=pl.ANY)],
+        out_specs=(vmem, vmem),
+        scratch_shapes=[
+            pltpu.VMEM(weight.shape, f32),
+            pltpu.VMEM((count_a, channels), f32),
+            pltpu.VMEM((count_a, channels), f32),
+            pltpu.VMEM((count_b, channels), f32),
+            pltpu.VMEM((count_b, channels), f32),
+            pltpu.VMEM((count_b, channels), f32),
+            pltpu.VMEM((count_a, channels), f32),
+            pltpu.VMEM((count_a, channels), f32),
+            pltpu.VMEM((count_b, channels), f32),
+            pltpu.SemaphoreType.DMA,
+            pltpu.SemaphoreType.DMA((4, size)),
+            pltpu.SemaphoreType.DMA((4, size)),
+        ],
+        compiler_params=pltpu.CompilerParams(
+            collective_id=1 if back else 0,
+            has_side_effects=True,
+            vmem_limit_bytes=40 * 1024 * 1024,
+        ),
+        cost_estimate=pl.CostEstimate(
+            flops=8 * weight.size, bytes_accessed=4 * weight.size, transcendentals=0
+        ),
+        name="spectral_back" if back else "spectral",
+    )(coarse, col, row, row_inv, col_inv, weight)
+    return image, spec
+
+
+def spec_parts(spec, mode_rows, mode_cols, size):
+    channels = spec.shape[1]
+    grid = spec.reshape(size, mode_rows // size, mode_cols // size, 2, channels)
+    grid = jnp.transpose(grid, (3, 1, 0, 2, 4)).reshape(2, -1, channels)
+    return grid[0], grid[1]
 
 
 def shifted(shard, axis, by):
@@ -193,9 +410,22 @@
     factor = 1.0 / (height * columns)
     weight_real = spectral_weight[0]
     weight_imag = spectral_weight[1]
-    spec_real, spec_imag = owned_modes(coarse_field, row_modes, col_modes)
-    out_real, out_imag = mix_modes(spec_real, spec_imag, weight_real, weight_imag, factor)
-    coarse_image = owned_image(out_real, out_imag, row_modes, col_modes, local_rows, columns)
+    mode_rows, mode_cols = row_modes.shape[0], col_modes.shape[0]
+    whole_tiles = (
+        mode_rows % devices == 0
+        and mode_cols % devices == 0
+        and (2 * local_rows * mode_cols // devices) % 8 == 0
+        and (2 * (mode_rows // devices) * (mode_cols // devices)) % 8 == 0
+    )
+    if whole_tiles:
+        near_cols = mode_cols // devices
+        tables = spectral_tables(row_modes, col_modes, local_rows, columns, devices)
+        coarse_image, spec = spectral_path(coarse_field, spectral_weight, tables, near_cols, False)
+        spec_real, spec_imag = spec_parts(spec, mode_rows, mode_cols, devices)
+    else:
+        spec_real, spec_imag = owned_modes(coarse_field, row_modes, col_modes)
+        out_real, out_imag = mix_modes(spec_real, spec_imag, weight_real, weight_imag, factor)
+        coarse_image = owned_image(out_real, out_imag, row_modes, col_modes, local_rows, columns)
     mixed_field = [
         tuple(
             (
@@ -211,11 +441,17 @@
     activation_in = rebuilt_field + narrow("hcw,co->how", field, skip_weight)
     upstream = jax.vjp(jax.nn.gelu, activation_in)[1](as_float(cotangent))[0].astype(jnp.bfloat16)
     coarse_slope, bands_slope = analysis(upstream, row_filters, matrices)
-    back_real, back_imag = owned_modes(coarse_slope, row_modes, col_modes)
-    turned_real, turned_imag = mix_modes_back(
-        back_real, back_imag, weight_real, weight_imag, factor
-    )
-    image_back = owned_image(turned_real, turned_imag, row_modes, col_modes, local_rows, columns)
+    if whole_tiles:
+        image_back, spec = spectral_path(coarse_slope, spectral_weight, tables, near_cols, True)
+        back_real, back_imag = spec_parts(spec, mode_rows, mode_cols, devices)
+    else:
+        back_real, back_imag = owned_modes(coarse_slope, row_modes, col_modes)
+        turned_real, turned_imag = mix_modes_back(
+            back_real, back_imag, weight_real, weight_imag, factor
+        )
+        image_back = owned_image(
+            turned_real, turned_imag, row_modes, col_modes, local_rows, columns
+        )
     back_bands = [
         tuple(
             (

time: 582 us -> 340 us (0.58); the launches traced: 574 us -> 339 us
  waiting for transfers between devices: 239 us -> 91.2 us
  blocking collectives: 79.7 us -> 0 us
  matrix products: 133 us -> 63.1 us
  Pallas kernels: 0 us -> 55.7 us
  local copies, waits for them, and re-layouts: 27.3 us -> 34.8 us
    reduce_scatter x2 -> x0, waiting for transfers between devices: 114 us -> none  [owned_modes(): owned = lax.psum_scatter(term_all, 'row', scatter_dimension=0, tiled=True)]
    all_gather x4 -> x0, blocking collectives: 79.7 us -> none  [the longest x2 41.9 us: owned_image(): imag_piece = lax.all_gather(imag_owned, 'row', axis=0, tiled=True)]
    dot_general x24 -> x0, matrix products: 64.8 us -> none  [precise(): jnp.einsum(form, first_in, second_in, precision=lax.Precision.HIGHEST)]
    pallas_call x0 -> x2, Pallas kernels: none -> 55.7 us  [spectral_path(): pl.pallas_call(functools.partial(spectral_kernel, size, near_cols, back),...]
    psum x1, waiting for transfers between devices: 85.2 us -> 63.1 us  [per_device(): skip_total, detail_total = lax.psum((skip_local, detail_local), 'row')]
    ppermute x12, waiting for transfers between devices: 39 us -> 28.2 us  [shifted(): lax.ppermute(shard, axis, [(i, (i + by) % size) for i in range(size)])]
    reshape x0 -> x4, local copies, waits for them, and re-layouts: none -> 7.32 us  [the longest x2 7.25 us: spectral_tables(): row = row.reshape(mode_rows * near_cols * 2, height * near_cols * 2)]
  transfers between devices with their start and end apart: 15 -> 13, of which waited for: 15 -> 9; matrix products, arithmetic and copies ran while one was open for 6% -> 16% of each run, Pallas kernels for 0% -> 0%
where the time goes in v1:
time: 340 us; the launch traced here: 339 us
  waiting for transfers between devices  91.2 us (27%)
  matrix products  63.1 us (19%)
  other arithmetic  58.6 us (17%)
  Pallas kernels  55.7 us (16%)
  local copies, waits for them, and re-layouts  34.8 us (10%)
  starting transfers between devices  20.2 us (6%)
  between operations  15.4 us (5%)
    dot_general x54, matrix products, narrow(): jnp.einsum(form, first_in, second_in, preferred_element_type=jnp.float32)  63.1 us
    psum x1, waiting for transfers between devices, per_device(): skip_total, detail_total = lax.psum((skip_local, detail_local), 'row')  63.1 us
    pallas_call x2, Pallas kernels, spectral_path(): pl.pallas_call(functools.partial(spectral_kernel, size, near_cols, back),...  55.7 us
    another operation x12, other arithmetic, combine_rows(): stacked = jnp.stack(parities, axis=1)  35.9 us
    ppermute x12, waiting for transfers between devices, shifted(): lax.ppermute(shard, axis, [(i, (i + by) % size) for i in range(size)])  28.2 us
    ppermute x12, starting transfers between devices, shifted(): lax.ppermute(shard, axis, [(i, (i + by) % size) for i in range(size)])  20.1 us
    unnamed x78, local copies, waits for them, and re-layouts  9.53 us
    another operation x1, other arithmetic, per_device(): grad_spectral = jnp.stack([grad_real, grad_imag])  8.04 us
  transfers between devices with their start and end apart: 13, of which 9 were waited for; matrix products, arithmetic and copies ran while one was open for 16% of the time, Pallas kernels for 0%

profile of v1, /device:TPU:0, one launch (start us, length us, event | category | flops | bytes accessed | tf_op | source)
XLA Modules:
  0.0 339.0 jit_solution(15008888875959638908)
XLA Ops:
  8.2 5.5 %collective-permute-start = (bf16[2,128,512]{2,1,0:T(8,128)(2,1)S(1)}, bf16[2,128,512]{2,1,0:T(8,128)(2,1)S(1)}, u32[]{:S(2)}, u32[]{:S(2)}) collective-permute-start(bf16[2,128,512]{2,1,0:T(8,128)(2,1)S(1)} %slice.231), channel_id=1, source_target_pairs={{0,15},{1,0},{2,1},{3,2},{4,3},{5,4},{6,5},{7,6},{8,7},{9,8},{10,9... | collective-permute-start | bytes 786440 | tf_op jit(solution)/shard_map/ppermute | solution.py:228
  16.0 4.2 %multiply_bitcast_fusion = f32[32,2,2,32,2,2]{5,4,3,2,1,0:T(2,128)} fusion(f32[32,32,2,2]{3,1,2,0:T(8,128)S(1)} %copy.68, f32[2,2]{1,0:T(2,128)S(1)} %compare_convert_fusion), kind=kLoop, calls=%fused_computation.21 | loop fusion | flops 16384 | bytes 81936 | tf_op jit(solution)/shard_map/phrs,mn->pmrhns/transpose | solution.py:171
  20.2 7.2 %reshape.280.row_ref = f32[128,128]{1,0:T(8,128)S(1)} reshape(f32[32,2,2,32,2,2]{5,4,3,2,1,0:T(2,128)} %multiply_bitcast_fusion) | data formatting | bytes 131072 | tf_op jit(solution)/shard_map/reshape | solution.py:172
  28.8 3.1 convolution_convert_fusion.5
  32.9 3.6 %convolution_convert_fusion.7 = bf16[8,128,512]{2,1,0:T(8,128)(2,1)S(1)} fusion(f32[18,128,512]{2,1,0:T(8,128)S(1)} %maximum_convert_fusion, f32[]{:T(128)} %bitcast.3, f32[]{:T(128)} %bitcast.2, f32[]{:T(128)} %bitcast.1, f32[]{:T(128)} %bitcast, bf16[512,512]{1,0:T(8,128)(2,1)S(1)} %copy-done), kind=kOutput, calls=%fused_computation.67 | convolution fusion | flops 541589504 | bytes 9961488 | tf_op jit(solution)/shard_map/hcw,wv->hcv/dot_general | solution.py:240
  38.2 1.7 collective-permute-done.1
  39.9 2.9 convolution_convert_fusion.21
  42.8 2.6 convolution_convert_fusion.19
  45.9 4.6 %collective-permute-start.2 = (bf16[2,128,128]{2,1,0:T(8,128)(2,1)S(1)}, bf16[2,128,128]{2,1,0:T(8,128)(2,1)S(1)}, u32[]{:S(2)}, u32[]{:S(2)}) collective-permute-start(bf16[2,128,128]{2,1,0:T(8,128)(2,1)S(1)} %slice.576), channel_id=1, source_target_pairs={{0,15},{1,0},{2,1},{3,2},{4,3},{5,4},{6,5},{7,6},{8,7},{9,8},{10,9... | collective-permute-start | bytes 196616 | tf_op jit(solution)/shard_map/ppermute | solution.py:228
  50.9 1.6 collective-permute-done.2
  52.5 2.5 convolution_convert_fusion.34
  55.1 2.7 convolution_convert_fusion.37
  58.6 27.3 %spectral.1 = (bf16[2,128,64]{2,1,0:T(8,128)(2,1)S(1)}, f32[128,128]{1,0:T(8,128)S(1)}) custom-call(bf16[2,128,64]{2,1,0:T(8,128)(2,1)S(1)} %bitcast.281, f32[2,128,64]{2,1,0:T(8,128)S(1)} %bitcast.277, f32[128,128]{1,0:T(8,128)S(1)} %reshape.280.row_ref, f32[128,128]{1,0:T(8,128)S(1)} %multiply_bitcast_fusion.1.row_inv_ref, f32[2,128,64]{2,1,0:T(8,128)S(1)} %bitcast.278, ...), custom_call_target="tpu_custom_call" | custom-call | flops 16777216 | bytes 8388608 | tf_op jit(solution)/shard_map/spectral/pallas_call | solution.py:184
  86.6 6.0 %collective-permute-done.3 = bf16[2,128,128]{2,1,0:T(8,128)(2,1)S(1)} collective-permute-done((bf16[2,128,128]{2,1,0:T(8,128)(2,1)S(1)}, bf16[2,128,128]{2,1,0:T(8,128)(2,1)S(1)}, u32[]{:S(2)}, u32[]{:S(2)}) %collective-permute-start.3) | collective-permute-done | bytes 65568 | tf_op jit(solution)/shard_map/ppermute | solution.py:228
  92.6 5.0 %fusion.147 = (bf16[2,1,128,128]{3,2,0,1:T(8,128)(2,1)S(1)}, bf16[2,1,128,128]{3,2,0,1:T(8,128)(2,1)S(1)}) fusion(bf16[2,128,128]{2,1,0:T(8,128)(2,1)S(1)} %convolution_convert_fusion.33, bf16[2,128,128]{2,1,0:T(8,128)(2,1)S(1)} %convolution_convert_fusion.35, f32[]{:T(128)} %bitcast.19, f32[]{:T(128)} %bitcast.17, f32[]{:T(128)} %bitcast.2, f32[]{:T(128)} %bitcast, ...), kind=kLoop, calls=%fused_computation.298 | loop fusion | flops 720896 | bytes 393248 | tf_op jit(solution)/shard_map/stack | solution.py:293
  98.5 1.2 convolution_convert_fusion.20
  101.2 5.9 %collective-permute-done.4 = bf16[2,128,256]{2,1,0:T(8,128)(2,1)S(1)} collective-permute-done((bf16[2,128,256]{2,1,0:T(8,128)(2,1)S(1)}, bf16[2,128,256]{2,1,0:T(8,128)(2,1)S(1)}, u32[]{:S(2)}, u32[]{:S(2)}) %collective-permute-start.4) | collective-permute-done | bytes 131104 | tf_op jit(solution)/shard_map/ppermute | solution.py:228
  107.1 5.2 %fusion.95 = (bf16[4,1,128,256]{3,2,0,1:T(8,128)(2,1)S(1)}, bf16[4,1,128,256]{3,2,0,1:T(8,128)(2,1)S(1)}) fusion(bf16[4,128,256]{2,1,0:T(8,128)(2,1)S(1)} %copy-done.17, bf16[4,128,256]{2,1,0:T(8,128)(2,1)S(1)} %convolution_convert_fusion.20, f32[]{:T(128)} %bitcast.19, f32[]{:T(128)} %bitcast.17, f32[]{:T(128)} %bitcast.2, f32[]{:T(128)} %bitcast, ...), kind=kLoop, calls=%fused_computation.211 | loop fusion | flops 2883584 | bytes 1572896 | tf_op jit(solution)/shard_map/stack | solution.py:293
  113.5 1.8 convolution_convert_fusion.6
  116.2 7.7 %collective-permute-done.5 = bf16[2,128,512]{2,1,0:T(8,128)(2,1)S(1)} collective-permute-done((bf16[2,128,512]{2,1,0:T(8,128)(2,1)S(1)}, bf16[2,128,512]{2,1,0:T(8,128)(2,1)S(1)}, u32[]{:S(2)}, u32[]{:S(2)}) %collective-permute-start.5) | collective-permute-done | bytes 262176 | tf_op jit(solution)/shard_map/ppermute | solution.py:228
  124.0 6.1 %fusion.13 = (f32[8,1,128,512]{3,2,0,1:T(8,128)S(1)}, f32[8,1,128,512]{3,2,0,1:T(8,128)S(1)}) fusion(bf16[8,128,512]{2,1,0:T(8,128)(2,1)S(1)} %convolution_convert_fusion.6, bf16[8,128,512]{2,1,0:T(8,128)(2,1)S(1)} %copy-done.6, f32[]{:T(128)} %bitcast.19, f32[]{:T(128)} %bitcast.17, f32[]{:T(128)} %bitcast.2, f32[]{:T(128)} %bitcast, ...), kind=kLoop, calls=%fused_computation.43 | loop fusion | flops 10485760 | bytes 8388640 | tf_op jit(solution)/shard_map/stack | solution.py:293
  133.0 4.0 %fusion.2 = bf16[16,128,512]{2,1,0:T(8,128)(2,1)S(1)} fusion(bf16[16,128,512]{2,1,0:T(8,128)(2,1)S(1)} %copy-done.31, f32[8,2,128,512]{3,2,1,0:T(8,128)S(1)} %copy.90, bf16[16,128,512]{2,1,0:T(8,128)(2,1)S(1)} %copy-done.2, bf16[128,128]{1,0:T(8,128)(2,1)S(1)} %copy-done.27), kind=kOutput, calls=%fused_computation.7 | convolution fusion | flops 291504128 | bytes 10518528 | tf_op jit(solution)/shard_map/hcw,co->how/dot_general | solution.py:240
  137.1 1.3 convolution_bitcast_fusion
  138.5 2.5 collective-permute-done.6
  141.3 3.3 convolution_convert_fusion.3
  144.7 3.2 convolution_convert_fusion.1
  150.1 4.9 %collective-permute-start.7 = (bf16[2,128,256]{2,1,0:T(8,128)(2,1)S(1)}, bf16[2,128,256]{2,1,0:T(8,128)(2,1)S(1)}, u32[]{:S(2)}, u32[]{:S(2)}) collective-permute-start(bf16[2,128,256]{2,1,0:T(8,128)(2,1)S(1)} %slice.607), channel_id=1, source_target_pairs={{0,15},{1,0},{2,1},{3,2},{4,3},{5,4},{6,5},{7,6},{8,7},{9,8},{10,9... | collective-permute-start | bytes 393224 | tf_op jit(solution)/shard_map/ppermute | solution.py:228
  155.7 1.2 fusion.29
  158.8 3.1 convolution_convert_fusion.17
  161.9 2.6 convolution_convert_fusion.15
  166.8 3.5 %collective-permute-start.8 = (bf16[2,128,128]{2,1,0:T(8,128)(2,1)S(1)}, bf16[2,128,128]{2,1,0:T(8,128)(2,1)S(1)}, u32[]{:S(2)}, u32[]{:S(2)}) collective-permute-start(bf16[2,128,128]{2,1,0:T(8,128)(2,1)S(1)} %slice.609), channel_id=1, source_target_pairs={{0,15},{1,0},{2,1},{3,2},{4,3},{5,4},{6,5},{7,6},{8,7},{9,8},{10,9... | collective-permute-start | bytes 196616 | tf_op jit(solution)/shard_map/ppermute | solution.py:228
  170.3 1.9 collective-permute-done.8
  172.2 2.5 convolution_convert_fusion.30
  174.7 2.8 convolution_convert_fusion.32
  178.7 28.4 %spectral_back.1 = (bf16[2,128,64]{2,1,0:T(8,128)(2,1)S(1)}, f32[128,128]{1,0:T(8,128)S(1)}) custom-call(bf16[2,128,64]{2,1,0:T(8,128)(2,1)S(1)} %bitcast.282, f32[2,128,64]{2,1,0:T(8,128)S(1)} %bitcast.279, f32[128,128]{1,0:T(8,128)S(1)} %reshape.280.row_ref, f32[128,128]{1,0:T(8,128)S(1)} %multiply_bitcast_fusion.1.row_inv_ref, ...), custom_call_target="tpu_custom_call" | custom-call | flops 16777216 | bytes 8388608 | tf_op jit(solution)/shard_map/spectral_back/pallas_call | solution.py:184
  208.7 4.6 %add_multiply_fusion = (f32[1,64,128,128]{3,2,1,0:T(8,128)}, f32[1,64,128,128]{3,2,1,0:T(8,128)}) fusion(f32[64,128]{1,0:T(8,128)S(1)} %bitcast.295, f32[64,128]{1,0:T(8,128)S(1)} %bitcast.293, f32[64,128]{1,0:T(8,128)S(1)} %bitcast.294, f32[64,128]{1,0:T(8,128)S(1)} %bitcast.292), kind=kLoop, calls=%fused_computation.20 | loop fusion | flops 8388608 | bytes 8519680 | tf_op jit(solution)/shard_map/mul | solution.py:495
  214.1 5.0 %fusion.145 = (bf16[2,1,128,128]{3,2,0,1:T(8,128)(2,1)S(1)}, bf16[2,1,128,128]{3,2,0,1:T(8,128)(2,1)S(1)}) fusion(bf16[2,128,128]{2,1,0:T(8,128)(2,1)S(1)} %convolution_convert_fusion.29, bf16[2,128,128]{2,1,0:T(8,128)(2,1)S(1)} %convolution_convert_fusion.31, f32[]{:T(128)} %bitcast.19, f32[]{:T(128)} %bitcast.17, f32[]{:T(128)} %bitcast.2, f32[]{:T(128)} %bitcast, ...), kind=kLoop, calls=%fused_computation.296 | loop fusion | flops 720896 | bytes 393248 | tf_op jit(solution)/shard_map/stack | solution.py:293
  219.3 1.2 convolution_convert_fusion.16
  220.6 8.0 %pad_maximum_fusion = f32[2,64,128,128]{3,2,1,0:T(8,128)} fusion(f32[1,64,128,128]{3,2,1,0:T(8,128)} %get-tuple-element.43, f32[1,64,128,128]{3,2,1,0:T(8,128)} %get-tuple-element.42), kind=kLoop, calls=%fused_computation | loop fusion | flops 2097152 | bytes 16777216 | tf_op jit(solution)/shard_map/stack | solution.py:503
  228.7 5.2 %fusion.93 = (bf16[4,1,128,256]{3,2,0,1:T(8,128)(2,1)S(1)}, bf16[4,1,128,256]{3,2,0,1:T(8,128)(2,1)S(1)}) fusion(bf16[4,128,256]{2,1,0:T(8,128)(2,1)S(1)} %copy-done.15, bf16[4,128,256]{2,1,0:T(8,128)(2,1)S(1)} %convolution_convert_fusion.16, f32[]{:T(128)} %bitcast.19, f32[]{:T(128)} %bitcast.17, f32[]{:T(128)} %bitcast.2, f32[]{:T(128)} %bitcast, ...), kind=kLoop, calls=%fused_computation.209 | loop fusion | flops 2883584 | bytes 1572896 | tf_op jit(solution)/shard_map/stack | solution.py:293
  235.0 2.0 convolution_convert_fusion.2
  238.5 63.1 %all-reduce.3.cloned.1.call-done = (f32[3,3,128,128]{3,2,1,0:T(8,128)}, f32[128,128]{0,1:T(8,128)}) async-done(((f32[3,3,128,128]{3,2,1,0:T(8,128)}, f32[128,128]{0,1:T(8,128)}), (f32[3,3,128,128]{3,2,1,0:T(8,128)}, f32[128,128]{0,1:T(8,128)})) %all-reduce.3.cloned.1.call-update) | async-done | bytes 655376 | tf_op jit(solution)/shard_map/psum | solution.py:480
  303.2 2.1 broadcast_multiply_fusion
  305.3 7.9 %fusion.21 = (f32[8,1,128,512]{3,2,0,1:T(8,128)S(1)}, f32[8,1,128,512]{3,2,0,1:T(8,128)S(1)}) fusion(bf16[8,128,512]{2,1,0:T(8,128)(2,1)} %copy-done.7, bf16[8,128,512]{2,1,0:T(8,128)(2,1)S(1)} %copy-done.4, f32[]{:T(128)} %bitcast.19, f32[]{:T(128)} %bitcast.17, f32[]{:T(128)} %bitcast.2, f32[]{:T(128)} %bitcast, bf16[7,128,512]{2,1,0:T(8,128)(2,1)} %slice.637, ...), kind=kLoop, calls=%fused_computation.51 | loop fusion | flops 10485760 | bytes 8388640 | tf_op jit(solution)/shard_map/stack | solution.py:293
  313.8 2.7 copy.114
  316.5 5.4 %copy.116 = f32[16,128,512]{1,2,0:T(8,128)} copy(f32[16,128,512]{2,1,0:T(8,128)} %bitcast.285) | data formatting | bytes 8388608 | tf_op jit(solution)/shard_map/reshape | solution.py:294
  321.9 4.9 %bitcast_add_fusion = f32[16,128,512]{1,2,0:T(8,128)} fusion(f32[16,128,512]{1,2,0:T(8,128)} %copy.116, bf16[16,128,512]{2,1,0:T(8,128)(2,1)S(1)} %fusion.2, bf16[128,128]{1,0:T(8,128)(2,1)S(1)} %copy-done.28), kind=kOutput, calls=%fused_computation.17 | convolution fusion | flops 269484032 | bytes 10518528 | tf_op jit(solution)/shard_map/how,co->hcw/dot_general | solution.py:240
  326.8 5.3 %copy.121 = f32[16,128,512]{2,1,0:T(8,128)} copy(f32[16,128,512]{1,2,0:T(8,128)} %bitcast_add_fusion) | data formatting | bytes 8388608
  (221 shorter events, 32.2 us)
Async XLA Ops:
  7.2 21.6 %copy-start = (bf16[512,512]{1,0:T(8,128)(2,1)S(1)}, bf16[512,512]{1,0:T(8,128)(2,1)}, u32[]{:S(2)}) copy-start(bf16[512,512]{1,0:T(8,128)(2,1)} %param.15) | copy-start | bytes 1572868
  7.2 294.4 %all-reduce.3.cloned.1.call-start = ((), (), s32[]{:S(2)}) async-start(), calls=%async_computation | async-start | bytes 1310720 | tf_op jit(solution)/shard_map/psum | solution.py:480
  8.2 20.2 %collective-permute-start = (bf16[2,128,512]{2,1,0:T(8,128)(2,1)S(1)}, bf16[2,128,512]{2,1,0:T(8,128)(2,1)S(1)}, u32[]{:S(2)}, u32[]{:S(2)}) collective-permute-start(bf16[2,128,512]{2,1,0:T(8,128)(2,1)S(1)} %slice.231), channel_id=1, source_target_pairs={{0,15},{1,0},{2,1},{3,2},{4,3},{5,4},{6,5},{7,6},{8,7},{9,8},{10,9... | collective-permute-start | bytes 786440 | tf_op jit(solution)/shard_map/ppermute | solution.py:228
  20.2 7.3 %copy-start.29 = (f32[2,4]{1,0:T(2,128)S(1)}, f32[2,4]{1,0:T(2,128)}, u32[]{:S(2)}) copy-start(f32[2,4]{1,0:T(2,128)} %param.14) | copy-start | bytes 100
  20.2 8.2 %copy-start.1 = (bf16[16,128,512]{2,1,0:T(8,128)(2,1)S(1)}, bf16[16,128,512]{2,1,0:T(8,128)(2,1)}, u32[]{:S(2)}) copy-start(bf16[16,128,512]{2,1,0:T(8,128)(2,1)} %param.12) | copy-start | bytes 6291460
  28.8 3.1 copy-start.11
  32.9 25.7 %slice-start = ((s8[8388608]{0:T(1024)(128)(4,1)}), s8[4194304]{0:T(1024)(128)(4,1)S(1)}, s32[]{:S(2)}) async-start(s8[8388608]{0:T(1024)(128)(4,1)} %bitcast.273), calls=%async_computation.1 | async-start | bytes 8388608
  36.6 22.0 %slice-start.1 = ((s8[8388608]{0:T(1024)(128)(4,1)}), s8[4194304]{0:T(1024)(128)(4,1)S(1)}, s32[]{:S(2)}) async-start(s8[8388608]{0:T(1024)(128)(4,1)} %bitcast.273), calls=%async_computation.2 | async-start | bytes 8388608
  36.6 3.3 collective-permute-start.1
  38.1 4.7 %copy-start.5 = (bf16[8,128,512]{2,1,0:T(8,128)(2,1)}, bf16[8,128,512]{2,1,0:T(8,128)(2,1)S(1)}, u32[]{:S(2)}) copy-start(bf16[8,128,512]{2,1,0:T(8,128)(2,1)S(1)} %convolution_convert_fusion.4) | copy-start | bytes 3145732
  38.1 1.8 copy-start.32
  42.8 43.5 %copy-start.18 = (bf16[4,128,256]{2,1,0:T(8,128)(2,1)}, bf16[4,128,256]{2,1,0:T(8,128)(2,1)S(1)}, u32[]{:S(2)}) copy-start(bf16[4,128,256]{2,1,0:T(8,128)(2,1)S(1)} %convolution_convert_fusion.21) | copy-start | bytes 786436
  42.8 9.7 %copy-start.20 = (bf16[128,128]{1,0:T(8,128)(2,1)S(1)}, bf16[128,128]{1,0:T(8,128)(2,1)}, u32[]{:S(2)}) copy-start(bf16[128,128]{1,0:T(8,128)(2,1)} %param.17) | copy-start | bytes 98308
  45.9 6.5 %collective-permute-start.2 = (bf16[2,128,128]{2,1,0:T(8,128)(2,1)S(1)}, bf16[2,128,128]{2,1,0:T(8,128)(2,1)S(1)}, u32[]{:S(2)}, u32[]{:S(2)}) collective-permute-start(bf16[2,128,128]{2,1,0:T(8,128)(2,1)S(1)} %slice.576), channel_id=1, source_target_pairs={{0,15},{1,0},{2,1},{3,2},{4,3},{5,4},{6,5},{7,6},{8,7},{9,8},{10,9... | collective-permute-start | bytes 196616 | tf_op jit(solution)/shard_map/ppermute | solution.py:228
  50.8 35.7 %copy-start.16 = (bf16[4,128,256]{2,1,0:T(8,128)(2,1)}, bf16[4,128,256]{2,1,0:T(8,128)(2,1)S(1)}, u32[]{:S(2)}) copy-start(bf16[4,128,256]{2,1,0:T(8,128)(2,1)S(1)} %convolution_convert_fusion.18) | copy-start | bytes 786436
  55.1 30.8 %copy-start.22 = (bf16[2,128,128]{1,2,0:T(8,128)(2,1)}, bf16[2,128,128]{1,2,0:T(8,128)(2,1)S(1)}, u32[]{:S(2)}) copy-start(bf16[2,128,128]{1,2,0:T(8,128)(2,1)S(1)} %convolution_convert_fusion.34) | copy-start | bytes 196612
  85.9 14.1 %copy-start.9 = (bf16[8,128,512]{2,1,0:T(8,128)(2,1)S(1)}, bf16[8,128,512]{2,1,0:T(8,128)(2,1)}, u32[]{:S(2)}) copy-start(bf16[8,128,512]{2,1,0:T(8,128)(2,1)} %copy-done.8) | copy-start | bytes 3145732
  86.2 6.4 %collective-permute-start.3 = (bf16[2,128,128]{2,1,0:T(8,128)(2,1)S(1)}, bf16[2,128,128]{2,1,0:T(8,128)(2,1)S(1)}, u32[]{:S(2)}, u32[]{:S(2)}) collective-permute-start(bf16[2,128,128]{2,1,0:T(8,128)(2,1)S(1)} %pad_maximum_fusion.21), channel_id=1, source_target_pairs={{0,1},{1,2},{2,3},{3,4},{4,5},{5,6},{6,7},{7,8},{8,9},{9,10},{10,1... | collective-permute-start | bytes 196616 | tf_op jit(solution)/shard_map/ppermute | solution.py:228
  86.6 13.2 %slice-start.9 = ((bf16[4,128,256]{2,1,0:T(8,128)(2,1)}), bf16[1,128,256]{2,1,0:T(8,128)(2,1)S(1)}, s32[]{:S(2)}) async-start(bf16[4,128,256]{2,1,0:T(8,128)(2,1)} %copy-done.16), calls=%async_computation.10 | async-start | bytes 131072 | tf_op jit(solution)/shard_map/slice | solution.py:307
  97.6 9.5 %copy-start.17 = (bf16[4,128,256]{2,1,0:T(8,128)(2,1)S(1)}, bf16[4,128,256]{2,1,0:T(8,128)(2,1)}, u32[]{:S(2)}) copy-start(bf16[4,128,256]{2,1,0:T(8,128)(2,1)} %copy-done.16) | copy-start | bytes 786436
  97.6 9.5 %slice-start.10 = ((bf16[4,128,256]{2,1,0:T(8,128)(2,1)}), bf16[3,128,256]{2,1,0:T(8,128)(2,1)S(1)}, s32[]{:S(2)}) async-start(bf16[4,128,256]{2,1,0:T(8,128)(2,1)} %copy-done.16), calls=%async_computation.11 | async-start | bytes 393216 | tf_op jit(solution)/shard_map/slice | solution.py:310
  99.8 7.3 %collective-permute-start.4 = (bf16[2,128,256]{2,1,0:T(8,128)(2,1)S(1)}, bf16[2,128,256]{2,1,0:T(8,128)(2,1)S(1)}, u32[]{:S(2)}, u32[]{:S(2)}) collective-permute-start(bf16[2,128,256]{2,1,0:T(8,128)(2,1)S(1)} %pad_maximum_fusion.17), channel_id=1, source_target_pairs={{0,1},{1,2},{2,3},{3,4},{4,5},{5,6},{6,7},{7,8},{8,9},{9,10},{10,1... | collective-permute-start | bytes 393224 | tf_op jit(solution)/shard_map/ppermute | solution.py:228
  113.5 1.9 slice-start.5
  115.4 8.6 %copy-start.6 = (bf16[8,128,512]{2,1,0:T(8,128)(2,1)S(1)}, bf16[8,128,512]{2,1,0:T(8,128)(2,1)}, u32[]{:S(2)}) copy-start(bf16[8,128,512]{2,1,0:T(8,128)(2,1)} %copy-done.5) | copy-start | bytes 3145732
  115.4 8.6 %slice-start.6 = ((bf16[8,128,512]{2,1,0:T(8,128)(2,1)}), bf16[7,128,512]{2,1,0:T(8,128)(2,1)S(1)}, s32[]{:S(2)}) async-start(bf16[8,128,512]{2,1,0:T(8,128)(2,1)} %copy-done.5), calls=%async_computation.7 | async-start | bytes 1835008 | tf_op jit(solution)/shard_map/slice | solution.py:310
  115.4 8.5 %collective-permute-start.5 = (bf16[2,128,512]{2,1,0:T(8,128)(2,1)S(1)}, bf16[2,128,512]{2,1,0:T(8,128)(2,1)S(1)}, u32[]{:S(2)}, u32[]{:S(2)}) collective-permute-start(bf16[2,128,512]{2,1,0:T(8,128)(2,1)S(1)} %pad_maximum_fusion.12), channel_id=1, source_target_pairs={{0,1},{1,2},{2,3},{3,4},{4,5},{5,6},{6,7},{7,8},{8,9},{9,10},{10,1... | collective-permute-start | bytes 786440 | tf_op jit(solution)/shard_map/ppermute | solution.py:228
  130.8 2.2 copy-start.31
  137.1 3.9 %collective-permute-start.6 = (bf16[2,128,512]{2,1,0:T(8,128)(2,1)S(1)}, bf16[2,128,512]{2,1,0:T(8,128)(2,1)S(1)}, u32[]{:S(2)}, u32[]{:S(2)}) collective-permute-start(bf16[2,128,512]{2,1,0:T(8,128)(2,1)S(1)} %slice.605), channel_id=1, source_target_pairs={{0,15},{1,0},{2,1},{3,2},{4,3},{5,4},{6,5},{7,6},{8,7},{9,8},{10,9... | collective-permute-start | bytes 786440 | tf_op jit(solution)/shard_map/ppermute | solution.py:228
  144.7 3.2 copy-start.13
  150.1 8.0 %collective-permute-start.7 = (bf16[2,128,256]{2,1,0:T(8,128)(2,1)S(1)}, bf16[2,128,256]{2,1,0:T(8,128)(2,1)S(1)}, u32[]{:S(2)}, u32[]{:S(2)}) collective-permute-start(bf16[2,128,256]{2,1,0:T(8,128)(2,1)S(1)} %slice.607), channel_id=1, source_target_pairs={{0,15},{1,0},{2,1},{3,2},{4,3},{5,4},{6,5},{7,6},{8,7},{9,8},{10,9... | collective-permute-start | bytes 393224 | tf_op jit(solution)/shard_map/ppermute | solution.py:228
  155.7 2.3 copy-start.3
  155.7 22.9 %slice-start.2 = ((s8[8388608]{0:T(1024)(128)(4,1)}), s8[4194304]{0:T(1024)(128)(4,1)S(1)}, s32[]{:S(2)}) async-start(s8[8388608]{0:T(1024)(128)(4,1)} %bitcast.275), calls=%async_computation.3 | async-start | bytes 8388608
  158.1 6.9 %copy-start.19 = (bf16[4,128,256]{2,1,0:T(8,128)(2,1)S(1)}, bf16[4,128,256]{2,1,0:T(8,128)(2,1)}, u32[]{:S(2)}) copy-start(bf16[4,128,256]{2,1,0:T(8,128)(2,1)} %copy-done.18) | copy-start | bytes 786436
  158.8 19.9 %slice-start.3 = ((s8[8388608]{0:T(1024)(128)(4,1)}), s8[4194304]{0:T(1024)(128)(4,1)S(1)}, s32[]{:S(2)}) async-start(s8[8388608]{0:T(1024)(128)(4,1)} %bitcast.275), calls=%async_computation.4 | async-start | bytes 8388608
  165.6 12.7 %copy-start.23 = (bf16[2,128,128]{1,2,0:T(8,128)(2,1)S(1)}, bf16[2,128,128]{1,2,0:T(8,128)(2,1)}, u32[]{:S(2)}) copy-start(bf16[2,128,128]{1,2,0:T(8,128)(2,1)} %copy-done.22) | copy-start | bytes 196612
  166.8 40.3 %copy-start.14 = (bf16[4,128,256]{2,1,0:T(8,128)(2,1)}, bf16[4,128,256]{2,1,0:T(8,128)(2,1)S(1)}, u32[]{:S(2)}) copy-start(bf16[4,128,256]{2,1,0:T(8,128)(2,1)S(1)} %convolution_convert_fusion.14) | copy-start | bytes 786436
  166.8 5.4 %collective-permute-start.8 = (bf16[2,128,128]{2,1,0:T(8,128)(2,1)S(1)}, bf16[2,128,128]{2,1,0:T(8,128)(2,1)S(1)}, u32[]{:S(2)}, u32[]{:S(2)}) collective-permute-start(bf16[2,128,128]{2,1,0:T(8,128)(2,1)S(1)} %slice.609), channel_id=1, source_target_pairs={{0,15},{1,0},{2,1},{3,2},{4,3},{5,4},{6,5},{7,6},{8,7},{9,8},{10,9... | collective-permute-start | bytes 196616 | tf_op jit(solution)/shard_map/ppermute | solution.py:228
  207.6 6.4 %collective-permute-start.9 = (bf16[2,128,128]{2,1,0:T(8,128)(2,1)S(1)}, bf16[2,128,128]{2,1,0:T(8,128)(2,1)S(1)}, u32[]{:S(2)}, u32[]{:S(2)}) collective-permute-start(bf16[2,128,128]{2,1,0:T(8,128)(2,1)S(1)} %pad_maximum_fusion.24), channel_id=1, source_target_pairs={{0,1},{1,2},{2,3},{3,4},{4,5},{5,6},{6,7},{7,8},{8,9},{9,10},{10,1... | collective-permute-start | bytes 196616 | tf_op jit(solution)/shard_map/ppermute | solution.py:228
  208.7 10.6 %copy-start.26 = (bf16[4,128,128]{1,2,0:T(8,128)(2,1)S(1)}, bf16[4,128,128]{1,2,0:T(8,128)(2,1)}, u32[]{:S(2)}) copy-start(bf16[4,128,128]{1,2,0:T(8,128)(2,1)} %fusion.35) | copy-start | bytes 393220
  213.3 7.2 %slice-start.7 = ((bf16[4,128,256]{2,1,0:T(8,128)(2,1)}), bf16[1,128,256]{2,1,0:T(8,128)(2,1)S(1)}, s32[]{:S(2)}) async-start(bf16[4,128,256]{2,1,0:T(8,128)(2,1)} %copy-done.14), calls=%async_computation.8 | async-start | bytes 131072 | tf_op jit(solution)/shard_map/slice | solution.py:307
  220.5 8.1 %collective-permute-start.10 = (bf16[2,128,256]{2,1,0:T(8,128)(2,1)S(1)}, bf16[2,128,256]{2,1,0:T(8,128)(2,1)S(1)}, u32[]{:S(2)}, u32[]{:S(2)}) collective-permute-start(bf16[2,128,256]{2,1,0:T(8,128)(2,1)S(1)} %pad_maximum_fusion.19), channel_id=1, source_target_pairs={{0,1},{1,2},{2,3},{3,4},{4,5},{5,6},{6,7},{7,8},{8,9},{9,10},{10,1... | collective-permute-start | bytes 393224 | tf_op jit(solution)/shard_map/ppermute | solution.py:228
  220.6 8.1 %copy-start.15 = (bf16[4,128,256]{2,1,0:T(8,128)(2,1)S(1)}, bf16[4,128,256]{2,1,0:T(8,128)(2,1)}, u32[]{:S(2)}) copy-start(bf16[4,128,256]{2,1,0:T(8,128)(2,1)} %copy-done.14) | copy-start | bytes 786436
  220.6 8.1 %slice-start.8 = ((bf16[4,128,256]{2,1,0:T(8,128)(2,1)}), bf16[3,128,256]{2,1,0:T(8,128)(2,1)S(1)}, s32[]{:S(2)}) async-start(bf16[4,128,256]{2,1,0:T(8,128)(2,1)} %copy-done.14), calls=%async_computation.9 | async-start | bytes 393216 | tf_op jit(solution)/shard_map/slice | solution.py:310
  235.0 3.1 slice-start.4
  237.1 66.1 %copy-start.30 = (f32[3,3]{1,0:T(4,128)S(1)}, f32[3,3]{1,0:T(4,128)}, u32[]{:S(2)}) copy-start(f32[3,3]{1,0:T(4,128)} %constant.56) | copy-start | bytes 112
  238.3 66.9 %collective-permute-start.11 = (bf16[2,128,512]{2,1,0:T(8,128)(2,1)S(1)}, bf16[2,128,512]{2,1,0:T(8,128)(2,1)S(1)}, u32[]{:S(2)}, u32[]{:S(2)}) collective-permute-start(bf16[2,128,512]{2,1,0:T(8,128)(2,1)S(1)} %pad_maximum_fusion.15), channel_id=1, source_target_pairs={{0,1},{1,2},{2,3},{3,4},{4,5},{5,6},{6,7},{7,8},{8,9},{9,10},{10,1... | collective-permute-start | bytes 786440 | tf_op jit(solution)/shard_map/ppermute | solution.py:228
  303.2 2.1 copy-start.4
  316.5 5.4 %copy-start.28 = (bf16[128,128]{1,0:T(8,128)(2,1)S(1)}, bf16[128,128]{1,0:T(8,128)(2,1)}, u32[]{:S(2)}) copy-start(bf16[128,128]{1,0:T(8,128)(2,1)} %param.19) | copy-start | bytes 98308
  (10 other events, 14.4 us)
Sparse Core Ops, SparseCore 0:
  208.8 92.7 all-reduce.2

commit v2 on v1

--- a/solution.py
+++ b/solution.py
@@ -86,12 +86,12 @@
     fetch = pltpu.make_async_copy(weight_hbm, weight, weight_sem)
     fetch.start()
     enter_together(size)
-    rows = coarse_ref.shape[0]
+    rows = coarse_ref.shape[1]
     total = None
     for row in range(rows):
         part = lax.dot_general(
             col_ref[row],
-            coarse_ref[row].astype(jnp.float32),
+            coarse_ref[0, row].astype(jnp.float32),
             NT,
             precision=HIGHEST,
             preferred_element_type=jnp.float32,
@@ -163,6 +163,7 @@
     same_row = jnp.eye(local_rows, dtype=jnp.float32)
     wave = jnp.stack([cos_col.T, -sin_col.T], axis=1).reshape(size, near_cols, 2, columns)
     col = jnp.einsum("hg,dmrw->gdhmrw", same_row, wave).reshape(local_rows, -1, columns)
+    col = jnp.pad(col, ((0, 0), (0, 0), (0, columns)))
     col_inv = col
     turn = jnp.stack(
         [jnp.stack([cos_row, sin_row], axis=-1), jnp.stack([-sin_row, cos_row], axis=-1)], axis=2
@@ -177,14 +178,14 @@
 def spectral_path(coarse, weight, tables, near_cols, back):
     col, row, row_inv, col_inv = tables
     size = lax.axis_size("row")
-    local_rows, channels, columns = coarse.shape
+    channels = coarse.shape[2]
     count_a, count_b = col.shape[1], row.shape[0]
     f32 = jnp.float32
     vmem = pl.BlockSpec(memory_space=pltpu.VMEM)
     image, spec = pl.pallas_call(
         functools.partial(spectral_kernel, size, near_cols, back),
         out_shape=(
-            jax.ShapeDtypeStruct(coarse.shape, jnp.bfloat16),
+            jax.ShapeDtypeStruct(coarse.shape[1:], jnp.bfloat16),
             jax.ShapeDtypeStruct((count_b, channels), f32),
         ),
         in_specs=[vmem] * 5 + [pl.BlockSpec(memory_space=pl.ANY)],
@@ -223,11 +224,6 @@
     return grid[0], grid[1]
 
 
-def shifted(shard, axis, by):
-    size = lax.axis_size(axis)
-    return lax.ppermute(shard, axis, [(i, (i + by) % size) for i in range(size)])
-
-
 def as_float(values):
     return values.astype(jnp.float32)
 
@@ -251,73 +247,6 @@
     turns = row_modes[:, None] * positions[None, :] % length
     angles = turns.astype(jnp.float32) * (2.0 * math.pi / length)
     return (jnp.cos(angles), jnp.sin(angles))
-
-
-def row_pass(values, row_filters):
-    incoming = shifted(values[:2], "row", -1)
-    spread = as_float(jnp.concatenate([values, incoming], axis=0))
-    row_count = values.shape[0]
-    outputs = []
-    for branch in range(2):
-        running = row_filters[branch, 0] * spread[0:row_count:2]
-        for offset in range(1, 4):
-            running = (
-                running + row_filters[branch, offset] * spread[offset : offset + row_count : 2]
-            )
-        outputs.append(running.astype(jnp.bfloat16))
-    return (outputs[0], outputs[1])
-
-
-def analysis(values, row_filters, matrices):
-    band_list = []
-    current = values
-    for matrix in matrices:
-        low_rows, high_rows = row_pass(current, row_filters)
-        low_cols = narrow("hcw,wv->hcv", low_rows, matrix).astype(jnp.bfloat16)
-        high_cols = narrow("hcw,wv->hcv", high_rows, matrix).astype(jnp.bfloat16)
-        halfway = low_cols.shape[2] // 2
-        current = low_cols[:, :, :halfway]
-        band_list.append(
-            (low_cols[:, :, halfway:], high_cols[:, :, :halfway], high_cols[:, :, halfway:])
-        )
-    return (current, band_list)
-
-
-def combine_rows(low_now, high_now, low_prev, high_prev, row_filters):
-    parities = []
-    for parity in range(2):
-        running = row_filters[0, parity] * low_now + row_filters[1, parity] * high_now
-        running = running + row_filters[0, parity + 2] * low_prev
-        running = running + row_filters[1, parity + 2] * high_prev
-        parities.append(running)
-    stacked = jnp.stack(parities, axis=1)
-    return stacked.reshape((2 * low_now.shape[0],) + low_now.shape[1:])
-
-
-def synthesis(top_array, band_list, row_filters, matrices):
-    current = top_array
-    for octave in (2, 1, 0):
-        band_one, band_two, band_three = band_list[octave]
-        low_sum = narrow(
-            "hcv,wv->hcw", jnp.concatenate([current, band_one], axis=2), matrices[octave]
-        ).astype(jnp.bfloat16)
-        high_sum = narrow(
-            "hcv,wv->hcw", jnp.concatenate([band_two, band_three], axis=2), matrices[octave]
-        ).astype(jnp.bfloat16)
-        edges = jnp.concatenate([low_sum[-1:], high_sum[-1:]], axis=0)
-        earlier = shifted(edges, "row", 1)
-        low_prev = jnp.concatenate([earlier[0:1], low_sum[:-1]], axis=0)
-        high_prev = jnp.concatenate([earlier[1:2], high_sum[:-1]], axis=0)
-        current = combine_rows(
-            as_float(low_sum),
-            as_float(high_sum),
-            as_float(low_prev),
-            as_float(high_prev),
-            row_filters,
-        )
-        if octave > 0:
-            current = current.astype(jnp.bfloat16)
-    return current
 
 
 def owned_modes(coarse, row_modes, col_modes):
@@ -389,6 +318,295 @@
     return (real_out, imag_out)
 
 
+def greet_ring(receives_from):
+    barrier = pltpu.get_barrier_semaphore()
+    pl.semaphore_signal(barrier, inc=1, device_id={"row": receives_from}, device_id_type=MESH)
+    pl.semaphore_wait(barrier, 1)
+
+
+def analysis_kernel(
+    size,
+    values,
+    taps,
+    filter_1,
+    filter_2,
+    filter_3,
+    out_1,
+    out_2,
+    out_3,
+    halo_1,
+    halo_2,
+    halo_3,
+    send_sem,
+    recv_sem,
+):
+    me = lax.axis_index("row")
+    above, below = lax.rem(me + size - 1, size), lax.rem(me + 1, size)
+    greet_ring(below)
+
+    def copy(level, source, halo):
+        return pltpu.make_async_remote_copy(
+            src_ref=source,
+            dst_ref=halo,
+            send_sem=send_sem.at[level],
+            recv_sem=recv_sem.at[level],
+            device_id={"row": above},
+            device_id_type=MESH,
+        )
+
+    def one(get, row, matrix, out):
+        loaded = [as_float(get(2 * row + offset)) for offset in range(4)]
+        halves = []
+        for branch in range(2):
+            running = taps[branch, 0] * loaded[0]
+            for offset in range(1, 4):
+                running = running + taps[branch, offset] * loaded[offset]
+            halves.append(running.astype(jnp.bfloat16))
+        both = jnp.concatenate(halves, axis=0)
+        done = jnp.dot(both, matrix[...], preferred_element_type=jnp.float32).astype(jnp.bfloat16)
+        count = halves[0].shape[0]
+        out[0, row] = done[:count]
+        out[1, row] = done[count:]
+
+    def span(get, first, last, matrix, out):
+        def body(row, carry):
+            one(get, row, matrix, out)
+            return carry
+
+        lax.fori_loop(first, last, body, 0)
+
+    def edged(get, halo, count):
+        return lambda row: get(row) if row < count else halo[row - count]
+
+    count = values.shape[0]
+    half_1, half_2 = filter_1.shape[0] // 2, filter_2.shape[0] // 2
+    get_1 = lambda row: values[row]
+    get_2 = lambda row: out_1[0, row, :, :half_1]
+    get_3 = lambda row: out_2[0, row, :, :half_2]
+    first = copy(0, values.at[pl.ds(0, 2)], halo_1)
+    first.start()
+    span(get_1, 0, 2, filter_1, out_1)
+    second = copy(1, out_1.at[0, pl.ds(0, 2), :, pl.ds(0, half_1)], halo_2)
+    second.start()
+    early = min(6, count // 2 - 1)
+    span(get_1, 2, early, filter_1, out_1)
+    span(get_2, 0, 2, filter_2, out_2)
+    third = copy(2, out_2.at[0, pl.ds(0, 2), :, pl.ds(0, half_2)], halo_3)
+    third.start()
+    span(get_1, early, count // 2 - 1, filter_1, out_1)
+    first.wait()
+    one(edged(get_1, halo_1, count), count // 2 - 1, filter_1, out_1)
+    span(get_2, 2, count // 4 - 1, filter_2, out_2)
+    second.wait()
+    one(edged(get_2, halo_2, count // 2), count // 4 - 1, filter_2, out_2)
+    span(get_3, 0, count // 8 - 1, filter_3, out_3)
+    third.wait()
+    one(edged(get_3, halo_3, count // 4), count // 8 - 1, filter_3, out_3)
+
+
+def analysis_call(values, row_filters, matrices, back):
+    size = lax.axis_size("row")
+    count, channels, columns = values.shape
+    vmem = pl.BlockSpec(memory_space=pltpu.VMEM)
+    widths = [columns >> level for level in range(3)]
+    return pl.pallas_call(
+        functools.partial(analysis_kernel, size),
+        out_shape=tuple(
+            jax.ShapeDtypeStruct((2, count >> level + 1, channels, widths[level]), jnp.bfloat16)
+            for level in range(3)
+        ),
+        in_specs=[vmem, pl.BlockSpec(memory_space=pltpu.SMEM), vmem, vmem, vmem],
+        out_specs=(vmem, vmem, vmem),
+        scratch_shapes=[
+            *(pltpu.VMEM((2, channels, width), jnp.bfloat16) for width in widths),
+            pltpu.SemaphoreType.DMA((3,)),
+            pltpu.SemaphoreType.DMA((3,)),
+        ],
+        compiler_params=pltpu.CompilerParams(
+            collective_id=3 if back else 2,
+            has_side_effects=True,
+            vmem_limit_bytes=40 * 1024 * 1024,
+        ),
+        name="analysis_back" if back else "analysis",
+    )(values, row_filters, *matrices)
+
+
+def gelu_slope(value):
+    scale = math.sqrt(2.0 / math.pi)
+    square = value * value
+    bend = jnp.tanh(scale * (value + 0.044715 * (square * value)))
+    return 0.5 * (1.0 + bend) + 0.5 * value * (1.0 - bend * bend) * (
+        scale * (1.0 + 3 * 0.044715 * square)
+    )
+
+
+def synthesis_kernel(
+    size,
+    back,
+    image,
+    out_1,
+    out_2,
+    out_3,
+    taps,
+    turned_1,
+    turned_2,
+    turned_3,
+    detail,
+    skip,
+    plain,
+    *rest,
+):
+    if back:
+        result, *rest = rest
+    else:
+        cotangent, result, *rest = rest
+    syn_1, syn_2, syn_3, halo_1, halo_2, halo_3, top_1, top_2, send_sem, recv_sem = rest
+    me = lax.axis_index("row")
+    above, below = lax.rem(me + size - 1, size), lax.rem(me + 1, size)
+    greet_ring(above)
+
+    def copy(level, syn, halo):
+        return pltpu.make_async_remote_copy(
+            src_ref=syn.at[:, syn.shape[1] - 1],
+            dst_ref=halo,
+            send_sem=send_sem.at[level],
+            recv_sem=recv_sem.at[level],
+            device_id={"row": below},
+            device_id_type=MESH,
+        )
+
+    def mixed(level, member, band):
+        return jnp.dot(detail[level, member], band, preferred_element_type=jnp.float32).astype(
+            jnp.bfloat16
+        )
+
+    def one(level, row, top, out, turned, syn):
+        half = out.shape[3] // 2
+        if half % 128 == 0:
+            low = [top[row], mixed(level, 0, out[0, row, :, half:])]
+            high = [mixed(level, 1, out[1, row, :, :half]), mixed(level, 2, out[1, row, :, half:])]
+            low, high = jnp.concatenate(low, axis=1), jnp.concatenate(high, axis=1)
+        else:
+            bands, lower = out[1, row], lax.broadcasted_iota(jnp.int32, out.shape[2:], 1) < half
+            low = jnp.where(lower, as_float(top[row]), as_float(mixed(level, 0, out[0, row])))
+            high = jnp.where(
+                lower, as_float(mixed(level, 1, bands)), as_float(mixed(level, 2, bands))
+            )
+            low, high = low.astype(jnp.bfloat16), high.astype(jnp.bfloat16)
+        both = jnp.concatenate([low, high], axis=0)
+        done = jnp.dot(both, turned[...], preferred_element_type=jnp.float32).astype(jnp.bfloat16)
+        count = low.shape[0]
+        syn[0, row] = done[:count]
+        syn[1, row] = done[count:]
+
+    def joined(syn, row, previous):
+        low_now, high_now = as_float(syn[0, row]), as_float(syn[1, row])
+        low_prev, high_prev = as_float(previous(0)), as_float(previous(1))
+        pair = []
+        for parity in range(2):
+            running = taps[0, parity] * low_now + taps[1, parity] * high_now
+            running = running + taps[0, parity + 2] * low_prev
+            pair.append(running + taps[1, parity + 2] * high_prev)
+        return pair
+
+    def combine(syn, row, halo, top):
+        previous = (lambda part: halo[part]) if halo is not None else lambda part: syn[part, row - 1]
+        pair = joined(syn, row, previous)
+        for parity in range(2):
+            top[2 * row + parity] = pair[parity].astype(jnp.bfloat16)
+
+    def last(row, halo):
+        previous = (
+            (lambda part: halo[part]) if halo is not None else lambda part: syn_1[part, row - 1]
+        )
+        pair = joined(syn_1, row, previous)
+        for parity in range(2):
+            here = 2 * row + parity
+            value = pair[parity] + jnp.dot(
+                skip[...], plain[here], preferred_element_type=jnp.float32
+            )
+            if not back:
+                value = (as_float(cotangent[here]) * gelu_slope(value)).astype(jnp.bfloat16)
+            result[here] = value
+
+    def span(first, stop, call):
+        def body(row, carry):
+            call(row)
+            return carry
+
+        lax.fori_loop(first, stop, body, 0)
+
+    level_3 = lambda row: one(2, row, image, out_3, turned_3, syn_3)
+    level_2 = lambda row: one(1, row, top_2, out_2, turned_2, syn_2)
+    level_1 = lambda row: one(0, row, top_1, out_1, turned_1, syn_1)
+    rows_3, rows_2, rows_1 = syn_3.shape[1], syn_2.shape[1], syn_1.shape[1]
+    level_3(rows_3 - 1)
+    third = copy(2, syn_3, halo_3)
+    third.start()
+    span(0, rows_3 - 1, level_3)
+    combine(syn_3, rows_3 - 1, None, top_2)
+    level_2(rows_2 - 1)
+    second = copy(1, syn_2, halo_2)
+    second.start()
+    level_2(rows_2 - 2)
+    combine(syn_2, rows_2 - 1, None, top_1)
+    level_1(rows_1 - 1)
+    first = copy(0, syn_1, halo_1)
+    first.start()
+    level_1(rows_1 - 2)
+    last(rows_1 - 1, None)
+    span(1, rows_3 - 1, lambda row: combine(syn_3, row, None, top_2))
+    third.wait()
+    combine(syn_3, 0, halo_3, top_2)
+    span(0, rows_2 - 2, level_2)
+    span(1, rows_2 - 1, lambda row: combine(syn_2, row, None, top_1))
+    span(2, rows_1 - 2, level_1)
+    span(3, rows_1 - 1, lambda row: last(row, None))
+    second.wait()
+    combine(syn_2, 0, halo_2, top_1)
+    span(0, 2, level_1)
+    span(1, 3, lambda row: last(row, None))
+    first.wait()
+    last(0, halo_1)
+
+
+def synthesis_call(image, bands, row_filters, turned, detail, skip, plain, cotangent):
+    back = cotangent is None
+    size = lax.axis_size("row")
+    vmem = pl.BlockSpec(memory_space=pltpu.VMEM)
+    smem = pl.BlockSpec(memory_space=pltpu.SMEM)
+    channels = plain.shape[1]
+    extra = [] if back else [cotangent]
+    return pl.pallas_call(
+        functools.partial(synthesis_kernel, size, back),
+        out_shape=jax.ShapeDtypeStruct(plain.shape, jnp.float32 if back else jnp.bfloat16),
+        in_specs=[vmem] * 4 + [smem] + [vmem] * (6 + len(extra)),
+        out_specs=vmem,
+        scratch_shapes=[
+            *(pltpu.VMEM(band.shape, jnp.bfloat16) for band in bands),
+            *(pltpu.VMEM((2, channels, band.shape[3]), jnp.bfloat16) for band in bands),
+            pltpu.VMEM((plain.shape[0] // 2, channels, bands[0].shape[3] // 2), jnp.bfloat16),
+            pltpu.VMEM((plain.shape[0] // 4, channels, bands[1].shape[3] // 2), jnp.bfloat16),
+            pltpu.SemaphoreType.DMA((3,)),
+            pltpu.SemaphoreType.DMA((3,)),
+        ],
+        compiler_params=pltpu.CompilerParams(
+            collective_id=5 if back else 4,
+            has_side_effects=True,
+            vmem_limit_bytes=48 * 1024 * 1024,
+        ),
+        name="synthesis_back" if back else "synthesis",
+    )(image, *bands, row_filters, *turned, detail, skip, plain, *extra)
+
+
+def split_bands(full):
+    band_list = []
+    for both in full:
+        half = both.shape[3] // 2
+        band_list.append((both[0, :, :, half:], both[1, :, :, :half], both[1, :, :, half:]))
+    return full[2][0, :, :, : full[2].shape[3] // 2], band_list
+
+
 def per_device(
     field,
     cotangent,
@@ -404,7 +622,9 @@
 ):
     matrices = (col_filter_1, col_filter_2, col_filter_3)
     devices = lax.axis_size("row")
-    coarse_field, bands_field = analysis(field, row_filters, matrices)
+    full_field = analysis_call(field, row_filters, matrices, False)
+    coarse_field, bands_field = split_bands(full_field)
+    turned = tuple(matrix.T for matrix in matrices)
     local_rows, channels, columns = coarse_field.shape
     height = local_rows * devices
     factor = 1.0 / (height * columns)
@@ -420,29 +640,28 @@
     if whole_tiles:
         near_cols = mode_cols // devices
         tables = spectral_tables(row_modes, col_modes, local_rows, columns, devices)
-        coarse_image, spec = spectral_path(coarse_field, spectral_weight, tables, near_cols, False)
+        coarse_image, spec = spectral_path(full_field[2], spectral_weight, tables, near_cols, False)
         spec_real, spec_imag = spec_parts(spec, mode_rows, mode_cols, devices)
     else:
         spec_real, spec_imag = owned_modes(coarse_field, row_modes, col_modes)
         out_real, out_imag = mix_modes(spec_real, spec_imag, weight_real, weight_imag, factor)
         coarse_image = owned_image(out_real, out_imag, row_modes, col_modes, local_rows, columns)
-    mixed_field = [
-        tuple(
-            (
-                narrow(
-                    "hcw,co->how", bands_field[octave][member], detail_weight[octave, member]
-                ).astype(jnp.bfloat16)
-                for member in range(3)
-            )
-        )
-        for octave in range(3)
-    ]
-    rebuilt_field = synthesis(coarse_image, mixed_field, row_filters, matrices)
-    activation_in = rebuilt_field + narrow("hcw,co->how", field, skip_weight)
-    upstream = jax.vjp(jax.nn.gelu, activation_in)[1](as_float(cotangent))[0].astype(jnp.bfloat16)
-    coarse_slope, bands_slope = analysis(upstream, row_filters, matrices)
+        coarse_image = jnp.pad(coarse_image, ((0, 0), (0, 0), (0, columns)))
+    detail_turned = jnp.swapaxes(detail_weight, 2, 3)
+    upstream = synthesis_call(
+        coarse_image,
+        full_field,
+        row_filters,
+        turned,
+        detail_turned,
+        skip_weight.T,
+        field,
+        cotangent,
+    )
+    full_slope = analysis_call(upstream, row_filters, matrices, True)
+    coarse_slope, bands_slope = split_bands(full_slope)
     if whole_tiles:
-        image_back, spec = spectral_path(coarse_slope, spectral_weight, tables, near_cols, True)
+        image_back, spec = spectral_path(full_slope[2], spectral_weight, tables, near_cols, True)
         back_real, back_imag = spec_parts(spec, mode_rows, mode_cols, devices)
     else:
         back_real, back_imag = owned_modes(coarse_slope, row_modes, col_modes)
@@ -452,19 +671,10 @@
         image_back = owned_image(
             turned_real, turned_imag, row_modes, col_modes, local_rows, columns
         )
-    back_bands = [
-        tuple(
-            (
-                narrow(
-                    "how,co->hcw", bands_slope[octave][member], detail_weight[octave, member]
-                ).astype(jnp.bfloat16)
-                for member in range(3)
-            )
-        )
-        for octave in range(3)
-    ]
-    rebuilt_slope = synthesis(image_back, back_bands, row_filters, matrices)
-    grad_field = rebuilt_slope + narrow("how,co->hcw", upstream, skip_weight)
+        image_back = jnp.pad(image_back, ((0, 0), (0, 0), (0, columns)))
+    grad_field = synthesis_call(
+        image_back, full_slope, row_filters, turned, detail_weight, skip_weight, upstream, None
+    )
     skip_local = narrow("hcw,how->co", field, upstream)
     detail_local = jnp.stack(
         [

time: 340 us -> 219 us (0.64)
  matrix products: 63.1 us -> 3.44 us
  Pallas kernels: 55.7 us -> 107 us
  waiting for transfers between devices: 91.2 us -> 43 us
  other arithmetic: 58.6 us -> 18.1 us
  starting transfers between devices: 20.2 us -> 0.04 us
    dot_general x54 -> x10, matrix products: 63.1 us -> 3.44 us  [narrow(): jnp.einsum(form, first_in, second_in, preferred_element_type=jnp.float32)]
    pallas_call x0 -> x4, Pallas kernels: none -> 50.4 us  [the longest x2 31.4 us: synthesis_call(): pl.pallas_call(functools.partial(synthesis_kernel, size, back), out_shape...]
    another operation x13 -> x1, other arithmetic: 35.9 us -> 0.01 us  [the longest x12 35.9 us: combine_rows(): stacked = jnp.stack(parities, axis=1)]
    ppermute x12 -> x0, waiting for transfers between devices: 28.2 us -> none  [shifted(): lax.ppermute(shard, axis, [(i, (i + by) % size) for i in range(size)])]
    ppermute x12 -> x0, starting transfers between devices: 20.1 us -> none  [shifted(): lax.ppermute(shard, axis, [(i, (i + by) % size) for i in range(size)])]
    psum x1, waiting for transfers between devices: 63.1 us -> 43 us  [per_device(): skip_total, detail_total = lax.psum((skip_local, detail_local), 'row')]
    unnamed x78 -> x65, local copies, waits for them, and re-layouts: 9.53 us -> 21.8 us
    reshape x1 -> x0, local copies, waits for them, and re-layouts: 5.35 us -> none  [combine_rows(): return stacked.reshape((2 * low_now.shape[0],) + low_now.shape[1:])]
  transfers between devices with their start and end apart: 13 -> 1, of which waited for: 9 -> 1; matrix products, arithmetic and copies ran while one was open for 16% -> 3% of each run, Pallas kernels for 0% -> 20%
where the time goes in v2:
time: 219 us; the launch traced here: 218 us
  Pallas kernels  107 us (49%)
  waiting for transfers between devices  43 us (20%)
  local copies, waits for them, and re-layouts  31.9 us (15%)
  other arithmetic  18.1 us (8%)
  between operations  14.6 us (7%)
  matrix products  3.44 us (2%)
    pallas_call x2, Pallas kernels, spectral_path(): pl.pallas_call(functools.partial(spectral_kernel, size, near_cols, back),...  56.4 us
    psum x1, waiting for transfers between devices, per_device(): skip_total, detail_total = lax.psum((skip_local, detail_local), 'row')  43 us
    pallas_call x2, Pallas kernels, synthesis_call(): pl.pallas_call(functools.partial(synthesis_kernel, size, back), out_shape...  31.4 us
    unnamed x65, local copies, waits for them, and re-layouts  21.8 us
    pallas_call x2, Pallas kernels, analysis_call(): pl.pallas_call(functools.partial(analysis_kernel, size), out_shape=tuple(...  19 us
    reshape x2, local copies, waits for them, and re-layouts, spectral_tables(): row = row.reshape(mode_rows * near_cols * 2, height * near_cols * 2)  7.09 us
    transpose x1, other arithmetic, spectral_tables(): row = jnp.einsum('phrs,mn->pmrhns', turn, same_col)  5.6 us
    another operation x1, other arithmetic, per_device(): grad_spectral = jnp.stack([grad_real, grad_imag])  4.51 us
  transfers between devices with their start and end apart: 1, of which 1 were waited for; matrix products, arithmetic and copies ran while one was open for 3% of the time, Pallas kernels for 20%

profile of v2, /device:TPU:0, one launch (start us, length us, event | category | flops | bytes accessed | tf_op | source)
XLA Modules:
  0.0 218.0 jit_solution(5101124867113511709)
XLA Ops:
  7.2 0.0 all-reduce.4.cloned.1.call-start
  7.2 0.1 copy.50
  7.3 0.7 mul.209
  8.0 0.1 copy.48
  8.1 0.2 fusion.50
  8.3 0.6 copy.49
  8.9 1.5 copy.57
  10.4 1.5 copy.55
  11.9 0.8 fusion.48
  12.7 1.0 copy.54
  13.7 1.9 copy.56
  15.6 1.3 copy.53
  16.9 1.4 copy.51
  18.3 5.6 %multiply_bitcast_fusion = f32[32,2,2,32,2,2]{5,4,3,2,1,0:T(2,128)} fusion(f32[32,32,2,2]{3,1,2,0:T(8,128)} %copy.51, f32[2,2]{1,0:T(2,128)S(1)} %compare_convert_fusion), kind=kLoop, calls=%fused_computation.3 | loop fusion | flops 16384 | bytes 81936 | tf_op jit(solution)/shard_map/phrs,mn->pmrhns/transpose | solution.py:172
  23.9 7.0 %reshape.266.row_ref = f32[128,128]{1,0:T(8,128)S(1)} reshape(f32[32,2,2,32,2,2]{5,4,3,2,1,0:T(2,128)} %multiply_bitcast_fusion) | data formatting | bytes 131072 | tf_op jit(solution)/shard_map/reshape | solution.py:173
  31.0 0.1 copy.52
  31.1 0.9 broadcast_multiply_fusion.1
  32.0 0.7 copy-done.19
  32.8 12.2 %analysis.1 = (bf16[2,8,128,512]{3,2,1,0:T(8,128)(2,1)S(1)}, bf16[2,4,128,256]{3,2,1,0:T(8,128)(2,1)S(1)}, bf16[2,2,128,128]{3,2,1,0:T(8,128)(2,1)S(1)}) custom-call(bf16[16,128,512]{2,1,0:T(8,128)(2,1)S(1)} %copy-done.2, f32[2,4]{1,0:T(2,128)S(1)} %copy-done.27, bf16[512,512]{1,0:T(8,128)(2,1)S(1)} %copy-done.4, bf16[256,256]{1,0:T(8,128)(2,1)S(1)} %copy-done.9, ...), custom_call_target="tpu_custom_call" | custom-call | tf_op jit(solution)/shard_map/analysis/pallas_call | solution.py:412
  45.1 3.4 %copy-done = f32[2,64,128,128]{3,2,1,0:T(8,128)S(1)} copy-done((f32[2,64,128,128]{3,2,1,0:T(8,128)S(1)}, f32[2,64,128,128]{3,2,1,0:T(8,128)}, u32[]{:S(2)}) %copy-start) | copy-done | bytes 8388632
  48.4 0.8 copy-done.15
  49.3 27.4 %spectral.1 = (bf16[2,128,128]{2,1,0:T(8,128)(2,1)S(1)}, f32[128,128]{1,0:T(8,128)S(1)}) custom-call(bf16[2,2,128,128]{3,2,1,0:T(8,128)(2,1)S(1)} %get-tuple-element.14.coarse_ref.out_3, f32[2,128,128]{2,1,0:T(8,128)S(1)} %pad.4.col_ref.col_inv_ref, f32[128,128]{1,0:T(8,128)S(1)} %copy-done.15, f32[128,128]{1,0:T(8,128)S(1)} %multiply_bitcast_fusion.1.row_inv_ref, ...), custom_call_target="tpu_custom_call" | custom-call | flops 16777216 | bytes 8388608 | tf_op jit(solution)/shard_map/spectral/pallas_call | solution.py:185
  76.8 16.8 %synthesis.1.values.plain = bf16[16,128,512]{2,1,0:T(8,128)(2,1)S(1)} custom-call(bf16[2,128,128]{2,1,0:T(8,128)(2,1)S(1)} %get-tuple-element.15.image, bf16[2,8,128,512]{3,2,1,0:T(8,128)(2,1)S(1)} %get-tuple-element.16.out_1, bf16[2,4,128,256]{3,2,1,0:T(8,128)(2,1)S(1)} %get-tuple-element.17.out_2, ...), custom_call_target="tpu_custom_call" | custom-call | tf_op jit(solution)/shard_map/synthesis/pallas_call | solution.py:580
  93.7 1.4 convolution_bitcast_fusion
  95.0 6.8 %analysis_back.1 = (bf16[2,8,128,512]{3,2,1,0:T(8,128)(2,1)S(1)}, bf16[2,4,128,256]{3,2,1,0:T(8,128)(2,1)S(1)}, bf16[2,2,128,128]{3,2,1,0:T(8,128)(2,1)S(1)}) custom-call(bf16[16,128,512]{2,1,0:T(8,128)(2,1)S(1)} %synthesis.1.values.plain, f32[2,4]{1,0:T(2,128)S(1)} %copy-done.27, bf16[512,512]{1,0:T(8,128)(2,1)S(1)} %copy-done.4, ...), custom_call_target="tpu_custom_call" | custom-call | tf_op jit(solution)/shard_map/analysis_back/pallas_call | solution.py:412
  101.9 0.3 convolution_bitcast_fusion.7
  102.2 0.3 convolution_bitcast_fusion.8
  102.5 0.7 copy-done.5
  103.1 0.3 convolution_bitcast_fusion.9
  103.4 0.2 convolution_bitcast_fusion.4
  103.6 0.2 convolution_bitcast_fusion.5
  103.8 0.2 convolution_bitcast_fusion.6
  104.0 0.2 convolution_bitcast_fusion.1
  104.3 0.2 convolution_bitcast_fusion.2
  104.4 0.2 convolution_bitcast_fusion.3
  104.7 0.0 copy-done.7
  104.8 0.9 pad_maximum_fusion.1
  105.6 0.0 all-reduce.4.cloned.1.call-update
  105.7 3.4 %copy-done.1 = f32[2,64,128,128]{3,2,1,0:T(8,128)S(1)} copy-done((f32[2,64,128,128]{3,2,1,0:T(8,128)S(1)}, f32[2,64,128,128]{3,2,1,0:T(8,128)}, u32[]{:S(2)}) %copy-start.1) | copy-done | bytes 8388632
  109.0 29.0 %spectral_back.1 = (bf16[2,128,128]{2,1,0:T(8,128)(2,1)S(1)}, f32[128,128]{1,0:T(8,128)S(1)}) custom-call(bf16[2,2,128,128]{3,2,1,0:T(8,128)(2,1)S(1)} %get-tuple-element.18.coarse_ref.out_3, f32[2,128,128]{2,1,0:T(8,128)S(1)} %pad.4.col_ref.col_inv_ref, f32[128,128]{1,0:T(8,128)S(1)} %copy-done.16, f32[128,128]{1,0:T(8,128)S(1)} %copy-done.18, ...), custom_call_target="tpu_custom_call" | custom-call | flops 16777216 | bytes 8388608 | tf_op jit(solution)/shard_map/spectral_back/pallas_call | solution.py:185
  138.2 2.4 %add_multiply_fusion = (f32[1,64,128,128]{3,2,1,0:T(8,128)S(1)}, f32[1,64,128,128]{3,2,1,0:T(8,128)S(1)}) fusion(f32[64,128]{1,0:T(8,128)S(1)} %bitcast.137, f32[64,128]{1,0:T(8,128)S(1)} %bitcast.135, f32[64,128]{1,0:T(8,128)S(1)} %bitcast.136, f32[64,128]{1,0:T(8,128)S(1)} %bitcast.134), kind=kLoop, calls=%fused_computation.2 | loop fusion | flops 8388608 | bytes 8519680 | tf_op jit(solution)/shard_map/mul | solution.py:705
  140.7 14.5 %synthesis_back.1 = f32[16,128,512]{2,1,0:T(8,128)} custom-call(bf16[2,128,128]{2,1,0:T(8,128)(2,1)S(1)} %get-tuple-element.19.image, bf16[2,8,128,512]{3,2,1,0:T(8,128)(2,1)S(1)} %copy-done.6, bf16[2,4,128,256]{3,2,1,0:T(8,128)(2,1)S(1)} %copy-done.8, bf16[2,2,128,128]{3,2,1,0:T(8,128)(2,1)S(1)} %get-tuple-element.18.coarse_ref.out_3, ...), custom_call_target="tpu_custom_call" | custom-call | tf_op jit(solution)/shard_map/synthesis_back/pallas_call | solution.py:580
  155.2 4.5 %pad_maximum_fusion = f32[2,64,128,128]{3,2,1,0:T(8,128)} fusion(f32[1,64,128,128]{3,2,1,0:T(8,128)S(1)} %get-tuple-element.39, f32[1,64,128,128]{3,2,1,0:T(8,128)S(1)} %get-tuple-element.38), kind=kLoop, calls=%fused_computation | loop fusion | flops 2097152 | bytes 16777216 | tf_op jit(solution)/shard_map/stack | solution.py:713
  159.7 43.0 %all-reduce.4.cloned.1.call-done = (f32[3,3,128,128]{3,2,1,0:T(8,128)}, f32[128,128]{0,1:T(8,128)}) async-done(((f32[3,3,128,128]{3,2,1,0:T(8,128)}, f32[128,128]{0,1:T(8,128)}), (f32[3,3,128,128]{3,2,1,0:T(8,128)}, f32[128,128]{0,1:T(8,128)})) %all-reduce.4.cloned.1.call-update) | async-done | bytes 655376 | tf_op jit(solution)/shard_map/psum | solution.py:690
  202.8 0.8 broadcast_multiply_fusion.2
  203.6 0.7 copy.66
  204.3 2.0 broadcast_multiply_fusion
  206.3 4.8 %copy.80 = f32[16,128,512]{2,1,0:T(8,128)} copy(f32[16,128,512]{2,1,0:T(8,128)} %synthesis_back.1) | data formatting | bytes 8388608
  (64 shorter events, 0.3 us)
Async XLA Ops:
  7.2 195.6 %all-reduce.4.cloned.1.call-start = ((), (), s32[]{:S(2)}) async-start(), calls=%async_computation | async-start | bytes 1310720 | tf_op jit(solution)/shard_map/psum | solution.py:690
  13.7 63.0 %copy-start.12 = (bf16[256,256]{0,1:T(8,128)(2,1)}, bf16[256,256]{0,1:T(8,128)(2,1)S(1)}, u32[]{:S(2)}) copy-start(bf16[256,256]{0,1:T(8,128)(2,1)S(1)} %copy.54) | copy-start | bytes 393220
  18.3 13.7 %copy-start.2 = (bf16[16,128,512]{2,1,0:T(8,128)(2,1)S(1)}, bf16[16,128,512]{2,1,0:T(8,128)(2,1)}, u32[]{:S(2)}) copy-start(bf16[16,128,512]{2,1,0:T(8,128)(2,1)} %plain.1) | copy-start | bytes 6291460
  18.3 13.7 %copy-start.4 = (bf16[512,512]{1,0:T(8,128)(2,1)S(1)}, bf16[512,512]{1,0:T(8,128)(2,1)}, u32[]{:S(2)}) copy-start(bf16[512,512]{1,0:T(8,128)(2,1)} %filter_1.3) | copy-start | bytes 1572868
  18.3 13.7 %copy-start.9 = (bf16[256,256]{1,0:T(8,128)(2,1)S(1)}, bf16[256,256]{1,0:T(8,128)(2,1)}, u32[]{:S(2)}) copy-start(bf16[256,256]{1,0:T(8,128)(2,1)} %filter_2.3) | copy-start | bytes 393220
  18.3 13.7 %copy-start.27 = (f32[2,4]{1,0:T(2,128)S(1)}, f32[2,4]{1,0:T(2,128)}, u32[]{:S(2)}) copy-start(f32[2,4]{1,0:T(2,128)} %taps.7) | copy-start | bytes 100
  30.9 1.0 copy-start.14
  31.1 45.6 %copy-start.17 = (f32[128,128]{1,0:T(8,128)}, f32[128,128]{1,0:T(8,128)S(1)}, u32[]{:S(2)}) copy-start(f32[128,128]{1,0:T(8,128)S(1)} %multiply_bitcast_fusion.1.row_inv_ref) | copy-start | bytes 196612
  32.0 0.8 copy-start.19
  45.0 3.4 %copy-start = (f32[2,64,128,128]{3,2,1,0:T(8,128)S(1)}, f32[2,64,128,128]{3,2,1,0:T(8,128)}, u32[]{:S(2)}) copy-start(f32[2,64,128,128]{3,2,1,0:T(8,128)} %weight_hbm.3) | copy-start | bytes 25165828
  48.4 0.8 copy-start.15
  49.3 27.5 %copy-start.11 = (bf16[3,3,128,128]{2,3,1,0:T(8,128)(2,1)S(1)}, bf16[3,3,128,128]{2,3,1,0:T(8,128)(2,1)}, u32[]{:S(2)}) copy-start(bf16[3,3,128,128]{2,3,1,0:T(8,128)(2,1)} %copy.56) | copy-start | bytes 884740
  49.3 27.5 %copy-start.21 = (bf16[128,128]{0,1:T(8,128)(2,1)S(1)}, bf16[128,128]{0,1:T(8,128)(2,1)}, u32[]{:S(2)}) copy-start(bf16[128,128]{0,1:T(8,128)(2,1)} %copy.55) | copy-start | bytes 98308
  49.3 27.5 %copy-start.24 = (bf16[128,128]{0,1:T(8,128)(2,1)S(1)}, bf16[128,128]{0,1:T(8,128)(2,1)}, u32[]{:S(2)}) copy-start(bf16[128,128]{0,1:T(8,128)(2,1)} %copy.57) | copy-start | bytes 98308
  76.7 16.9 %copy-start.25 = (f32[128,128]{1,0:T(8,128)}, f32[128,128]{1,0:T(8,128)S(1)}, u32[]{:S(2)}) copy-start(f32[128,128]{1,0:T(8,128)S(1)} %get-tuple-element.22) | copy-start | bytes 196612
  76.8 16.9 %copy-start.3 = (bf16[16,128,512]{2,1,0:T(8,128)(2,1)S(1)}, bf16[16,128,512]{2,1,0:T(8,128)(2,1)}, u32[]{:S(2)}) copy-start(bf16[16,128,512]{2,1,0:T(8,128)(2,1)} %plain.1) | copy-start | bytes 6291460
  93.6 1.4 copy-start.20
  101.8 1.3 copy-start.5
  101.8 2.8 %copy-start.7 = (bf16[2,4,128,256]{3,2,1,0:T(8,128)(2,1)}, bf16[2,4,128,256]{3,2,1,0:T(8,128)(2,1)S(1)}, u32[]{:S(2)}) copy-start(bf16[2,4,128,256]{3,2,1,0:T(8,128)(2,1)S(1)} %get-tuple-element.21.out_2) | copy-start | bytes 1572868
  101.8 3.8 %copy-start.16 = (f32[128,128]{1,0:T(8,128)S(1)}, f32[128,128]{1,0:T(8,128)}, u32[]{:S(2)}) copy-start(f32[128,128]{1,0:T(8,128)} %copy-done.14) | copy-start | bytes 196612
  101.9 3.8 %copy-start.18 = (f32[128,128]{1,0:T(8,128)S(1)}, f32[128,128]{1,0:T(8,128)}, u32[]{:S(2)}) copy-start(f32[128,128]{1,0:T(8,128)} %copy-done.17) | copy-start | bytes 196612
  105.7 3.4 %copy-start.1 = (f32[2,64,128,128]{3,2,1,0:T(8,128)S(1)}, f32[2,64,128,128]{3,2,1,0:T(8,128)}, u32[]{:S(2)}) copy-start(f32[2,64,128,128]{3,2,1,0:T(8,128)} %weight_hbm.3) | copy-start | bytes 25165828
  109.0 29.0 %copy-start.26 = (f32[128,128]{1,0:T(8,128)S(1)}, f32[128,128]{1,0:T(8,128)}, u32[]{:S(2)}) copy-start(f32[128,128]{1,0:T(8,128)} %copy-done.25) | copy-start | bytes 196612
  138.2 2.4 %copy-start.6 = (bf16[2,8,128,512]{3,2,1,0:T(8,128)(2,1)S(1)}, bf16[2,8,128,512]{3,2,1,0:T(8,128)(2,1)}, u32[]{:S(2)}) copy-start(bf16[2,8,128,512]{3,2,1,0:T(8,128)(2,1)} %copy-done.5) | copy-start | bytes 6291460
  138.2 2.4 %copy-start.8 = (bf16[2,4,128,256]{3,2,1,0:T(8,128)(2,1)S(1)}, bf16[2,4,128,256]{3,2,1,0:T(8,128)(2,1)}, u32[]{:S(2)}) copy-start(bf16[2,4,128,256]{3,2,1,0:T(8,128)(2,1)} %copy-done.7) | copy-start | bytes 1572868
  138.2 2.4 %copy-start.10 = (bf16[3,3,128,128]{3,2,1,0:T(8,128)(2,1)S(1)}, bf16[3,3,128,128]{3,2,1,0:T(8,128)(2,1)}, u32[]{:S(2)}) copy-start(bf16[3,3,128,128]{3,2,1,0:T(8,128)(2,1)} %detail.1) | copy-start | bytes 884740
  138.2 2.4 %copy-start.13 = (bf16[256,256]{0,1:T(8,128)(2,1)S(1)}, bf16[256,256]{0,1:T(8,128)(2,1)}, u32[]{:S(2)}) copy-start(bf16[256,256]{0,1:T(8,128)(2,1)} %copy-done.12) | copy-start | bytes 393220
  138.2 2.4 %copy-start.22 = (bf16[128,128]{0,1:T(8,128)(2,1)S(1)}, bf16[128,128]{0,1:T(8,128)(2,1)}, u32[]{:S(2)}) copy-start(bf16[128,128]{0,1:T(8,128)(2,1)} %copy.55) | copy-start | bytes 98308
  138.2 2.4 %copy-start.23 = (bf16[128,128]{1,0:T(8,128)(2,1)S(1)}, bf16[128,128]{1,0:T(8,128)(2,1)}, u32[]{:S(2)}) copy-start(bf16[128,128]{1,0:T(8,128)(2,1)} %skip.1) | copy-start | bytes 98308
  155.2 49.1 %copy-start.28 = (f32[3,3]{1,0:T(4,128)S(1)}, f32[3,3]{1,0:T(4,128)}, u32[]{:S(2)}) copy-start(f32[3,3]{1,0:T(4,128)} %constant.49) | copy-start | bytes 112
Sparse Core Ops, SparseCore 0:
  105.8 96.9 all-reduce.3

commit v3 on v2

--- a/solution.py
+++ b/solution.py
@@ -29,60 +29,109 @@
     pl.semaphore_wait(barrier, size - 1)
 
 
-def exchange(size, tile, send, land, send_sem, recv_sem):
+def tiles_copy(size, tile, send, land, send_sem, recv_sem, step):
     me = lax.axis_index("row")
-
-    def copy(step, partner, place):
-        return pltpu.make_async_remote_copy(
-            src_ref=send.at[pl.ds(pl.multiple_of(partner * tile, tile), tile)],
-            dst_ref=land.at[pl.ds(pl.multiple_of(place * tile, tile), tile)],
-            send_sem=send_sem.at[step],
-            recv_sem=recv_sem.at[step],
-            device_id={"row": partner},
-            device_id_type=MESH,
-        )
-
-    def start(step, carry):
-        copy(step, lax.rem(me + step, size), me).start()
-        return carry
-
-    def finish(step, carry):
-        source = lax.rem(me + size - step, size)
-        copy(step, source, source).wait_recv()
-        copy(step, lax.rem(me + step, size), me).wait_send()
-        return carry
-
-    lax.fori_loop(1, size, start, 0)
+    if step:
+        partner = lax.rem(me + step, size)
+        source = pl.ds(pl.multiple_of(partner * tile, tile), tile)
+        target = pl.ds(pl.multiple_of(me * tile, tile), tile)
+    else:
+        partner = lax.rem(me + 1, size)
+        source = target = pl.ds(0, (size - 1) * tile)
+    return pltpu.make_async_remote_copy(
+        src_ref=send.at[source],
+        dst_ref=land.at[target],
+        send_sem=send_sem,
+        recv_sem=recv_sem,
+        device_id={"row": partner},
+        device_id_type=MESH,
+    )
+
+
+def start_exchange(size, tile, send, land, send_sem, recv_sem):
+    me = lax.axis_index("row")
+    for step in range(1, size):
+        tiles_copy(size, tile, send, land, send_sem, recv_sem, step).start()
     own = pl.ds(pl.multiple_of(me * tile, tile), tile)
     land[own, :] = send[own, :]
-    lax.fori_loop(1, size, finish, 0)
+    return tiles_copy(size, tile, send, land, send_sem, recv_sem, 0)
+
+
+def channel_product(first, second):
+    return lax.dot_general(first, second, NT, preferred_element_type=jnp.float32)
+
+
+def local_sums(full_field, full_slope, field, upstream, sums, scales, skip_scale):
+    channels = field.shape[1]
+    for level in range(3):
+        left, right = full_field[level], full_slope[level]
+        half = left.shape[3] // 2
+        if half % 128 == 0:
+            halves = (slice(half, None), slice(0, half), slice(half, None))
+        else:
+            halves = (None, None, None)
+        for member, (branch, part) in enumerate(zip((0, 1, 1), halves)):
+
+            def body(row, total):
+                if part is not None:
+                    return total + channel_product(
+                        left[branch, row, :, part], right[branch, row, :, part]
+                    )
+                lane = lax.broadcasted_iota(jnp.int32, left.shape[2:], 1)
+                kept = (lane < half) if member == 1 else (lane >= half)
+                wide = jnp.where(kept, as_float(left[branch, row]), 0.0).astype(jnp.bfloat16)
+                return total + channel_product(wide, right[branch, row])
+
+            total = lax.fori_loop(
+                0, left.shape[1], body, jnp.zeros((channels, channels), jnp.float32)
+            )
+            start = (level * 3 + member) * channels
+            sums[start : start + channels, :] = (total * scales[level]).astype(jnp.bfloat16)
+    total = lax.fori_loop(
+        0,
+        field.shape[0],
+        lambda row, total: total + channel_product(field[row], upstream[row]),
+        jnp.zeros((channels, channels), jnp.float32),
+    )
+    sums[9 * channels : 10 * channels, :] = (total * skip_scale).astype(jnp.bfloat16)
+    if sums.shape[0] > 10 * channels:
+        sums[10 * channels :, :] = jnp.zeros(
+            (sums.shape[0] - 10 * channels, channels), jnp.bfloat16
+        )
 
 
 def spectral_kernel(
     size,
     near_cols,
     back,
+    scales,
     coarse_ref,
     col_ref,
     row_ref,
     row_inv_ref,
     col_inv_ref,
     weight_hbm,
-    image_ref,
-    spec_ref,
-    weight,
-    send_a,
-    land_a,
-    send_b,
-    send_c,
-    land_c,
-    send_d,
-    land_d,
-    rotated,
-    weight_sem,
-    send_sem,
-    recv_sem,
+    *rest,
 ):
+    if back:
+        full_field, full_slope = rest[:3], (*rest[3:5], coarse_ref)
+        field, upstream, image_ref, spec_ref, sums, *rest = rest[5:]
+    else:
+        image_ref, spec_ref, *rest = rest
+    (
+        weight,
+        send_a,
+        land_a,
+        send_b,
+        send_c,
+        land_c,
+        send_d,
+        land_d,
+        rotated,
+        weight_sem,
+        send_sem,
+        recv_sem,
+    ) = rest
     fetch = pltpu.make_async_copy(weight_hbm, weight, weight_sem)
     fetch.start()
     enter_together(size)
@@ -99,12 +148,16 @@
         total = part if total is None else total + part
     send_a[...] = total
     tile_a = send_a.shape[0] // size
-    exchange(size, tile_a, send_a, land_a, send_sem.at[0], recv_sem.at[0])
+    first = start_exchange(size, tile_a, send_a, land_a, send_sem.at[0], recv_sem.at[0])
+    if back:
+        local_sums(full_field, full_slope, field, upstream, sums, scales[:3], scales[3])
+    first.wait_recv()
     send_b[...] = lax.dot_general(
         row_ref[...], land_a[...], NN, precision=HIGHEST, preferred_element_type=jnp.float32
     )
     tile_b = send_b.shape[0] // size
-    exchange(size, tile_b, send_b, spec_ref, send_sem.at[1], recv_sem.at[1])
+    second = start_exchange(size, tile_b, send_b, spec_ref, send_sem.at[1], recv_sem.at[1])
+    second.wait_recv()
     spec = spec_ref[...]
     count = spec.shape[0]
     even = lax.broadcasted_iota(jnp.int32, spec.shape, 0) % 2 == 0
@@ -123,73 +176,90 @@
         turn = rotated[here, :].astype(jnp.bfloat16)
         pair = lax.broadcasted_iota(jnp.int32, (tile_b, plain.shape[1]), 0) // 2
         result = jnp.zeros((tile_b, plain.shape[1]), jnp.float32)
-        for member in range(per_tile):
-            mode = (member // per_row) * (modes // mode_rows) + source * per_row + member % per_row
-            one = lax.dot_general(
-                plain,
-                weight[0, mode].astype(jnp.bfloat16),
+        both = jnp.concatenate([plain, turn], axis=1)
+        channels = plain.shape[1]
+        for member in range(0, per_tile, 2):
+            blocks = []
+            for one in (member, member + 1):
+                mode = (one // per_row) * (modes // mode_rows) + source * per_row + one % per_row
+                blocks.append(
+                    jnp.concatenate(
+                        [weight[part, mode].astype(jnp.bfloat16) for part in range(2)],
+                        axis=1 if back else 0,
+                    )
+                )
+            done = lax.dot_general(
+                both,
+                jnp.concatenate(blocks, axis=0 if back else 1),
                 dims,
                 preferred_element_type=jnp.float32,
             )
-            two = lax.dot_general(
-                turn,
-                weight[1, mode].astype(jnp.bfloat16),
-                dims,
-                preferred_element_type=jnp.float32,
-            )
-            result = jnp.where(pair == member, one + two, result)
+            result = jnp.where(pair == member, done[:, :channels], result)
+            result = jnp.where(pair == member + 1, done[:, channels:], result)
         send_c[here, :] = result
         return carry
 
-    lax.fori_loop(0, size, mix, 0)
-    exchange(size, tile_b, send_c, land_c, send_sem.at[2], recv_sem.at[2])
+    lax.fori_loop(0, size, mix, 0, unroll=2)
+    third = start_exchange(size, tile_b, send_c, land_c, send_sem.at[2], recv_sem.at[2])
+    third.wait_recv()
     send_d[...] = lax.dot_general(
         row_inv_ref[...], land_c[...], NN, precision=HIGHEST, preferred_element_type=jnp.float32
     )
-    exchange(size, tile_a, send_d, land_d, send_sem.at[3], recv_sem.at[3])
+    fourth = start_exchange(size, tile_a, send_d, land_d, send_sem.at[3], recv_sem.at[3])
+    fourth.wait_recv()
     across = land_d[...].T
     for row in range(rows):
         image_ref[row] = lax.dot_general(
             across, col_inv_ref[row], NN, precision=HIGHEST, preferred_element_type=jnp.float32
         ).astype(jnp.bfloat16)
+    for sent in (first, second, third, fourth):
+        sent.wait_send()
 
 
 def spectral_tables(row_modes, col_modes, local_rows, columns, size):
     height = local_rows * size
     mode_rows, mode_cols = row_modes.shape[0], col_modes.shape[0]
     near_rows, near_cols = mode_rows // size, mode_cols // size
-    cos_col, sin_col = column_tables(col_modes, columns)
-    cos_row, sin_row = row_tables(row_modes, jnp.arange(height, dtype=jnp.int32), height)
-    same_row = jnp.eye(local_rows, dtype=jnp.float32)
-    wave = jnp.stack([cos_col.T, -sin_col.T], axis=1).reshape(size, near_cols, 2, columns)
-    col = jnp.einsum("hg,dmrw->gdhmrw", same_row, wave).reshape(local_rows, -1, columns)
-    col = jnp.pad(col, ((0, 0), (0, 0), (0, columns)))
+    count_a, count_b = height * near_cols * 2, mode_rows * near_cols * 2
+    where_a, where_b = jnp.arange(count_a), jnp.arange(count_b)
+    part_a, part_b = where_a % 2, where_b % 2
+    spot = where_a // 2
+    block = spot // (near_cols * local_rows)
+    col_of = col_modes[block * near_cols + spot % near_cols]
+    wide = jnp.arange(2 * columns)
+    turns = (col_of[:, None] * wide[None, :] + part_a[:, None] * (columns // 4)) % columns
+    col = jnp.cos(turns.astype(jnp.float32) * (2.0 * math.pi / columns))
+    same_row = (spot // near_cols % local_rows)[None, :] == jnp.arange(local_rows)[:, None]
+    inside = wide < columns
+    col = jnp.where(same_row[:, :, None] & inside[None, None, :], col[None], 0.0)
     col_inv = col
-    turn = jnp.stack(
-        [jnp.stack([cos_row, sin_row], axis=-1), jnp.stack([-sin_row, cos_row], axis=-1)], axis=2
-    )
-    same_col = jnp.eye(near_cols, dtype=jnp.float32)
-    row = jnp.einsum("phrs,mn->pmrhns", turn, same_col)
-    row = row.reshape(mode_rows * near_cols * 2, height * near_cols * 2)
+    row_of = row_modes[where_b // (2 * near_cols)]
+    quarter = (part_b[:, None] - part_a[None, :]) * (height // 4)
+    turns = (row_of[:, None] * (where_a // (2 * near_cols))[None, :] + quarter + height) % height
+    same_col = (where_b // 2 % near_cols)[:, None] == (where_a // 2 % near_cols)[None, :]
+    row = jnp.cos(turns.astype(jnp.float32) * (2.0 * math.pi / height))
+    row = jnp.where(same_col, row, 0.0)
     row_inv = row.T * (1.0 / (height * columns))
     return col, row, row_inv, col_inv
 
 
-def spectral_path(coarse, weight, tables, near_cols, back):
+def spectral_path(coarse, weight, tables, near_cols, extra, scales, sum_rows):
+    back = len(extra) > 0
     col, row, row_inv, col_inv = tables
     size = lax.axis_size("row")
     channels = coarse.shape[2]
     count_a, count_b = col.shape[1], row.shape[0]
     f32 = jnp.float32
     vmem = pl.BlockSpec(memory_space=pltpu.VMEM)
-    image, spec = pl.pallas_call(
-        functools.partial(spectral_kernel, size, near_cols, back),
+    return pl.pallas_call(
+        functools.partial(spectral_kernel, size, near_cols, back, scales),
         out_shape=(
             jax.ShapeDtypeStruct(coarse.shape[1:], jnp.bfloat16),
             jax.ShapeDtypeStruct((count_b, channels), f32),
+            *([jax.ShapeDtypeStruct((sum_rows, channels), jnp.bfloat16)] if back else []),
         ),
-        in_specs=[vmem] * 5 + [pl.BlockSpec(memory_space=pl.ANY)],
-        out_specs=(vmem, vmem),
+        in_specs=[vmem] * 5 + [pl.BlockSpec(memory_space=pl.ANY)] + [vmem] * len(extra),
+        out_specs=(vmem,) * (3 if back else 2),
         scratch_shapes=[
             pltpu.VMEM(weight.shape, f32),
             pltpu.VMEM((count_a, channels), f32),
@@ -201,8 +271,8 @@
             pltpu.VMEM((count_a, channels), f32),
             pltpu.VMEM((count_b, channels), f32),
             pltpu.SemaphoreType.DMA,
-            pltpu.SemaphoreType.DMA((4, size)),
-            pltpu.SemaphoreType.DMA((4, size)),
+            pltpu.SemaphoreType.DMA((4,)),
+            pltpu.SemaphoreType.DMA((4,)),
         ],
         compiler_params=pltpu.CompilerParams(
             collective_id=1 if back else 0,
@@ -213,8 +283,7 @@
             flops=8 * weight.size, bytes_accessed=4 * weight.size, transcendentals=0
         ),
         name="spectral_back" if back else "spectral",
-    )(coarse, col, row, row_inv, col_inv, weight)
-    return image, spec
+    )(coarse, col, row, row_inv, col_inv, weight, *extra)
 
 
 def spec_parts(spec, mode_rows, mode_cols, size):
@@ -457,13 +526,23 @@
     *rest,
 ):
     if back:
-        result, *rest = rest
+        sums, result, gathered, landed, total, send_more, recv_more, *rest = rest
     else:
-        cotangent, result, *rest = rest
+        cotangent, result, detail_turned, skip_turned, *rest = rest
+        for level in range(3):
+            for member in range(3):
+                detail_turned[level, member] = as_float(detail[level, member]).T.astype(
+                    jnp.bfloat16
+                )
+        skip_turned[...] = as_float(skip[...]).T.astype(jnp.bfloat16)
+        detail, skip = detail_turned, skip_turned
     syn_1, syn_2, syn_3, halo_1, halo_2, halo_3, top_1, top_2, send_sem, recv_sem = rest
     me = lax.axis_index("row")
     above, below = lax.rem(me + size - 1, size), lax.rem(me + 1, size)
-    greet_ring(above)
+    if back:
+        enter_together(size)
+    else:
+        greet_ring(above)
 
     def copy(level, syn, halo):
         return pltpu.make_async_remote_copy(
@@ -494,7 +573,9 @@
             )
             low, high = low.astype(jnp.bfloat16), high.astype(jnp.bfloat16)
         both = jnp.concatenate([low, high], axis=0)
-        done = jnp.dot(both, turned[...], preferred_element_type=jnp.float32).astype(jnp.bfloat16)
+        done = lax.dot_general(
+            both, turned[...], NT, preferred_element_type=jnp.float32
+        ).astype(jnp.bfloat16)
         count = low.shape[0]
         syn[0, row] = done[:count]
         syn[1, row] = done[count:]
@@ -543,6 +624,9 @@
     level_3(rows_3 - 1)
     third = copy(2, syn_3, halo_3)
     third.start()
+    if back:
+        chunk = sums.shape[0] // size
+        scatter = start_exchange(size, chunk, sums, landed, send_more.at[0], recv_more.at[0])
     span(0, rows_3 - 1, level_3)
     combine(syn_3, rows_3 - 1, None, top_2)
     level_2(rows_2 - 1)
@@ -561,6 +645,23 @@
     span(0, rows_2 - 2, level_2)
     span(1, rows_2 - 1, lambda row: combine(syn_2, row, None, top_1))
     span(2, rows_1 - 2, level_1)
+    if back:
+        scatter.wait_recv()
+        whole = as_float(landed[0:chunk, :])
+        for step in range(1, size):
+            whole = whole + as_float(landed[step * chunk : (step + 1) * chunk, :])
+        total[...] = whole.astype(jnp.bfloat16)
+        target = pl.ds(pl.multiple_of(me * chunk, chunk), chunk)
+        for step in range(1, size):
+            pltpu.make_async_remote_copy(
+                src_ref=total,
+                dst_ref=gathered.at[target],
+                send_sem=send_more.at[1],
+                recv_sem=recv_more.at[1],
+                device_id={"row": lax.rem(me + step, size)},
+                device_id_type=MESH,
+            ).start()
+        gathered[target, :] = total[...]
     span(3, rows_1 - 1, lambda row: last(row, None))
     second.wait()
     combine(syn_2, 0, halo_2, top_1)
@@ -568,21 +669,33 @@
     span(1, 3, lambda row: last(row, None))
     first.wait()
     last(0, halo_1)
-
-
-def synthesis_call(image, bands, row_filters, turned, detail, skip, plain, cotangent):
-    back = cotangent is None
+    if back:
+        scatter.wait_send()
+        tiles_copy(size, chunk, landed, gathered, send_more.at[1], recv_more.at[1], 0).wait()
+
+
+def synthesis_call(image, bands, row_filters, matrices, detail, skip, plain, extra, back):
     size = lax.axis_size("row")
     vmem = pl.BlockSpec(memory_space=pltpu.VMEM)
     smem = pl.BlockSpec(memory_space=pltpu.SMEM)
     channels = plain.shape[1]
-    extra = [] if back else [cotangent]
+    result = jax.ShapeDtypeStruct(plain.shape, jnp.float32 if back else jnp.bfloat16)
+    own = [pltpu.VMEM(detail.shape, jnp.bfloat16), pltpu.VMEM(skip.shape, jnp.bfloat16)]
+    if back:
+        result = (result, jax.ShapeDtypeStruct(extra.shape, jnp.bfloat16))
+        own = [
+            pltpu.VMEM(extra.shape, jnp.bfloat16),
+            pltpu.VMEM((extra.shape[0] // size, channels), jnp.bfloat16),
+            pltpu.SemaphoreType.DMA((2,)),
+            pltpu.SemaphoreType.DMA((2,)),
+        ]
     return pl.pallas_call(
         functools.partial(synthesis_kernel, size, back),
-        out_shape=jax.ShapeDtypeStruct(plain.shape, jnp.float32 if back else jnp.bfloat16),
-        in_specs=[vmem] * 4 + [smem] + [vmem] * (6 + len(extra)),
-        out_specs=vmem,
+        out_shape=result,
+        in_specs=[vmem] * 4 + [smem] + [vmem] * 7,
+        out_specs=(vmem, vmem) if back else vmem,
         scratch_shapes=[
+            *own,
             *(pltpu.VMEM(band.shape, jnp.bfloat16) for band in bands),
             *(pltpu.VMEM((2, channels, band.shape[3]), jnp.bfloat16) for band in bands),
             pltpu.VMEM((plain.shape[0] // 2, channels, bands[0].shape[3] // 2), jnp.bfloat16),
@@ -596,7 +709,7 @@
             vmem_limit_bytes=48 * 1024 * 1024,
         ),
         name="synthesis_back" if back else "synthesis",
-    )(image, *bands, row_filters, *turned, detail, skip, plain, *extra)
+    )(image, *bands, row_filters, *matrices, detail, skip, plain, extra)
 
 
 def split_bands(full):
@@ -624,7 +737,13 @@
     devices = lax.axis_size("row")
     full_field = analysis_call(field, row_filters, matrices, False)
     coarse_field, bands_field = split_bands(full_field)
-    turned = tuple(matrix.T for matrix in matrices)
+    total_rows, total_cols = field.shape[0] * devices, field.shape[2]
+    scales = [
+        1.0 / math.sqrt((total_rows >> octave + 1) * (total_cols >> octave + 1))
+        for octave in range(3)
+    ] + [1.0 / math.sqrt(total_rows * total_cols)]
+    sum_rows = 10 * field.shape[1]
+    sum_rows = -(-sum_rows // (16 * devices)) * 16 * devices
     local_rows, channels, columns = coarse_field.shape
     height = local_rows * devices
     factor = 1.0 / (height * columns)
@@ -640,28 +759,33 @@
     if whole_tiles:
         near_cols = mode_cols // devices
         tables = spectral_tables(row_modes, col_modes, local_rows, columns, devices)
-        coarse_image, spec = spectral_path(full_field[2], spectral_weight, tables, near_cols, False)
+        coarse_image, spec = spectral_path(
+            full_field[2], spectral_weight, tables, near_cols, (), scales, sum_rows
+        )
         spec_real, spec_imag = spec_parts(spec, mode_rows, mode_cols, devices)
     else:
         spec_real, spec_imag = owned_modes(coarse_field, row_modes, col_modes)
         out_real, out_imag = mix_modes(spec_real, spec_imag, weight_real, weight_imag, factor)
         coarse_image = owned_image(out_real, out_imag, row_modes, col_modes, local_rows, columns)
         coarse_image = jnp.pad(coarse_image, ((0, 0), (0, 0), (0, columns)))
-    detail_turned = jnp.swapaxes(detail_weight, 2, 3)
     upstream = synthesis_call(
         coarse_image,
         full_field,
         row_filters,
-        turned,
-        detail_turned,
-        skip_weight.T,
+        matrices,
+        detail_weight,
+        skip_weight,
         field,
         cotangent,
+        False,
     )
     full_slope = analysis_call(upstream, row_filters, matrices, True)
     coarse_slope, bands_slope = split_bands(full_slope)
     if whole_tiles:
-        image_back, spec = spectral_path(full_slope[2], spectral_weight, tables, near_cols, True)
+        extra = (*full_field, *full_slope[:2], field, upstream)
+        image_back, spec, sums = spectral_path(
+            full_slope[2], spectral_weight, tables, near_cols, extra, scales, sum_rows
+        )
         back_real, back_imag = spec_parts(spec, mode_rows, mode_cols, devices)
     else:
         back_real, back_imag = owned_modes(coarse_slope, row_modes, col_modes)
@@ -672,36 +796,28 @@
             turned_real, turned_imag, row_modes, col_modes, local_rows, columns
         )
         image_back = jnp.pad(image_back, ((0, 0), (0, 0), (0, columns)))
-    grad_field = synthesis_call(
-        image_back, full_slope, row_filters, turned, detail_weight, skip_weight, upstream, None
-    )
-    skip_local = narrow("hcw,how->co", field, upstream)
-    detail_local = jnp.stack(
-        [
-            jnp.stack(
-                [
-                    narrow("hcw,how->co", bands_field[octave][member], bands_slope[octave][member])
-                    for member in range(3)
-                ]
-            )
+        shares = [
+            narrow("hcw,how->co", bands_field[octave][member], bands_slope[octave][member])
+            * scales[octave]
             for octave in range(3)
-        ]
-    )
-    skip_total, detail_total = lax.psum((skip_local, detail_local), "row")
-    total_rows = field.shape[0] * devices
-    total_cols = field.shape[2]
-    grad_skip = skip_total / math.sqrt(total_rows * total_cols)
-    divisors = jnp.array(
-        [
-            [
-                math.sqrt((total_rows >> octave + 1) * (total_cols >> octave + 1))
-                for member in range(3)
-            ]
-            for octave in range(3)
-        ],
-        jnp.float32,
-    )
-    grad_detail = detail_total / divisors[:, :, None, None]
+            for member in range(3)
+        ] + [narrow("hcw,how->co", field, upstream) * scales[3]]
+        sums = jnp.concatenate(shares, axis=0).astype(jnp.bfloat16)
+        sums = jnp.pad(sums, ((0, sum_rows - sums.shape[0]), (0, 0)))
+    grad_field, gathered = synthesis_call(
+        image_back,
+        full_slope,
+        row_filters,
+        matrices,
+        detail_weight,
+        skip_weight,
+        upstream,
+        sums,
+        True,
+    )
+    gathered = as_float(gathered[: 10 * channels])
+    grad_detail = gathered[: 9 * channels].reshape(3, 3, channels, channels)
+    grad_skip = gathered[9 * channels :]
     grad_real = (
         spec_real[:, :, None] * back_real[:, None, :]
         + spec_imag[:, :, None] * back_imag[:, None, :]

time: 219 us -> 142 us (0.65)
  waiting for transfers between devices: 43 us -> 0 us
  local copies, waits for them, and re-layouts: 31.9 us -> 15.3 us
  between operations: 14.6 us -> 0.93 us
  Pallas kernels: 107 us -> 118 us
  other arithmetic: 18.1 us -> 7.62 us
  matrix products: 3.44 us -> 0 us
    psum x1 -> x0, waiting for transfers between devices: 43 us -> none  [per_device(): skip_total, detail_total = lax.psum((skip_local, detail_local), 'row')]
    pallas_call x2, Pallas kernels: 31.4 us -> 44.9 us  [synthesis_call(): pl.pallas_call(functools.partial(synthesis_kernel, size, back), out_shape...]
    unnamed x65 -> x31, local copies, waits for them, and re-layouts: 21.8 us -> 10.9 us
    reshape x2 -> x0, local copies, waits for them, and re-layouts: 7.09 us -> none  [spectral_tables(): row = row.reshape(mode_rows * near_cols * 2, height * near_cols * 2)]
    transpose x1 -> x0, other arithmetic: 5.6 us -> none  [spectral_tables(): row = jnp.einsum('phrs,mn->pmrhns', turn, same_col)]
    dot_general x10 -> x0, matrix products: 3.44 us -> none  [narrow(): jnp.einsum(form, first_in, second_in, preferred_element_type=jnp.float32)]
    div x2 -> x0, other arithmetic: 2.83 us -> none  [the longest x1 1.98 us: per_device(): grad_detail = detail_total / divisors[:, :, None, None]]
    gather x0 -> x2, local copies, waits for them, and re-layouts: none -> 2.81 us  [the longest x1 1.59 us: spectral_tables(): col_of = col_modes[block * near_cols + spot % near_cols]]
  transfers between devices with their start and end apart: 1 -> 0, of which waited for: 1 -> 0; matrix products, arithmetic and copies ran while one was open for 3% -> 0% of each run, Pallas kernels for 20% -> 0%
where the time goes in v3:
time: 142 us
  Pallas kernels  118 us (83%)
  local copies, waits for them, and re-layouts  15.3 us (11%)
  other arithmetic  7.62 us (5%)
    pallas_call x2, Pallas kernels, spectral_path(): pl.pallas_call(functools.partial(spectral_kernel, size, near_cols, back,...  53.9 us
    pallas_call x2, Pallas kernels, synthesis_call(): pl.pallas_call(functools.partial(synthesis_kernel, size, back), out_shape...  44.9 us
    pallas_call x2, Pallas kernels, analysis_call(): pl.pallas_call(functools.partial(analysis_kernel, size), out_shape=tuple(...  19.1 us
    unnamed x31, local copies, waits for them, and re-layouts  10.9 us
    another operation x1, other arithmetic, per_device(): grad_spectral = jnp.stack([grad_real, grad_imag])  4.16 us

profile of v3, /device:TPU:0, one launch (start us, length us, event | category | flops | bytes accessed | tf_op | source)
XLA Modules:
  0.0 141.7 jit_solution(15732127310620892676)
XLA Ops:
  0.6 0.0 copy-start
  0.8 0.5 copy-done
  1.3 1.2 gather_fusion.1
  2.5 1.6 %gather_fusion = s32[128]{0:T(128)S(1)} fusion(s32[32]{0:T(128)} %param.21, s32[1024]{0:T(1024)S(1)} %pad_clamp_fusion.1), kind=kCustom, calls=%fused_computation | custom fusion | bytes 1536 | tf_op jit(solution)/shard_map/gather | solution.py:228
  4.1 0.3 fusion.3
  4.5 0.1 and_select_fusion.col_ref.col_inv_ref
  4.6 0.6 fusion.14
  5.2 0.0 copy-start.3
  5.2 1.6 %copy-done.3 = bf16[16,128,512]{2,1,0:T(8,128)(2,1)S(1)} copy-done((bf16[16,128,512]{2,1,0:T(8,128)(2,1)S(1)}, bf16[16,128,512]{2,1,0:T(8,128)(2,1)}, u32[]{:S(2)}) %copy-start.3) | copy-done | bytes 2097176
  6.8 0.0 copy-start.5
  6.8 1.0 copy-done.5
  7.8 0.0 copy-start.7
  7.8 0.9 copy-done.7
  8.7 0.0 copy-start.10
  8.7 0.8 copy-done.10
  9.5 0.0 copy-start.12
  9.5 0.7 copy-done.12
  10.2 12.2 %analysis.1 = (bf16[2,8,128,512]{3,2,1,0:T(8,128)(2,1)S(1)}, bf16[2,4,128,256]{3,2,1,0:T(8,128)(2,1)S(1)}, bf16[2,2,128,128]{3,2,1,0:T(8,128)(2,1)S(1)}) custom-call(bf16[16,128,512]{2,1,0:T(8,128)(2,1)S(1)} %copy-done.3, f32[2,4]{1,0:T(2,128)S(1)} %copy-done.12, bf16[512,512]{1,0:T(8,128)(2,1)S(1)} %copy-done.5, bf16[256,256]{1,0:T(8,128)(2,1)S(1)} %copy-done.7, ...), custom_call_target="tpu_custom_call" | custom-call | tf_op jit(solution)/shard_map/analysis/pallas_call | solution.py:481
  22.4 0.0 copy-start.2
  22.4 3.4 %copy-done.2 = f32[2,64,128,128]{3,2,1,0:T(8,128)S(1)} copy-done((f32[2,64,128,128]{3,2,1,0:T(8,128)S(1)}, f32[2,64,128,128]{3,2,1,0:T(8,128)}, u32[]{:S(2)}) %copy-start.2) | copy-done | bytes 8388632
  25.8 0.0 copy-start.6
  25.8 0.0 copy-start.8
  25.8 0.0 copy-start.9
  25.8 0.0 copy-start.11
  25.8 0.0 copy-start.13
  25.8 24.7 %spectral.1 = (bf16[2,128,128]{2,1,0:T(8,128)(2,1)S(1)}, f32[128,128]{1,0:T(8,128)S(1)}) custom-call(bf16[2,2,128,128]{3,2,1,0:T(8,128)(2,1)S(1)} %get-tuple-element.17.coarse_ref.out_3.rest_2_, f32[2,128,128]{2,1,0:T(8,128)S(1)} %and_select_fusion.col_ref.col_inv_ref, f32[128,128]{1,0:T(8,128)S(1)} %get-tuple-element.37.row_ref, ...), custom_call_target="tpu_custom_call" | custom-call | flops 16777216 | bytes 8388608 | tf_op jit(solution)/shard_map/spectral/pallas_call | solution.py:254
  50.6 0.0 copy-done.6
  50.6 0.0 copy-done.8
  50.6 0.0 copy-done.9
  50.6 0.0 copy-done.11
  50.6 0.0 copy-done.13
  50.6 0.0 copy-start.4
  50.6 17.1 %synthesis.1.values.rest_6_.plain = bf16[16,128,512]{2,1,0:T(8,128)(2,1)S(1)} custom-call(bf16[2,128,128]{2,1,0:T(8,128)(2,1)S(1)} %get-tuple-element.18.image, bf16[2,8,128,512]{3,2,1,0:T(8,128)(2,1)S(1)} %get-tuple-element.19.out_1.rest_0_, bf16[2,4,128,256]{3,2,1,0:T(8,128)(2,1)S(1)} %get-tuple-element.20.out_2.rest_1_, ...), custom_call_target="tpu_custom_call" | custom-call | tf_op jit(solution)/shard_map/synthesis/pallas_call | solution.py:692
  67.8 0.0 copy-start.1
  67.8 6.8 %analysis_back.1 = (bf16[2,8,128,512]{3,2,1,0:T(8,128)(2,1)S(1)}, bf16[2,4,128,256]{3,2,1,0:T(8,128)(2,1)S(1)}, bf16[2,2,128,128]{3,2,1,0:T(8,128)(2,1)S(1)}) custom-call(bf16[16,128,512]{2,1,0:T(8,128)(2,1)S(1)} %synthesis.1.values.rest_6_.plain, f32[2,4]{1,0:T(2,128)S(1)} %copy-done.13, bf16[512,512]{1,0:T(8,128)(2,1)S(1)} %copy-done.6, ...), custom_call_target="tpu_custom_call" | custom-call | tf_op jit(solution)/shard_map/analysis_back/pallas_call | solution.py:481
  74.6 0.0 copy-done.4
  74.6 29.2 %spectral_back.1 = (bf16[2,128,128]{2,1,0:T(8,128)(2,1)S(1)}, f32[128,128]{1,0:T(8,128)S(1)}, bf16[1280,128]{1,0:T(8,128)(2,1)S(1)}) custom-call(bf16[2,2,128,128]{3,2,1,0:T(8,128)(2,1)S(1)} %get-tuple-element.21.coarse_ref.out_3, f32[2,128,128]{2,1,0:T(8,128)S(1)} %and_select_fusion.col_ref.col_inv_ref, f32[128,128]{1,0:T(8,128)S(1)} %get-tuple-element.37.row_ref, ...), custom_call_target="tpu_custom_call" | custom-call | flops 16777216 | bytes 8388608 | tf_op jit(solution)/shard_map/spectral_back/pallas_call | solution.py:254
  103.8 0.0 copy-done.1
  103.8 27.7 %synthesis_back.1 = (f32[16,128,512]{2,1,0:T(8,128)}, bf16[1280,128]{1,0:T(8,128)(2,1)S(1)}) custom-call(bf16[2,128,128]{2,1,0:T(8,128)(2,1)S(1)} %get-tuple-element.24.image, bf16[2,8,128,512]{3,2,1,0:T(8,128)(2,1)S(1)} %get-tuple-element.22.rest_3_.out_1, bf16[2,4,128,256]{3,2,1,0:T(8,128)(2,1)S(1)} %get-tuple-element.23.rest_4_.out_2, ...), custom_call_target="tpu_custom_call" | custom-call | tf_op jit(solution)/shard_map/synthesis_back/pallas_call | solution.py:692
  131.6 0.6 slice.33
  132.3 0.9 slice.32
  133.1 2.3 %add_multiply_fusion = (f32[1,64,128,128]{3,2,1,0:T(8,128)S(1)}, f32[1,64,128,128]{3,2,1,0:T(8,128)S(1)}) fusion(f32[64,128]{1,0:T(8,128)S(1)} %bitcast.25, f32[64,128]{1,0:T(8,128)S(1)} %bitcast.23, f32[64,128]{1,0:T(8,128)S(1)} %bitcast.24, f32[64,128]{1,0:T(8,128)S(1)} %bitcast.22), kind=kLoop, calls=%fused_computation.4 | loop fusion | flops 8388608 | bytes 8519680 | tf_op jit(solution)/shard_map/mul | solution.py:821
  135.5 0.0 copy-start.14
  135.5 4.2 %pad_maximum_fusion = f32[2,64,128,128]{3,2,1,0:T(8,128)} fusion(f32[1,64,128,128]{3,2,1,0:T(8,128)S(1)} %get-tuple-element.31, f32[1,64,128,128]{3,2,1,0:T(8,128)S(1)} %get-tuple-element.30), kind=kLoop, calls=%fused_computation.2 | loop fusion | flops 2097152 | bytes 16777216 | tf_op jit(solution)/shard_map/stack | solution.py:829
  139.6 0.0 copy-done.14
  139.6 2.0 %copy.22 = f32[16,128,512]{2,1,0:T(8,128)} copy(f32[16,128,512]{2,1,0:T(8,128)S(1)} %copy-done.14) | data formatting | bytes 8388608
  (14 shorter events, 0.2 us)
Async XLA Ops:
  0.6 0.7 copy-start
  5.2 1.6 %copy-start.3 = (bf16[16,128,512]{2,1,0:T(8,128)(2,1)S(1)}, bf16[16,128,512]{2,1,0:T(8,128)(2,1)}, u32[]{:S(2)}) copy-start(bf16[16,128,512]{2,1,0:T(8,128)(2,1)} %rest_5_.1) | copy-start | bytes 6291460
  6.8 1.0 copy-start.5
  7.8 0.9 copy-start.7
  8.7 0.8 copy-start.10
  9.5 0.7 copy-start.12
  22.4 3.4 %copy-start.2 = (f32[2,64,128,128]{3,2,1,0:T(8,128)S(1)}, f32[2,64,128,128]{3,2,1,0:T(8,128)}, u32[]{:S(2)}) copy-start(f32[2,64,128,128]{3,2,1,0:T(8,128)} %weight_hbm.3) | copy-start | bytes 25165828
  25.8 24.8 %copy-start.6 = (bf16[512,512]{1,0:T(8,128)(2,1)S(1)}, bf16[512,512]{1,0:T(8,128)(2,1)}, u32[]{:S(2)}) copy-start(bf16[512,512]{1,0:T(8,128)(2,1)} %turned_1.3) | copy-start | bytes 1572868
  25.8 24.8 %copy-start.8 = (bf16[256,256]{1,0:T(8,128)(2,1)S(1)}, bf16[256,256]{1,0:T(8,128)(2,1)}, u32[]{:S(2)}) copy-start(bf16[256,256]{1,0:T(8,128)(2,1)} %turned_2.3) | copy-start | bytes 393220
  25.8 24.8 %copy-start.9 = (bf16[3,3,128,128]{3,2,1,0:T(8,128)(2,1)S(1)}, bf16[3,3,128,128]{3,2,1,0:T(8,128)(2,1)}, u32[]{:S(2)}) copy-start(bf16[3,3,128,128]{3,2,1,0:T(8,128)(2,1)} %detail.3) | copy-start | bytes 884740
  25.8 24.8 %copy-start.11 = (bf16[128,128]{1,0:T(8,128)(2,1)S(1)}, bf16[128,128]{1,0:T(8,128)(2,1)}, u32[]{:S(2)}) copy-start(bf16[128,128]{1,0:T(8,128)(2,1)} %skip.3) | copy-start | bytes 98308
  25.8 24.8 %copy-start.13 = (f32[2,4]{1,0:T(2,128)S(1)}, f32[2,4]{1,0:T(2,128)}, u32[]{:S(2)}) copy-start(f32[2,4]{1,0:T(2,128)} %taps.7) | copy-start | bytes 100
  50.6 24.0 %copy-start.4 = (bf16[16,128,512]{2,1,0:T(8,128)(2,1)S(1)}, bf16[16,128,512]{2,1,0:T(8,128)(2,1)}, u32[]{:S(2)}) copy-start(bf16[16,128,512]{2,1,0:T(8,128)(2,1)} %rest_5_.1) | copy-start | bytes 6291460
  67.8 36.1 %copy-start.1 = (bf16[16,128,512]{2,1,0:T(8,128)(2,1)}, bf16[16,128,512]{2,1,0:T(8,128)(2,1)S(1)}, u32[]{:S(2)}) copy-start(bf16[16,128,512]{2,1,0:T(8,128)(2,1)S(1)} %synthesis.1.values.rest_6_.plain) | copy-start | bytes 6291460
  135.5 4.2 %copy-start.14 = (f32[16,128,512]{2,1,0:T(8,128)S(1)}, f32[16,128,512]{2,1,0:T(8,128)}, u32[]{:S(2)}) copy-start(f32[16,128,512]{2,1,0:T(8,128)} %get-tuple-element.44) | copy-start | bytes 12582916

commit v4 on v3

--- a/solution.py
+++ b/solution.py
@@ -15,18 +15,17 @@
 TN = (((0,), (0,)), ((), ()))
 
 
-def enter_together(size):
+def greet_all(size):
     me = lax.axis_index("row")
     barrier = pltpu.get_barrier_semaphore()
-
-    def greet(step, carry):
+    for step in range(1, size):
         pl.semaphore_signal(
             barrier, inc=1, device_id={"row": lax.rem(me + step, size)}, device_id_type=MESH
         )
-        return carry
-
-    lax.fori_loop(1, size, greet, 0)
-    pl.semaphore_wait(barrier, size - 1)
+
+
+def hear_all(size):
+    pl.semaphore_wait(pltpu.get_barrier_semaphore(), size - 1)
 
 
 def tiles_copy(size, tile, send, land, send_sem, recv_sem, step):
@@ -115,7 +114,7 @@
 ):
     if back:
         full_field, full_slope = rest[:3], (*rest[3:5], coarse_ref)
-        field, upstream, image_ref, spec_ref, sums, *rest = rest[5:]
+        field, upstream, image_ref, spec_ref, share, sums, landed, more_sem, *rest = rest[5:]
     else:
         image_ref, spec_ref, *rest = rest
     (
@@ -134,7 +133,7 @@
     ) = rest
     fetch = pltpu.make_async_copy(weight_hbm, weight, weight_sem)
     fetch.start()
-    enter_together(size)
+    greet_all(size)
     rows = coarse_ref.shape[1]
     total = None
     for row in range(rows):
@@ -147,6 +146,7 @@
         )
         total = part if total is None else total + part
     send_a[...] = total
+    hear_all(size)
     tile_a = send_a.shape[0] // size
     first = start_exchange(size, tile_a, send_a, land_a, send_sem.at[0], recv_sem.at[0])
     if back:
@@ -157,6 +157,9 @@
     )
     tile_b = send_b.shape[0] // size
     second = start_exchange(size, tile_b, send_b, spec_ref, send_sem.at[1], recv_sem.at[1])
+    if back:
+        chunk = sums.shape[0] // size
+        scatter = start_exchange(size, chunk, sums, landed, more_sem.at[0], more_sem.at[1])
     second.wait_recv()
     spec = spec_ref[...]
     count = spec.shape[0]
@@ -206,6 +209,13 @@
         row_inv_ref[...], land_c[...], NN, precision=HIGHEST, preferred_element_type=jnp.float32
     )
     fourth = start_exchange(size, tile_a, send_d, land_d, send_sem.at[3], recv_sem.at[3])
+    if back:
+        scatter.wait_recv()
+        whole = as_float(landed[0:chunk, :])
+        for step in range(1, size):
+            whole = whole + as_float(landed[step * chunk : (step + 1) * chunk, :])
+        share[...] = whole.astype(jnp.bfloat16)
+        scatter.wait_send()
     fourth.wait_recv()
     across = land_d[...].T
     for row in range(rows):
@@ -214,6 +224,11 @@
         ).astype(jnp.bfloat16)
     for sent in (first, second, third, fourth):
         sent.wait_send()
+
+
+def picked(modes, places):
+    same = places[:, None] == jnp.arange(modes.shape[0])[None, :]
+    return jnp.sum(jnp.where(same, modes[None, :], 0), axis=1)
 
 
 def spectral_tables(row_modes, col_modes, local_rows, columns, size):
@@ -225,7 +240,7 @@
     part_a, part_b = where_a % 2, where_b % 2
     spot = where_a // 2
     block = spot // (near_cols * local_rows)
-    col_of = col_modes[block * near_cols + spot % near_cols]
+    col_of = picked(col_modes, block * near_cols + spot % near_cols)
     wide = jnp.arange(2 * columns)
     turns = (col_of[:, None] * wide[None, :] + part_a[:, None] * (columns // 4)) % columns
     col = jnp.cos(turns.astype(jnp.float32) * (2.0 * math.pi / columns))
@@ -233,7 +248,7 @@
     inside = wide < columns
     col = jnp.where(same_row[:, :, None] & inside[None, None, :], col[None], 0.0)
     col_inv = col
-    row_of = row_modes[where_b // (2 * near_cols)]
+    row_of = picked(row_modes, where_b // (2 * near_cols))
     quarter = (part_b[:, None] - part_a[None, :]) * (height // 4)
     turns = (row_of[:, None] * (where_a // (2 * near_cols))[None, :] + quarter + height) % height
     same_col = (where_b // 2 % near_cols)[:, None] == (where_a // 2 % near_cols)[None, :]
@@ -256,11 +271,20 @@
         out_shape=(
             jax.ShapeDtypeStruct(coarse.shape[1:], jnp.bfloat16),
             jax.ShapeDtypeStruct((count_b, channels), f32),
-            *([jax.ShapeDtypeStruct((sum_rows, channels), jnp.bfloat16)] if back else []),
+            *([jax.ShapeDtypeStruct((sum_rows // size, channels), jnp.bfloat16)] if back else []),
         ),
-        in_specs=[vmem] * 5 + [pl.BlockSpec(memory_space=pl.ANY)] + [vmem] * len(extra),
+        in_specs=[vmem] * 5 + [pl.BlockSpec(memory_space=pltpu.HBM)] + [vmem] * len(extra),
         out_specs=(vmem,) * (3 if back else 2),
         scratch_shapes=[
+            *(
+                [
+                    pltpu.VMEM((sum_rows, channels), jnp.bfloat16),
+                    pltpu.VMEM((sum_rows, channels), jnp.bfloat16),
+                    pltpu.SemaphoreType.DMA((2,)),
+                ]
+                if back
+                else []
+            ),
             pltpu.VMEM(weight.shape, f32),
             pltpu.VMEM((count_a, channels), f32),
             pltpu.VMEM((count_a, channels), f32),
@@ -277,7 +301,7 @@
         compiler_params=pltpu.CompilerParams(
             collective_id=1 if back else 0,
             has_side_effects=True,
-            vmem_limit_bytes=40 * 1024 * 1024,
+            vmem_limit_bytes=24 * 1024 * 1024,
         ),
         cost_estimate=pl.CostEstimate(
             flops=8 * weight.size, bytes_accessed=4 * weight.size, transcendentals=0
@@ -286,11 +310,44 @@
     )(coarse, col, row, row_inv, col_inv, weight, *extra)
 
 
-def spec_parts(spec, mode_rows, mode_cols, size):
-    channels = spec.shape[1]
-    grid = spec.reshape(size, mode_rows // size, mode_cols // size, 2, channels)
-    grid = jnp.transpose(grid, (3, 1, 0, 2, 4)).reshape(2, -1, channels)
-    return grid[0], grid[1]
+def outer_kernel(factor, field_ref, slope_ref, out_ref):
+    slope = slope_ref[...] * factor
+    count = slope.shape[0]
+    even = lax.broadcasted_iota(jnp.int32, slope.shape, 0) % 2 == 0
+    turned = jnp.where(even, pltpu.roll(slope, count - 1, 0), -pltpu.roll(slope, 1, 0))
+    both = jnp.concatenate([slope, turned], axis=1)
+    across = field_ref[...].T
+    channels = across.shape[0]
+    pair = lax.broadcasted_iota(jnp.int32, across.shape, 1) // 2
+    near_cols = out_ref.shape[3]
+    for mode in range(count // 2):
+        done = jnp.dot(
+            jnp.where(pair == mode, across, 0.0), both, preferred_element_type=jnp.float32
+        )
+        for part in range(2):
+            out_ref[part, mode // near_cols, 0, mode % near_cols] = done[
+                :, part * channels : (part + 1) * channels
+            ]
+
+
+def outer_products(spec_field, spec_slope, near_rows, near_cols, factor):
+    size = lax.axis_size("row")
+    count, channels = spec_field.shape
+    tile = count // size
+    shape = (2, near_rows, size, near_cols, channels, channels)
+    spec = pl.BlockSpec((tile, channels), lambda block: (block, 0))
+    result = pl.pallas_call(
+        functools.partial(outer_kernel, factor),
+        grid=(size,),
+        out_shape=jax.ShapeDtypeStruct(shape, jnp.float32),
+        in_specs=[spec, spec],
+        out_specs=pl.BlockSpec(
+            (2, near_rows, 1, near_cols, channels, channels),
+            lambda block: (0, 0, block, 0, 0, 0),
+        ),
+        name="outer_products",
+    )(spec_field, spec_slope)
+    return result.reshape(2, -1, channels, channels)
 
 
 def as_float(values):
@@ -494,7 +551,10 @@
         compiler_params=pltpu.CompilerParams(
             collective_id=3 if back else 2,
             has_side_effects=True,
-            vmem_limit_bytes=40 * 1024 * 1024,
+            vmem_limit_bytes=24 * 1024 * 1024,
+        ),
+        cost_estimate=pl.CostEstimate(
+            flops=6 * values.size * columns, bytes_accessed=16 * values.size, transcendentals=0
         ),
         name="analysis_back" if back else "analysis",
     )(values, row_filters, *matrices)
@@ -526,7 +586,7 @@
     *rest,
 ):
     if back:
-        sums, result, gathered, landed, total, send_more, recv_more, *rest = rest
+        share, result, gathered, send_more, recv_more, *rest = rest
     else:
         cotangent, result, detail_turned, skip_turned, *rest = rest
         for level in range(3):
@@ -540,7 +600,8 @@
     me = lax.axis_index("row")
     above, below = lax.rem(me + size - 1, size), lax.rem(me + 1, size)
     if back:
-        enter_together(size)
+        greet_all(size)
+        hear_all(size)
     else:
         greet_ring(above)
 
@@ -625,8 +686,18 @@
     third = copy(2, syn_3, halo_3)
     third.start()
     if back:
-        chunk = sums.shape[0] // size
-        scatter = start_exchange(size, chunk, sums, landed, send_more.at[0], recv_more.at[0])
+        chunk = share.shape[0]
+        target = pl.ds(pl.multiple_of(me * chunk, chunk), chunk)
+        for step in range(1, size):
+            pltpu.make_async_remote_copy(
+                src_ref=share,
+                dst_ref=gathered.at[target],
+                send_sem=send_more.at[0],
+                recv_sem=recv_more.at[0],
+                device_id={"row": lax.rem(me + step, size)},
+                device_id_type=MESH,
+            ).start()
+        gathered[target, :] = share[...]
     span(0, rows_3 - 1, level_3)
     combine(syn_3, rows_3 - 1, None, top_2)
     level_2(rows_2 - 1)
@@ -645,23 +716,6 @@
     span(0, rows_2 - 2, level_2)
     span(1, rows_2 - 1, lambda row: combine(syn_2, row, None, top_1))
     span(2, rows_1 - 2, level_1)
-    if back:
-        scatter.wait_recv()
-        whole = as_float(landed[0:chunk, :])
-        for step in range(1, size):
-            whole = whole + as_float(landed[step * chunk : (step + 1) * chunk, :])
-        total[...] = whole.astype(jnp.bfloat16)
-        target = pl.ds(pl.multiple_of(me * chunk, chunk), chunk)
-        for step in range(1, size):
-            pltpu.make_async_remote_copy(
-                src_ref=total,
-                dst_ref=gathered.at[target],
-                send_sem=send_more.at[1],
-                recv_sem=recv_more.at[1],
-                device_id={"row": lax.rem(me + step, size)},
-                device_id_type=MESH,
-            ).start()
-        gathered[target, :] = total[...]
     span(3, rows_1 - 1, lambda row: last(row, None))
     second.wait()
     combine(syn_2, 0, halo_2, top_1)
@@ -670,8 +724,7 @@
     first.wait()
     last(0, halo_1)
     if back:
-        scatter.wait_send()
-        tiles_copy(size, chunk, landed, gathered, send_more.at[1], recv_more.at[1], 0).wait()
+        tiles_copy(size, chunk, gathered, gathered, send_more.at[0], recv_more.at[0], 0).wait()
 
 
 def synthesis_call(image, bands, row_filters, matrices, detail, skip, plain, extra, back):
@@ -682,13 +735,9 @@
     result = jax.ShapeDtypeStruct(plain.shape, jnp.float32 if back else jnp.bfloat16)
     own = [pltpu.VMEM(detail.shape, jnp.bfloat16), pltpu.VMEM(skip.shape, jnp.bfloat16)]
     if back:
-        result = (result, jax.ShapeDtypeStruct(extra.shape, jnp.bfloat16))
-        own = [
-            pltpu.VMEM(extra.shape, jnp.bfloat16),
-            pltpu.VMEM((extra.shape[0] // size, channels), jnp.bfloat16),
-            pltpu.SemaphoreType.DMA((2,)),
-            pltpu.SemaphoreType.DMA((2,)),
-        ]
+        whole = (extra.shape[0] * size, channels)
+        result = (result, jax.ShapeDtypeStruct(whole, jnp.bfloat16))
+        own = [pltpu.SemaphoreType.DMA((1,)), pltpu.SemaphoreType.DMA((1,))]
     return pl.pallas_call(
         functools.partial(synthesis_kernel, size, back),
         out_shape=result,
@@ -707,6 +756,11 @@
             collective_id=5 if back else 4,
             has_side_effects=True,
             vmem_limit_bytes=48 * 1024 * 1024,
+        ),
+        cost_estimate=pl.CostEstimate(
+            flops=6 * plain.size * plain.shape[2],
+            bytes_accessed=32 * plain.size,
+            transcendentals=plain.size,
         ),
         name="synthesis_back" if back else "synthesis",
     )(image, *bands, row_filters, *matrices, detail, skip, plain, extra)
@@ -759,10 +813,9 @@
     if whole_tiles:
         near_cols = mode_cols // devices
         tables = spectral_tables(row_modes, col_modes, local_rows, columns, devices)
-        coarse_image, spec = spectral_path(
+        coarse_image, spec_field = spectral_path(
             full_field[2], spectral_weight, tables, near_cols, (), scales, sum_rows
         )
-        spec_real, spec_imag = spec_parts(spec, mode_rows, mode_cols, devices)
     else:
         spec_real, spec_imag = owned_modes(coarse_field, row_modes, col_modes)
         out_real, out_imag = mix_modes(spec_real, spec_imag, weight_real, weight_imag, factor)
@@ -783,10 +836,9 @@
     coarse_slope, bands_slope = split_bands(full_slope)
     if whole_tiles:
         extra = (*full_field, *full_slope[:2], field, upstream)
-        image_back, spec, sums = spectral_path(
+        image_back, spec_back, share = spectral_path(
             full_slope[2], spectral_weight, tables, near_cols, extra, scales, sum_rows
         )
-        back_real, back_imag = spec_parts(spec, mode_rows, mode_cols, devices)
     else:
         back_real, back_imag = owned_modes(coarse_slope, row_modes, col_modes)
         turned_real, turned_imag = mix_modes_back(
@@ -802,8 +854,10 @@
             for octave in range(3)
             for member in range(3)
         ] + [narrow("hcw,how->co", field, upstream) * scales[3]]
-        sums = jnp.concatenate(shares, axis=0).astype(jnp.bfloat16)
+        sums = jnp.concatenate(shares, axis=0)
         sums = jnp.pad(sums, ((0, sum_rows - sums.shape[0]), (0, 0)))
+        share = lax.psum_scatter(sums, "row", scatter_dimension=0, tiled=True)
+        share = share.astype(jnp.bfloat16)
     grad_field, gathered = synthesis_call(
         image_back,
         full_slope,
@@ -812,21 +866,25 @@
         detail_weight,
         skip_weight,
         upstream,
-        sums,
+        share,
         True,
     )
     gathered = as_float(gathered[: 10 * channels])
     grad_detail = gathered[: 9 * channels].reshape(3, 3, channels, channels)
     grad_skip = gathered[9 * channels :]
-    grad_real = (
-        spec_real[:, :, None] * back_real[:, None, :]
-        + spec_imag[:, :, None] * back_imag[:, None, :]
-    ) * factor
-    grad_imag = (
-        spec_real[:, :, None] * back_imag[:, None, :]
-        - spec_imag[:, :, None] * back_real[:, None, :]
-    ) * factor
-    grad_spectral = jnp.stack([grad_real, grad_imag])
+    if whole_tiles:
+        near_rows = mode_rows // devices
+        grad_spectral = outer_products(spec_field, spec_back, near_rows, near_cols, factor)
+    else:
+        grad_real = (
+            spec_real[:, :, None] * back_real[:, None, :]
+            + spec_imag[:, :, None] * back_imag[:, None, :]
+        ) * factor
+        grad_imag = (
+            spec_real[:, :, None] * back_imag[:, None, :]
+            - spec_imag[:, :, None] * back_real[:, None, :]
+        ) * factor
+        grad_spectral = jnp.stack([grad_real, grad_imag])
     return (grad_field, grad_detail, grad_skip, grad_spectral)
 
 

time: 142 us -> 144 us (1.014)
  Pallas kernels: 118 us -> 124 us
  other arithmetic: 7.62 us -> 2.58 us
    pallas_call x0 -> x1, Pallas kernels: none -> 10.5 us  [outer_products(): pl.pallas_call(functools.partial(outer_kernel, factor), grid=(size,), out...]
    pallas_call x2, Pallas kernels: 44.9 us -> 37.4 us  [synthesis_call(): pl.pallas_call(functools.partial(synthesis_kernel, size, back), out_shape...]
    another operation x1 -> x0, other arithmetic: 4.16 us -> none  [per_device(): grad_spectral = jnp.stack([grad_real, grad_imag])]
    unnamed x31 -> x43, local copies, waits for them, and re-layouts: 10.9 us -> 14.7 us
    gather x2 -> x0, local copies, waits for them, and re-layouts: 2.81 us -> none  [the longest x1 1.59 us: spectral_tables(): col_of = col_modes[block * near_cols + spot % near_cols]]
    pallas_call x2, Pallas kernels: 53.9 us -> 56.7 us  [spectral_path(): pl.pallas_call(functools.partial(spectral_kernel, size, near_cols, back,...]
    mul x1 -> x0, other arithmetic: 2.34 us -> none  [per_device(): (spec_real[:, :, None] * back_real[:, None, :] + spec_imag[:, :, None] *...]
    reduce_sum x0 -> x2, other arithmetic: none -> 1.49 us  [picked(): return jnp.sum(jnp.where(same, modes[None, :], 0), axis=1)]
where the time goes in v4:
time: 144 us; the launch traced here: 143 us
  Pallas kernels  124 us (86%)
  local copies, waits for them, and re-layouts  16.2 us (11%)
  other arithmetic  2.58 us (2%)
    pallas_call x2, Pallas kernels, spectral_path(): pl.pallas_call(functools.partial(spectral_kernel, size, near_cols, back,...  56.7 us
    pallas_call x2, Pallas kernels, synthesis_call(): pl.pallas_call(functools.partial(synthesis_kernel, size, back), out_shape...  37.4 us
    pallas_call x2, Pallas kernels, analysis_call(): pl.pallas_call(functools.partial(analysis_kernel, size), out_shape=tuple(...  19.1 us
    unnamed x43, local copies, waits for them, and re-layouts  14.7 us
    pallas_call x1, Pallas kernels, outer_products(): pl.pallas_call(functools.partial(outer_kernel, factor), grid=(size,), out...  10.5 us

profile of v4, /device:TPU:0, one launch (start us, length us, event | category | flops | bytes accessed | tf_op | source)
XLA Modules:
  0.0 143.2 jit_solution(2527595475895152655)
XLA Ops:
  0.7 0.7 select_reduce_fusion.1
  1.5 0.7 select_reduce_fusion
  2.2 0.3 fusion.3
  2.6 0.1 and_select_fusion.col_ref.col_inv_ref
  2.7 0.6 fusion.14
  3.3 0.0 copy-start.1
  3.3 1.6 %copy-done.1 = bf16[16,128,512]{2,1,0:T(8,128)(2,1)S(1)} copy-done((bf16[16,128,512]{2,1,0:T(8,128)(2,1)S(1)}, bf16[16,128,512]{2,1,0:T(8,128)(2,1)}, u32[]{:S(2)}) %copy-start.1) | copy-done | bytes 2097176
  4.9 1.0 copy-done.10
  5.9 0.9 copy-done.14
  6.8 0.8 copy-done.16
  7.6 0.7 copy-done.19
  8.2 12.2 %analysis.1 = (bf16[2,8,128,512]{3,2,1,0:T(8,128)(2,1)S(1)}, bf16[2,4,128,256]{3,2,1,0:T(8,128)(2,1)S(1)}, bf16[2,2,128,128]{3,2,1,0:T(8,128)(2,1)S(1)}) custom-call(bf16[16,128,512]{2,1,0:T(8,128)(2,1)S(1)} %copy-done.1, f32[2,4]{1,0:T(2,128)S(1)} %copy-done.19, bf16[512,512]{1,0:T(8,128)(2,1)S(1)} %copy-done.10, bf16[256,256]{1,0:T(8,128)(2,1)S(1)} %copy-done.14, ...), custom_call_target="tpu_custom_call" | custom-call | flops 3221225472 | bytes 16777216 | tf_op jit(solution)/shard_map/analysis/pallas_call | solution.py:538
  20.5 0.0 copy-done
  20.5 0.0 copy-start.11
  20.5 0.0 copy-start.12
  20.5 0.0 copy-start.15
  20.5 0.0 copy-start.17
  20.5 0.0 copy-start.18
  20.6 0.0 copy-start.20
  20.6 24.2 %spectral.1 = (bf16[2,128,128]{2,1,0:T(8,128)(2,1)S(1)}, f32[128,128]{1,0:T(8,128)S(1)}) custom-call(bf16[2,2,128,128]{3,2,1,0:T(8,128)(2,1)S(1)} %get-tuple-element.17.coarse_ref.out_3.rest_2_, f32[2,128,128]{2,1,0:T(8,128)S(1)} %and_select_fusion.col_ref.col_inv_ref, f32[128,128]{1,0:T(8,128)S(1)} %get-tuple-element.31.row_ref, ...), custom_call_target="tpu_custom_call" | custom-call | flops 16777216 | bytes 8388608 | tf_op jit(solution)/shard_map/spectral/pallas_call | solution.py:269
  44.8 0.0 copy-start.8
  44.8 0.6 copy-done.8
  45.4 0.0 copy-done.11
  45.4 0.0 copy-done.12
  45.4 0.0 copy-done.15
  45.4 0.0 copy-done.17
  45.4 0.0 copy-done.18
  45.4 0.0 copy-done.20
  45.5 17.0 %synthesis.1.values.rest_6_.plain = bf16[16,128,512]{2,1,0:T(8,128)(2,1)S(1)} custom-call(bf16[2,128,128]{2,1,0:T(8,128)(2,1)S(1)} %get-tuple-element.18.image, bf16[2,8,128,512]{3,2,1,0:T(8,128)(2,1)S(1)} %get-tuple-element.19.out_1.rest_0_, bf16[2,4,128,256]{3,2,1,0:T(8,128)(2,1)S(1)} %get-tuple-element.20.out_2.rest_1_, ...), custom_call_target="tpu_custom_call" | custom-call | flops 3221225472 | bytes 33554432 | tf_op jit(solution)/shard_map/synthesis/pallas_call | solution.py:741
  62.5 0.0 copy-start.3
  62.5 0.0 copy-start.2
  62.5 6.8 %analysis_back.1 = (bf16[2,8,128,512]{3,2,1,0:T(8,128)(2,1)S(1)}, bf16[2,4,128,256]{3,2,1,0:T(8,128)(2,1)S(1)}, bf16[2,2,128,128]{3,2,1,0:T(8,128)(2,1)S(1)}) custom-call(bf16[16,128,512]{2,1,0:T(8,128)(2,1)S(1)} %synthesis.1.values.rest_6_.plain, f32[2,4]{1,0:T(2,128)S(1)} %copy-done.20, bf16[512,512]{1,0:T(8,128)(2,1)S(1)} %copy-done.11, ...), custom_call_target="tpu_custom_call" | custom-call | flops 3221225472 | bytes 16777216 | tf_op jit(solution)/shard_map/analysis_back/pallas_call | solution.py:538
  69.3 0.0 copy-start.4
  69.3 0.0 copy-start.6
  69.3 0.0 copy-done.3
  69.3 0.0 copy-done.2
  69.3 32.5 %spectral_back.1 = (bf16[2,128,128]{2,1,0:T(8,128)(2,1)S(1)}, f32[128,128]{1,0:T(8,128)S(1)}, bf16[80,128]{1,0:T(8,128)(2,1)S(1)}) custom-call(bf16[2,2,128,128]{3,2,1,0:T(8,128)(2,1)S(1)} %get-tuple-element.21.coarse_ref.out_3, f32[2,128,128]{2,1,0:T(8,128)S(1)} %and_select_fusion.col_ref.col_inv_ref, f32[128,128]{1,0:T(8,128)S(1)} %get-tuple-element.31.row_ref, ...), custom_call_target="tpu_custom_call" | custom-call | flops 16777216 | bytes 8388608 | tf_op jit(solution)/shard_map/spectral_back/pallas_call | solution.py:269
  101.8 0.0 copy-done.4
  101.8 0.0 copy-done.6
  101.8 0.6 copy-done.9
  102.5 1.6 %copy-done.5 = bf16[2,8,128,512]{3,2,1,0:T(8,128)(2,1)S(1)} copy-done((bf16[2,8,128,512]{3,2,1,0:T(8,128)(2,1)S(1)}, bf16[2,8,128,512]{3,2,1,0:T(8,128)(2,1)}, u32[]{:S(2)}) %copy-start.5) | copy-done | bytes 2097176
  104.1 1.0 copy-done.7
  105.1 1.0 copy-done.13
  106.1 20.4 %synthesis_back.1 = (f32[16,128,512]{2,1,0:T(8,128)}, bf16[1280,128]{1,0:T(8,128)(2,1)S(1)}) custom-call(bf16[2,128,128]{2,1,0:T(8,128)(2,1)S(1)} %get-tuple-element.24.image, bf16[2,8,128,512]{3,2,1,0:T(8,128)(2,1)S(1)} %copy-done.5, bf16[2,4,128,256]{3,2,1,0:T(8,128)(2,1)S(1)} %copy-done.7, ...), custom_call_target="tpu_custom_call" | custom-call | flops 3221225472 | bytes 33554432 | tf_op jit(solution)/shard_map/synthesis_back/pallas_call | solution.py:741
  126.5 0.6 slice.9
  127.1 0.9 slice.8
  128.0 10.5 %outer_products.1 = f32[2,2,16,2,128,128]{5,4,3,2,1,0:T(8,128)} custom-call(f32[128,128]{1,0:T(8,128)} %copy-done.8, f32[128,128]{1,0:T(8,128)} %copy-done.9), custom_call_target="tpu_custom_call" | custom-call | tf_op jit(solution)/shard_map/outer_products/pallas_call | solution.py:339
  138.4 4.8 %copy.16 = f32[16,128,512]{2,1,0:T(8,128)} copy(f32[16,128,512]{2,1,0:T(8,128)} %get-tuple-element.38) | data formatting | bytes 8388608
  (16 shorter events, 0.1 us)
Async XLA Ops:
  3.3 1.6 %copy-start.1 = (bf16[16,128,512]{2,1,0:T(8,128)(2,1)S(1)}, bf16[16,128,512]{2,1,0:T(8,128)(2,1)}, u32[]{:S(2)}) copy-start(bf16[16,128,512]{2,1,0:T(8,128)(2,1)} %rest_5_.1) | copy-start | bytes 6291460
  4.9 1.0 copy-start.10
  5.9 0.9 copy-start.14
  6.8 0.8 copy-start.16
  7.6 0.7 copy-start.19
  8.2 12.2 %copy-start = (f32[2,64,128,128]{3,2,1,0:T(8,128)S(1)}, f32[2,64,128,128]{3,2,1,0:T(8,128)}, u32[]{:S(2)}) copy-start(f32[2,64,128,128]{3,2,1,0:T(8,128)} %weight_hbm.3) | copy-start | bytes 25165828
  20.5 24.9 %copy-start.11 = (bf16[512,512]{1,0:T(8,128)(2,1)S(1)}, bf16[512,512]{1,0:T(8,128)(2,1)}, u32[]{:S(2)}) copy-start(bf16[512,512]{1,0:T(8,128)(2,1)} %turned_1.3) | copy-start | bytes 1572868
  20.5 24.9 %copy-start.12 = (bf16[3,3,128,128]{3,2,1,0:T(8,128)(2,1)S(1)}, bf16[3,3,128,128]{3,2,1,0:T(8,128)(2,1)}, u32[]{:S(2)}) copy-start(bf16[3,3,128,128]{3,2,1,0:T(8,128)(2,1)} %detail.3) | copy-start | bytes 884740
  20.5 24.9 %copy-start.15 = (bf16[256,256]{1,0:T(8,128)(2,1)S(1)}, bf16[256,256]{1,0:T(8,128)(2,1)}, u32[]{:S(2)}) copy-start(bf16[256,256]{1,0:T(8,128)(2,1)} %turned_2.3) | copy-start | bytes 393220
  20.5 24.9 %copy-start.17 = (bf16[128,128]{1,0:T(8,128)(2,1)S(1)}, bf16[128,128]{1,0:T(8,128)(2,1)}, u32[]{:S(2)}) copy-start(bf16[128,128]{1,0:T(8,128)(2,1)} %turned_3.3) | copy-start | bytes 98308
  20.5 24.9 %copy-start.18 = (bf16[128,128]{1,0:T(8,128)(2,1)S(1)}, bf16[128,128]{1,0:T(8,128)(2,1)}, u32[]{:S(2)}) copy-start(bf16[128,128]{1,0:T(8,128)(2,1)} %skip.3) | copy-start | bytes 98308
  20.6 24.9 %copy-start.20 = (f32[2,4]{1,0:T(2,128)S(1)}, f32[2,4]{1,0:T(2,128)}, u32[]{:S(2)}) copy-start(f32[2,4]{1,0:T(2,128)} %taps.7) | copy-start | bytes 100
  44.8 0.6 copy-start.8
  62.5 6.9 %copy-start.3 = (bf16[16,128,512]{2,1,0:T(8,128)(2,1)}, bf16[16,128,512]{2,1,0:T(8,128)(2,1)S(1)}, u32[]{:S(2)}) copy-start(bf16[16,128,512]{2,1,0:T(8,128)(2,1)S(1)} %synthesis.1.values.rest_6_.plain) | copy-start | bytes 6291460
  62.5 6.9 %copy-start.2 = (bf16[16,128,512]{2,1,0:T(8,128)(2,1)S(1)}, bf16[16,128,512]{2,1,0:T(8,128)(2,1)}, u32[]{:S(2)}) copy-start(bf16[16,128,512]{2,1,0:T(8,128)(2,1)} %rest_5_.1) | copy-start | bytes 6291460
  69.3 32.5 %copy-start.4 = (bf16[2,8,128,512]{3,2,1,0:T(8,128)(2,1)}, bf16[2,8,128,512]{3,2,1,0:T(8,128)(2,1)S(1)}, u32[]{:S(2)}) copy-start(bf16[2,8,128,512]{3,2,1,0:T(8,128)(2,1)S(1)} %get-tuple-element.22.rest_3_.out_1) | copy-start | bytes 6291460
  69.3 32.5 %copy-start.6 = (bf16[2,4,128,256]{3,2,1,0:T(8,128)(2,1)}, bf16[2,4,128,256]{3,2,1,0:T(8,128)(2,1)S(1)}, u32[]{:S(2)}) copy-start(bf16[2,4,128,256]{3,2,1,0:T(8,128)(2,1)S(1)} %get-tuple-element.23.rest_4_.out_2) | copy-start | bytes 1572868
  101.8 0.6 copy-start.9
  102.5 1.6 %copy-start.5 = (bf16[2,8,128,512]{3,2,1,0:T(8,128)(2,1)S(1)}, bf16[2,8,128,512]{3,2,1,0:T(8,128)(2,1)}, u32[]{:S(2)}) copy-start(bf16[2,8,128,512]{3,2,1,0:T(8,128)(2,1)} %copy-done.4) | copy-start | bytes 6291460
  104.1 1.0 copy-start.7
  105.1 1.0 copy-start.13

commit v5 on v4

--- a/solution.py
+++ b/solution.py
@@ -9,10 +9,8 @@
 from jax.sharding import PartitionSpec as P
 
 MESH = pl.DeviceIdType.MESH
-HIGHEST = lax.Precision.HIGHEST
 NN = (((1,), (0,)), ((), ()))
 NT = (((1,), (1,)), ((), ()))
-TN = (((0,), (0,)), ((), ()))
 
 
 def greet_all(size):
@@ -60,8 +58,8 @@
     return lax.dot_general(first, second, NT, preferred_element_type=jnp.float32)
 
 
-def local_sums(full_field, full_slope, field, upstream, sums, scales, skip_scale):
-    channels = field.shape[1]
+def local_sums(full_field, full_slope, skip_share, sums, scales, skip_scale):
+    channels = skip_share.shape[0]
     for level in range(3):
         left, right = full_field[level], full_slope[level]
         half = left.shape[3] // 2
@@ -86,13 +84,9 @@
             )
             start = (level * 3 + member) * channels
             sums[start : start + channels, :] = (total * scales[level]).astype(jnp.bfloat16)
-    total = lax.fori_loop(
-        0,
-        field.shape[0],
-        lambda row, total: total + channel_product(field[row], upstream[row]),
-        jnp.zeros((channels, channels), jnp.float32),
-    )
-    sums[9 * channels : 10 * channels, :] = (total * skip_scale).astype(jnp.bfloat16)
+    sums[9 * channels : 10 * channels, :] = (skip_share[...] * skip_scale).astype(
+        jnp.bfloat16
+    )
     if sums.shape[0] > 10 * channels:
         sums[10 * channels :, :] = jnp.zeros(
             (sums.shape[0] - 10 * channels, channels), jnp.bfloat16
@@ -109,16 +103,15 @@
     row_ref,
     row_inv_ref,
     col_inv_ref,
-    weight_hbm,
+    weight,
     *rest,
 ):
     if back:
         full_field, full_slope = rest[:3], (*rest[3:5], coarse_ref)
-        field, upstream, image_ref, spec_ref, share, sums, landed, more_sem, *rest = rest[5:]
+        skip_share, image_ref, spec_ref, share, sums, landed, more_sem, *rest = rest[5:]
     else:
         image_ref, spec_ref, *rest = rest
     (
-        weight,
         send_a,
         land_a,
         send_b,
@@ -127,21 +120,17 @@
         send_d,
         land_d,
         rotated,
-        weight_sem,
         send_sem,
         recv_sem,
     ) = rest
-    fetch = pltpu.make_async_copy(weight_hbm, weight, weight_sem)
-    fetch.start()
     greet_all(size)
     rows = coarse_ref.shape[1]
     total = None
     for row in range(rows):
         part = lax.dot_general(
-            col_ref[row],
-            coarse_ref[0, row].astype(jnp.float32),
+            col_ref[row].astype(jnp.bfloat16),
+            coarse_ref[0, row],
             NT,
-            precision=HIGHEST,
             preferred_element_type=jnp.float32,
         )
         total = part if total is None else total + part
@@ -150,10 +139,13 @@
     tile_a = send_a.shape[0] // size
     first = start_exchange(size, tile_a, send_a, land_a, send_sem.at[0], recv_sem.at[0])
     if back:
-        local_sums(full_field, full_slope, field, upstream, sums, scales[:3], scales[3])
+        local_sums(full_field, full_slope, skip_share, sums, scales[:3], scales[3])
     first.wait_recv()
     send_b[...] = lax.dot_general(
-        row_ref[...], land_a[...], NN, precision=HIGHEST, preferred_element_type=jnp.float32
+        row_ref[...].astype(jnp.bfloat16),
+        land_a[...].astype(jnp.bfloat16),
+        NN,
+        preferred_element_type=jnp.float32,
     )
     tile_b = send_b.shape[0] // size
     second = start_exchange(size, tile_b, send_b, spec_ref, send_sem.at[1], recv_sem.at[1])
@@ -166,7 +158,6 @@
     even = lax.broadcasted_iota(jnp.int32, spec.shape, 0) % 2 == 0
     turned = jnp.where(even, -pltpu.roll(spec, count - 1, 0), pltpu.roll(spec, 1, 0))
     rotated[...] = -turned if back else turned
-    fetch.wait()
     per_tile = tile_b // 2
     modes = weight.shape[1]
     per_row = near_cols
@@ -206,7 +197,10 @@
     third = start_exchange(size, tile_b, send_c, land_c, send_sem.at[2], recv_sem.at[2])
     third.wait_recv()
     send_d[...] = lax.dot_general(
-        row_inv_ref[...], land_c[...], NN, precision=HIGHEST, preferred_element_type=jnp.float32
+        row_inv_ref[...].astype(jnp.bfloat16),
+        land_c[...].astype(jnp.bfloat16),
+        NN,
+        preferred_element_type=jnp.float32,
     )
     fourth = start_exchange(size, tile_a, send_d, land_d, send_sem.at[3], recv_sem.at[3])
     if back:
@@ -217,10 +211,13 @@
         share[...] = whole.astype(jnp.bfloat16)
         scatter.wait_send()
     fourth.wait_recv()
-    across = land_d[...].T
+    across = land_d[...].T.astype(jnp.bfloat16)
     for row in range(rows):
         image_ref[row] = lax.dot_general(
-            across, col_inv_ref[row], NN, precision=HIGHEST, preferred_element_type=jnp.float32
+            across,
+            col_inv_ref[row].astype(jnp.bfloat16),
+            NN,
+            preferred_element_type=jnp.float32,
         ).astype(jnp.bfloat16)
     for sent in (first, second, third, fourth):
         sent.wait_send()
@@ -273,7 +270,7 @@
             jax.ShapeDtypeStruct((count_b, channels), f32),
             *([jax.ShapeDtypeStruct((sum_rows // size, channels), jnp.bfloat16)] if back else []),
         ),
-        in_specs=[vmem] * 5 + [pl.BlockSpec(memory_space=pltpu.HBM)] + [vmem] * len(extra),
+        in_specs=[vmem] * (6 + len(extra)),
         out_specs=(vmem,) * (3 if back else 2),
         scratch_shapes=[
             *(
@@ -285,7 +282,6 @@
                 if back
                 else []
             ),
-            pltpu.VMEM(weight.shape, f32),
             pltpu.VMEM((count_a, channels), f32),
             pltpu.VMEM((count_a, channels), f32),
             pltpu.VMEM((count_b, channels), f32),
@@ -294,7 +290,6 @@
             pltpu.VMEM((count_a, channels), f32),
             pltpu.VMEM((count_a, channels), f32),
             pltpu.VMEM((count_b, channels), f32),
-            pltpu.SemaphoreType.DMA,
             pltpu.SemaphoreType.DMA((4,)),
             pltpu.SemaphoreType.DMA((4,)),
         ],
@@ -310,44 +305,11 @@
     )(coarse, col, row, row_inv, col_inv, weight, *extra)
 
 
-def outer_kernel(factor, field_ref, slope_ref, out_ref):
-    slope = slope_ref[...] * factor
-    count = slope.shape[0]
-    even = lax.broadcasted_iota(jnp.int32, slope.shape, 0) % 2 == 0
-    turned = jnp.where(even, pltpu.roll(slope, count - 1, 0), -pltpu.roll(slope, 1, 0))
-    both = jnp.concatenate([slope, turned], axis=1)
-    across = field_ref[...].T
-    channels = across.shape[0]
-    pair = lax.broadcasted_iota(jnp.int32, across.shape, 1) // 2
-    near_cols = out_ref.shape[3]
-    for mode in range(count // 2):
-        done = jnp.dot(
-            jnp.where(pair == mode, across, 0.0), both, preferred_element_type=jnp.float32
-        )
-        for part in range(2):
-            out_ref[part, mode // near_cols, 0, mode % near_cols] = done[
-                :, part * channels : (part + 1) * channels
-            ]
-
-
-def outer_products(spec_field, spec_slope, near_rows, near_cols, factor):
-    size = lax.axis_size("row")
-    count, channels = spec_field.shape
-    tile = count // size
-    shape = (2, near_rows, size, near_cols, channels, channels)
-    spec = pl.BlockSpec((tile, channels), lambda block: (block, 0))
-    result = pl.pallas_call(
-        functools.partial(outer_kernel, factor),
-        grid=(size,),
-        out_shape=jax.ShapeDtypeStruct(shape, jnp.float32),
-        in_specs=[spec, spec],
-        out_specs=pl.BlockSpec(
-            (2, near_rows, 1, near_cols, channels, channels),
-            lambda block: (0, 0, block, 0, 0, 0),
-        ),
-        name="outer_products",
-    )(spec_field, spec_slope)
-    return result.reshape(2, -1, channels, channels)
+def spec_parts(spec, mode_rows, mode_cols, size):
+    channels = spec.shape[1]
+    grid = spec.reshape(size, mode_rows // size, mode_cols // size, 2, channels)
+    grid = jnp.transpose(grid, (3, 1, 0, 2, 4)).reshape(2, -1, channels)
+    return grid[0], grid[1]
 
 
 def as_float(values):
@@ -588,7 +550,8 @@
     if back:
         share, result, gathered, send_more, recv_more, *rest = rest
     else:
-        cotangent, result, detail_turned, skip_turned, *rest = rest
+        cotangent, result, skip_share, detail_turned, skip_turned, *rest = rest
+        skip_share[...] = jnp.zeros_like(skip_share)
         for level in range(3):
             for member in range(3):
                 detail_turned[level, member] = as_float(detail[level, member]).T.astype(
@@ -669,6 +632,7 @@
             )
             if not back:
                 value = (as_float(cotangent[here]) * gelu_slope(value)).astype(jnp.bfloat16)
+                skip_share[...] += channel_product(plain[here], value)
             result[here] = value
 
     def span(first, stop, call):
@@ -734,15 +698,16 @@
     channels = plain.shape[1]
     result = jax.ShapeDtypeStruct(plain.shape, jnp.float32 if back else jnp.bfloat16)
     own = [pltpu.VMEM(detail.shape, jnp.bfloat16), pltpu.VMEM(skip.shape, jnp.bfloat16)]
+    second = jax.ShapeDtypeStruct(skip.shape, jnp.float32)
     if back:
         whole = (extra.shape[0] * size, channels)
-        result = (result, jax.ShapeDtypeStruct(whole, jnp.bfloat16))
+        second = jax.ShapeDtypeStruct(whole, jnp.bfloat16)
         own = [pltpu.SemaphoreType.DMA((1,)), pltpu.SemaphoreType.DMA((1,))]
     return pl.pallas_call(
         functools.partial(synthesis_kernel, size, back),
-        out_shape=result,
+        out_shape=(result, second),
         in_specs=[vmem] * 4 + [smem] + [vmem] * 7,
-        out_specs=(vmem, vmem) if back else vmem,
+        out_specs=(vmem, vmem),
         scratch_shapes=[
             *own,
             *(pltpu.VMEM(band.shape, jnp.bfloat16) for band in bands),
@@ -755,7 +720,7 @@
         compiler_params=pltpu.CompilerParams(
             collective_id=5 if back else 4,
             has_side_effects=True,
-            vmem_limit_bytes=48 * 1024 * 1024,
+            vmem_limit_bytes=24 * 1024 * 1024,
         ),
         cost_estimate=pl.CostEstimate(
             flops=6 * plain.size * plain.shape[2],
@@ -821,7 +786,7 @@
         out_real, out_imag = mix_modes(spec_real, spec_imag, weight_real, weight_imag, factor)
         coarse_image = owned_image(out_real, out_imag, row_modes, col_modes, local_rows, columns)
         coarse_image = jnp.pad(coarse_image, ((0, 0), (0, 0), (0, columns)))
-    upstream = synthesis_call(
+    upstream, skip_share = synthesis_call(
         coarse_image,
         full_field,
         row_filters,
@@ -835,7 +800,7 @@
     full_slope = analysis_call(upstream, row_filters, matrices, True)
     coarse_slope, bands_slope = split_bands(full_slope)
     if whole_tiles:
-        extra = (*full_field, *full_slope[:2], field, upstream)
+        extra = (*full_field, *full_slope[:2], skip_share)
         image_back, spec_back, share = spectral_path(
             full_slope[2], spectral_weight, tables, near_cols, extra, scales, sum_rows
         )
@@ -853,7 +818,7 @@
             * scales[octave]
             for octave in range(3)
             for member in range(3)
-        ] + [narrow("hcw,how->co", field, upstream) * scales[3]]
+        ] + [skip_share * scales[3]]
         sums = jnp.concatenate(shares, axis=0)
         sums = jnp.pad(sums, ((0, sum_rows - sums.shape[0]), (0, 0)))
         share = lax.psum_scatter(sums, "row", scatter_dimension=0, tiled=True)
@@ -873,18 +838,14 @@
     grad_detail = gathered[: 9 * channels].reshape(3, 3, channels, channels)
     grad_skip = gathered[9 * channels :]
     if whole_tiles:
-        near_rows = mode_rows // devices
-        grad_spectral = outer_products(spec_field, spec_back, near_rows, near_cols, factor)
-    else:
-        grad_real = (
-            spec_real[:, :, None] * back_real[:, None, :]
-            + spec_imag[:, :, None] * back_imag[:, None, :]
-        ) * factor
-        grad_imag = (
-            spec_real[:, :, None] * back_imag[:, None, :]
-            - spec_imag[:, :, None] * back_real[:, None, :]
-        ) * factor
-        grad_spectral = jnp.stack([grad_real, grad_imag])
+        spec_real, spec_imag = spec_parts(spec_field, mode_rows, mode_cols, devices)
+        back_real, back_imag = spec_parts(spec_back, mode_rows, mode_cols, devices)
+    beside_real = jnp.stack([back_real, back_imag]) * factor
+    beside_imag = jnp.stack([back_imag, -back_real]) * factor
+    grad_spectral = (
+        spec_real[None, :, :, None] * beside_real[:, :, None, :]
+        + spec_imag[None, :, :, None] * beside_imag[:, :, None, :]
+    )
     return (grad_field, grad_detail, grad_skip, grad_spectral)
 
 

time: 144 us -> 122 us (0.85)
  Pallas kernels: 124 us -> 105 us
  local copies, waits for them, and re-layouts: 16.2 us -> 8.59 us
  other arithmetic: 2.58 us -> 7.56 us
    pallas_call x1 -> x0, Pallas kernels: 10.5 us -> none  [outer_products(): pl.pallas_call(functools.partial(outer_kernel, factor), grid=(size,), out...]
    unnamed x43 -> x27, local copies, waits for them, and re-layouts: 14.7 us -> 7.02 us
    pallas_call x2, Pallas kernels: 56.7 us -> 51.9 us  [spectral_path(): pl.pallas_call(functools.partial(spectral_kernel, size, near_cols, back,...]
    add x0 -> x1, other arithmetic: none -> 4.62 us  [per_device(): spec_real[None, :, :, None] * beside_real[:, :, None, :]]
    pallas_call x2, Pallas kernels: 37.4 us -> 34 us  [synthesis_call(): pl.pallas_call(functools.partial(synthesis_kernel, size, back), out_shape...]
where the time goes in v5:
time: 122 us
  Pallas kernels  105 us (86%)
  local copies, waits for them, and re-layouts  8.59 us (7%)
  other arithmetic  7.56 us (6%)
    pallas_call x2, Pallas kernels, spectral_path(): pl.pallas_call(functools.partial(spectral_kernel, size, near_cols, back,...  51.9 us
    pallas_call x2, Pallas kernels, synthesis_call(): pl.pallas_call(functools.partial(synthesis_kernel, size, back), out_shape...  34 us
    pallas_call x2, Pallas kernels, analysis_call(): pl.pallas_call(functools.partial(analysis_kernel, size), out_shape=tuple(...  19.2 us
    unnamed x27, local copies, waits for them, and re-layouts  7.02 us
    add x1, other arithmetic, per_device(): spec_real[None, :, :, None] * beside_real[:, :, None, :]  4.62 us

profile of v5, /device:TPU:0, one launch (start us, length us, event | category | flops | bytes accessed | tf_op | source)
XLA Modules:
  0.0 122.1 jit_solution(6058443906690056738)
XLA Ops:
  0.6 0.0 copy-start
  0.7 0.9 select_reduce_fusion.1
  1.6 0.9 select_reduce_fusion
  2.6 0.3 fusion.3
  2.9 0.1 and_select_fusion.col_ref.col_inv_ref
  3.0 0.6 fusion.14
  3.6 0.0 copy-start.1
  3.6 1.6 %copy-done.1 = bf16[16,128,512]{2,1,0:T(8,128)(2,1)S(1)} copy-done((bf16[16,128,512]{2,1,0:T(8,128)(2,1)S(1)}, bf16[16,128,512]{2,1,0:T(8,128)(2,1)}, u32[]{:S(2)}) %copy-start.1) | copy-done | bytes 2097176
  5.2 0.0 copy-start.3
  5.2 1.0 copy-done.3
  6.2 0.0 copy-start.6
  6.2 0.9 copy-done.6
  7.2 0.0 copy-start.8
  7.2 0.8 copy-done.8
  7.9 0.0 copy-start.11
  7.9 0.7 copy-done.11
  8.6 0.0 copy-start.2
  8.6 0.0 copy-start.5
  8.6 0.0 copy-start.10
  8.6 12.2 %analysis.1 = (bf16[2,8,128,512]{3,2,1,0:T(8,128)(2,1)S(1)}, bf16[2,4,128,256]{3,2,1,0:T(8,128)(2,1)S(1)}, bf16[2,2,128,128]{3,2,1,0:T(8,128)(2,1)S(1)}) custom-call(bf16[16,128,512]{2,1,0:T(8,128)(2,1)S(1)} %copy-done.1, f32[2,4]{1,0:T(2,128)S(1)} %copy-done.11, bf16[512,512]{1,0:T(8,128)(2,1)S(1)} %copy-done.3, bf16[256,256]{1,0:T(8,128)(2,1)S(1)} %copy-done.6, ...), custom_call_target="tpu_custom_call" | custom-call | flops 3221225472 | bytes 16777216 | tf_op jit(solution)/shard_map/analysis/pallas_call | solution.py:500
  20.8 0.0 copy-done
  20.8 0.0 copy-start.4
  20.9 0.0 copy-start.7
  20.9 0.0 copy-start.9
  20.9 0.0 copy-start.12
  20.9 23.4 %spectral.1 = (bf16[2,128,128]{2,1,0:T(8,128)(2,1)S(1)}, f32[128,128]{1,0:T(8,128)S(1)}) custom-call(bf16[2,2,128,128]{3,2,1,0:T(8,128)(2,1)S(1)} %get-tuple-element.19.coarse_ref.out_3.rest_2_, f32[2,128,128]{2,1,0:T(8,128)S(1)} %and_select_fusion.col_ref.col_inv_ref, f32[128,128]{1,0:T(8,128)S(1)} %get-tuple-element.41.row_ref, ...), custom_call_target="tpu_custom_call" | custom-call | flops 16777216 | bytes 8388608 | tf_op jit(solution)/shard_map/spectral/pallas_call | solution.py:266
  44.4 0.0 copy-done.2
  44.4 0.0 copy-done.5
  44.4 0.0 copy-done.10
  44.4 16.5 %synthesis.1 = (bf16[16,128,512]{2,1,0:T(8,128)(2,1)S(1)}, f32[128,128]{1,0:T(8,128)S(1)}) custom-call(bf16[2,128,128]{2,1,0:T(8,128)(2,1)S(1)} %get-tuple-element.20.image, bf16[2,8,128,512]{3,2,1,0:T(8,128)(2,1)S(1)} %get-tuple-element.21.out_1.rest_0_, bf16[2,4,128,256]{3,2,1,0:T(8,128)(2,1)S(1)} %get-tuple-element.22.out_2.rest_1_, ...), custom_call_target="tpu_custom_call" | custom-call | flops 3221225472 | bytes 33554432 | tf_op jit(solution)/shard_map/synthesis/pallas_call | solution.py:706
  60.9 0.0 copy-done.4
  60.9 0.0 copy-done.7
  60.9 0.0 copy-done.9
  61.0 0.0 copy-done.12
  61.0 7.0 %analysis_back.1 = (bf16[2,8,128,512]{3,2,1,0:T(8,128)(2,1)S(1)}, bf16[2,4,128,256]{3,2,1,0:T(8,128)(2,1)S(1)}, bf16[2,2,128,128]{3,2,1,0:T(8,128)(2,1)S(1)}) custom-call(bf16[16,128,512]{2,1,0:T(8,128)(2,1)S(1)} %get-tuple-element.23.values.plain, f32[2,4]{1,0:T(2,128)S(1)} %copy-done.12, bf16[512,512]{1,0:T(8,128)(2,1)S(1)} %copy-done.4, ...), custom_call_target="tpu_custom_call" | custom-call | flops 3221225472 | bytes 16777216 | tf_op jit(solution)/shard_map/analysis_back/pallas_call | solution.py:500
  67.9 28.5 %spectral_back.1 = (bf16[2,128,128]{2,1,0:T(8,128)(2,1)S(1)}, f32[128,128]{1,0:T(8,128)S(1)}, bf16[80,128]{1,0:T(8,128)(2,1)S(1)}) custom-call(bf16[2,2,128,128]{3,2,1,0:T(8,128)(2,1)S(1)} %get-tuple-element.24.coarse_ref.out_3, f32[2,128,128]{2,1,0:T(8,128)S(1)} %and_select_fusion.col_ref.col_inv_ref, f32[128,128]{1,0:T(8,128)S(1)} %get-tuple-element.41.row_ref, ...), custom_call_target="tpu_custom_call" | custom-call | flops 16777216 | bytes 8388608 | tf_op jit(solution)/shard_map/spectral_back/pallas_call | solution.py:266
  96.5 17.4 %synthesis_back.1 = (f32[16,128,512]{2,1,0:T(8,128)S(1)}, bf16[1280,128]{1,0:T(8,128)(2,1)S(1)}) custom-call(bf16[2,128,128]{2,1,0:T(8,128)(2,1)S(1)} %get-tuple-element.28.image, bf16[2,8,128,512]{3,2,1,0:T(8,128)(2,1)S(1)} %get-tuple-element.25.rest_3_.out_1, bf16[2,4,128,256]{3,2,1,0:T(8,128)(2,1)S(1)} %get-tuple-element.26.rest_4_.out_2, ...), custom_call_target="tpu_custom_call" | custom-call | flops 3221225472 | bytes 33554432 | tf_op jit(solution)/shard_map/synthesis_back/pallas_call | solution.py:706
  113.9 0.6 slice.29
  114.7 0.9 slice.28
  115.5 4.6 %multiply_add_fusion = f32[2,64,128,128]{3,2,1,0:T(8,128)} fusion(f32[2,64,128]{2,1,0:T(8,128)S(1)} %get-tuple-element.39, f32[64,128]{1,0:T(8,128)S(1)} %bitcast.21, f32[2,64,128]{2,1,0:T(8,128)S(1)} %get-tuple-element.38, f32[64,128]{1,0:T(8,128)S(1)} %bitcast.20), kind=kLoop, calls=%fused_computation | loop fusion | flops 6291456 | bytes 8585216 | tf_op jit(solution)/shard_map/add | solution.py:846
  120.1 2.0 %copy.24 = f32[16,128,512]{2,1,0:T(8,128)} copy(f32[16,128,512]{2,1,0:T(8,128)S(1)} %get-tuple-element.48) | data formatting | bytes 8388608
  (13 shorter events, 0.2 us)
Async XLA Ops:
  0.6 20.2 %copy-start = (f32[2,64,128,128]{3,2,1,0:T(8,128)S(1)}, f32[2,64,128,128]{3,2,1,0:T(8,128)}, u32[]{:S(2)}) copy-start(f32[2,64,128,128]{3,2,1,0:T(8,128)} %weight.3) | copy-start | bytes 25165828
  3.6 1.6 %copy-start.1 = (bf16[16,128,512]{2,1,0:T(8,128)(2,1)S(1)}, bf16[16,128,512]{2,1,0:T(8,128)(2,1)}, u32[]{:S(2)}) copy-start(bf16[16,128,512]{2,1,0:T(8,128)(2,1)} %plain.1) | copy-start | bytes 6291460
  5.2 1.0 copy-start.3
  6.2 0.9 copy-start.6
  7.2 0.8 copy-start.8
  7.9 0.7 copy-start.11
  8.6 35.8 %copy-start.2 = (bf16[16,128,512]{2,1,0:T(8,128)(2,1)S(1)}, bf16[16,128,512]{2,1,0:T(8,128)(2,1)}, u32[]{:S(2)}) copy-start(bf16[16,128,512]{2,1,0:T(8,128)(2,1)} %rest_0_.1) | copy-start | bytes 6291460
  8.6 35.8 %copy-start.5 = (bf16[3,3,128,128]{3,2,1,0:T(8,128)(2,1)S(1)}, bf16[3,3,128,128]{3,2,1,0:T(8,128)(2,1)}, u32[]{:S(2)}) copy-start(bf16[3,3,128,128]{3,2,1,0:T(8,128)(2,1)} %detail.3) | copy-start | bytes 884740
  8.6 35.8 %copy-start.10 = (bf16[128,128]{1,0:T(8,128)(2,1)S(1)}, bf16[128,128]{1,0:T(8,128)(2,1)}, u32[]{:S(2)}) copy-start(bf16[128,128]{1,0:T(8,128)(2,1)} %skip.3) | copy-start | bytes 98308
  20.8 40.1 %copy-start.4 = (bf16[512,512]{1,0:T(8,128)(2,1)S(1)}, bf16[512,512]{1,0:T(8,128)(2,1)}, u32[]{:S(2)}) copy-start(bf16[512,512]{1,0:T(8,128)(2,1)} %turned_1.3) | copy-start | bytes 1572868
  20.9 40.1 %copy-start.7 = (bf16[256,256]{1,0:T(8,128)(2,1)S(1)}, bf16[256,256]{1,0:T(8,128)(2,1)}, u32[]{:S(2)}) copy-start(bf16[256,256]{1,0:T(8,128)(2,1)} %turned_2.3) | copy-start | bytes 393220
  20.9 40.1 %copy-start.9 = (bf16[128,128]{1,0:T(8,128)(2,1)S(1)}, bf16[128,128]{1,0:T(8,128)(2,1)}, u32[]{:S(2)}) copy-start(bf16[128,128]{1,0:T(8,128)(2,1)} %turned_3.3) | copy-start | bytes 98308
  20.9 40.1 %copy-start.12 = (f32[2,4]{1,0:T(2,128)S(1)}, f32[2,4]{1,0:T(2,128)}, u32[]{:S(2)}) copy-start(f32[2,4]{1,0:T(2,128)} %taps.7) | copy-start | bytes 100

commit v6 on v5

--- a/solution.py
+++ b/solution.py
@@ -80,7 +80,7 @@
                 return total + channel_product(wide, right[branch, row])
 
             total = lax.fori_loop(
-                0, left.shape[1], body, jnp.zeros((channels, channels), jnp.float32)
+                0, left.shape[1], body, jnp.zeros((channels, channels), jnp.float32), unroll=True
             )
             start = (level * 3 + member) * channels
             sums[start : start + channels, :] = (total * scales[level]).astype(jnp.bfloat16)
@@ -193,7 +193,7 @@
         send_c[here, :] = result
         return carry
 
-    lax.fori_loop(0, size, mix, 0, unroll=2)
+    lax.fori_loop(0, size, mix, 0, unroll=4 if size % 4 == 0 else 1)
     third = start_exchange(size, tile_b, send_c, land_c, send_sem.at[2], recv_sem.at[2])
     third.wait_recv()
     send_d[...] = lax.dot_general(
@@ -461,7 +461,7 @@
             one(get, row, matrix, out)
             return carry
 
-        lax.fori_loop(first, last, body, 0)
+        lax.fori_loop(first, last, body, 0, unroll=1 if (last - first) % 2 else 2)
 
     def edged(get, halo, count):
         return lambda row: get(row) if row < count else halo[row - count]
@@ -640,7 +640,7 @@
             call(row)
             return carry
 
-        lax.fori_loop(first, stop, body, 0)
+        lax.fori_loop(first, stop, body, 0, unroll=1 if (stop - first) % 2 else 2)
 
     level_3 = lambda row: one(2, row, image, out_3, turned_3, syn_3)
     level_2 = lambda row: one(1, row, top_2, out_2, turned_2, syn_2)

time: 122 us -> 116 us (0.951)
  Pallas kernels: 105 us -> 98.5 us
    pallas_call x2, Pallas kernels: 51.9 us -> 47.5 us  [spectral_path(): pl.pallas_call(functools.partial(spectral_kernel, size, near_cols, back,...]
    pallas_call x2, Pallas kernels: 34 us -> 31.8 us  [synthesis_call(): pl.pallas_call(functools.partial(synthesis_kernel, size, back), out_shape...]
where the time goes in v6:
time: 116 us
  Pallas kernels  98.5 us (85%)
  local copies, waits for them, and re-layouts  8.59 us (7%)
  other arithmetic  7.56 us (7%)
    pallas_call x2, Pallas kernels, spectral_path(): pl.pallas_call(functools.partial(spectral_kernel, size, near_cols, back,...  47.5 us
    pallas_call x2, Pallas kernels, synthesis_call(): pl.pallas_call(functools.partial(synthesis_kernel, size, back), out_shape...  31.8 us
    pallas_call x2, Pallas kernels, analysis_call(): pl.pallas_call(functools.partial(analysis_kernel, size), out_shape=tuple(...  19.2 us
    unnamed x27, local copies, waits for them, and re-layouts  7.02 us
    add x1, other arithmetic, per_device(): spec_real[None, :, :, None] * beside_real[:, :, None, :]  4.62 us

profile of v6, /device:TPU:0, one launch (start us, length us, event | category | flops | bytes accessed | tf_op | source)
XLA Modules:
  0.0 115.6 jit_solution(2407475852066334398)
XLA Ops:
  0.6 0.0 copy-start
  0.7 0.9 select_reduce_fusion.1
  1.6 0.9 select_reduce_fusion
  2.6 0.3 fusion.3
  2.9 0.1 and_select_fusion.col_ref.col_inv_ref
  3.0 0.6 fusion.14
  3.6 0.0 copy-start.1
  3.6 1.6 %copy-done.1 = bf16[16,128,512]{2,1,0:T(8,128)(2,1)S(1)} copy-done((bf16[16,128,512]{2,1,0:T(8,128)(2,1)S(1)}, bf16[16,128,512]{2,1,0:T(8,128)(2,1)}, u32[]{:S(2)}) %copy-start.1) | copy-done | bytes 2097176
  5.2 0.0 copy-start.3
  5.2 1.0 copy-done.3
  6.2 0.0 copy-start.6
  6.2 0.9 copy-done.6
  7.2 0.0 copy-start.8
  7.2 0.8 copy-done.8
  7.9 0.0 copy-start.11
  7.9 0.7 copy-done.11
  8.6 0.0 copy-start.2
  8.6 0.0 copy-start.5
  8.6 0.0 copy-start.10
  8.6 12.2 %analysis.1 = (bf16[2,8,128,512]{3,2,1,0:T(8,128)(2,1)S(1)}, bf16[2,4,128,256]{3,2,1,0:T(8,128)(2,1)S(1)}, bf16[2,2,128,128]{3,2,1,0:T(8,128)(2,1)S(1)}) custom-call(bf16[16,128,512]{2,1,0:T(8,128)(2,1)S(1)} %copy-done.1, f32[2,4]{1,0:T(2,128)S(1)} %copy-done.11, bf16[512,512]{1,0:T(8,128)(2,1)S(1)} %copy-done.3, bf16[256,256]{1,0:T(8,128)(2,1)S(1)} %copy-done.6, ...), custom_call_target="tpu_custom_call" | custom-call | flops 3221225472 | bytes 16777216 | tf_op jit(solution)/shard_map/analysis/pallas_call | solution.py:500
  20.8 0.0 copy-done
  20.8 0.0 copy-start.4
  20.9 0.0 copy-start.7
  20.9 0.0 copy-start.9
  20.9 0.0 copy-start.12
  20.9 22.9 %spectral.1 = (bf16[2,128,128]{2,1,0:T(8,128)(2,1)S(1)}, f32[128,128]{1,0:T(8,128)S(1)}) custom-call(bf16[2,2,128,128]{3,2,1,0:T(8,128)(2,1)S(1)} %get-tuple-element.19.coarse_ref.out_3.rest_2_, f32[2,128,128]{2,1,0:T(8,128)S(1)} %and_select_fusion.col_ref.col_inv_ref, f32[128,128]{1,0:T(8,128)S(1)} %get-tuple-element.41.row_ref, ...), custom_call_target="tpu_custom_call" | custom-call | flops 16777216 | bytes 8388608 | tf_op jit(solution)/shard_map/spectral/pallas_call | solution.py:266
  43.9 0.0 copy-done.2
  43.9 0.0 copy-done.5
  43.9 0.0 copy-done.10
  43.9 14.4 %synthesis.1 = (bf16[16,128,512]{2,1,0:T(8,128)(2,1)S(1)}, f32[128,128]{1,0:T(8,128)S(1)}) custom-call(bf16[2,128,128]{2,1,0:T(8,128)(2,1)S(1)} %get-tuple-element.20.image, bf16[2,8,128,512]{3,2,1,0:T(8,128)(2,1)S(1)} %get-tuple-element.21.out_1.rest_0_, bf16[2,4,128,256]{3,2,1,0:T(8,128)(2,1)S(1)} %get-tuple-element.22.out_2.rest_1_, ...), custom_call_target="tpu_custom_call" | custom-call | flops 3221225472 | bytes 33554432 | tf_op jit(solution)/shard_map/synthesis/pallas_call | solution.py:706
  58.3 0.0 copy-done.4
  58.3 0.0 copy-done.7
  58.3 0.0 copy-done.9
  58.3 0.0 copy-done.12
  58.4 7.0 %analysis_back.1 = (bf16[2,8,128,512]{3,2,1,0:T(8,128)(2,1)S(1)}, bf16[2,4,128,256]{3,2,1,0:T(8,128)(2,1)S(1)}, bf16[2,2,128,128]{3,2,1,0:T(8,128)(2,1)S(1)}) custom-call(bf16[16,128,512]{2,1,0:T(8,128)(2,1)S(1)} %get-tuple-element.23.values.plain, f32[2,4]{1,0:T(2,128)S(1)} %copy-done.12, bf16[512,512]{1,0:T(8,128)(2,1)S(1)} %copy-done.4, ...), custom_call_target="tpu_custom_call" | custom-call | flops 3221225472 | bytes 16777216 | tf_op jit(solution)/shard_map/analysis_back/pallas_call | solution.py:500
  65.3 24.5 %spectral_back.1 = (bf16[2,128,128]{2,1,0:T(8,128)(2,1)S(1)}, f32[128,128]{1,0:T(8,128)S(1)}, bf16[80,128]{1,0:T(8,128)(2,1)S(1)}) custom-call(bf16[2,2,128,128]{3,2,1,0:T(8,128)(2,1)S(1)} %get-tuple-element.24.coarse_ref.out_3, f32[2,128,128]{2,1,0:T(8,128)S(1)} %and_select_fusion.col_ref.col_inv_ref, f32[128,128]{1,0:T(8,128)S(1)} %get-tuple-element.41.row_ref, ...), custom_call_target="tpu_custom_call" | custom-call | flops 16777216 | bytes 8388608 | tf_op jit(solution)/shard_map/spectral_back/pallas_call | solution.py:266
  89.9 17.4 %synthesis_back.1 = (f32[16,128,512]{2,1,0:T(8,128)S(1)}, bf16[1280,128]{1,0:T(8,128)(2,1)S(1)}) custom-call(bf16[2,128,128]{2,1,0:T(8,128)(2,1)S(1)} %get-tuple-element.28.image, bf16[2,8,128,512]{3,2,1,0:T(8,128)(2,1)S(1)} %get-tuple-element.25.rest_3_.out_1, bf16[2,4,128,256]{3,2,1,0:T(8,128)(2,1)S(1)} %get-tuple-element.26.rest_4_.out_2, ...), custom_call_target="tpu_custom_call" | custom-call | flops 3221225472 | bytes 33554432 | tf_op jit(solution)/shard_map/synthesis_back/pallas_call | solution.py:706
  107.3 0.6 slice.29
  108.1 0.9 slice.28
  108.9 4.6 %multiply_add_fusion = f32[2,64,128,128]{3,2,1,0:T(8,128)} fusion(f32[2,64,128]{2,1,0:T(8,128)S(1)} %get-tuple-element.39, f32[64,128]{1,0:T(8,128)S(1)} %bitcast.21, f32[2,64,128]{2,1,0:T(8,128)S(1)} %get-tuple-element.38, f32[64,128]{1,0:T(8,128)S(1)} %bitcast.20), kind=kLoop, calls=%fused_computation | loop fusion | flops 6291456 | bytes 8585216 | tf_op jit(solution)/shard_map/add | solution.py:846
  113.5 2.0 %copy.24 = f32[16,128,512]{2,1,0:T(8,128)} copy(f32[16,128,512]{2,1,0:T(8,128)S(1)} %get-tuple-element.48) | data formatting | bytes 8388608
  (13 shorter events, 0.2 us)
Async XLA Ops:
  0.6 20.2 %copy-start = (f32[2,64,128,128]{3,2,1,0:T(8,128)S(1)}, f32[2,64,128,128]{3,2,1,0:T(8,128)}, u32[]{:S(2)}) copy-start(f32[2,64,128,128]{3,2,1,0:T(8,128)} %weight.3) | copy-start | bytes 25165828
  3.6 1.6 %copy-start.1 = (bf16[16,128,512]{2,1,0:T(8,128)(2,1)S(1)}, bf16[16,128,512]{2,1,0:T(8,128)(2,1)}, u32[]{:S(2)}) copy-start(bf16[16,128,512]{2,1,0:T(8,128)(2,1)} %plain.1) | copy-start | bytes 6291460
  5.2 1.0 copy-start.3
  6.2 0.9 copy-start.6
  7.2 0.8 copy-start.8
  7.9 0.7 copy-start.11
  8.6 35.3 %copy-start.2 = (bf16[16,128,512]{2,1,0:T(8,128)(2,1)S(1)}, bf16[16,128,512]{2,1,0:T(8,128)(2,1)}, u32[]{:S(2)}) copy-start(bf16[16,128,512]{2,1,0:T(8,128)(2,1)} %rest_0_.1) | copy-start | bytes 6291460
  8.6 35.3 %copy-start.5 = (bf16[3,3,128,128]{3,2,1,0:T(8,128)(2,1)S(1)}, bf16[3,3,128,128]{3,2,1,0:T(8,128)(2,1)}, u32[]{:S(2)}) copy-start(bf16[3,3,128,128]{3,2,1,0:T(8,128)(2,1)} %detail.3) | copy-start | bytes 884740
  8.6 35.3 %copy-start.10 = (bf16[128,128]{1,0:T(8,128)(2,1)S(1)}, bf16[128,128]{1,0:T(8,128)(2,1)}, u32[]{:S(2)}) copy-start(bf16[128,128]{1,0:T(8,128)(2,1)} %skip.3) | copy-start | bytes 98308
  20.8 37.5 %copy-start.4 = (bf16[512,512]{1,0:T(8,128)(2,1)S(1)}, bf16[512,512]{1,0:T(8,128)(2,1)}, u32[]{:S(2)}) copy-start(bf16[512,512]{1,0:T(8,128)(2,1)} %turned_1.3) | copy-start | bytes 1572868
  20.9 37.5 %copy-start.7 = (bf16[256,256]{1,0:T(8,128)(2,1)S(1)}, bf16[256,256]{1,0:T(8,128)(2,1)}, u32[]{:S(2)}) copy-start(bf16[256,256]{1,0:T(8,128)(2,1)} %turned_2.3) | copy-start | bytes 393220
  20.9 37.5 %copy-start.9 = (bf16[128,128]{1,0:T(8,128)(2,1)S(1)}, bf16[128,128]{1,0:T(8,128)(2,1)}, u32[]{:S(2)}) copy-start(bf16[128,128]{1,0:T(8,128)(2,1)} %turned_3.3) | copy-start | bytes 98308
  20.9 37.5 %copy-start.12 = (f32[2,4]{1,0:T(2,128)S(1)}, f32[2,4]{1,0:T(2,128)}, u32[]{:S(2)}) copy-start(f32[2,4]{1,0:T(2,128)} %taps.7) | copy-start | bytes 100
